TPU v7x, 256 devices: a whole 4x4x8 slice. The times are simulated.
256 devices in a mesh: ctx: 16 (over z, core), tp: 16 (over y, x).
Axes of the slice: x: 4, y: 4, z: 8, core: 2. Of those that a mesh axis runs over, the one named last changes fastest.
Arguments:
- hidden_rows: bfloat16 [8192, 8192], P('ctx', 'tp'), may hold values from -6 to 6
- w_value: bfloat16 [8192, 8192], P('ctx', 'tp'), may hold values from -0.0625 to 0.0625
- w_gate: bfloat16 [8192, 8192], P('ctx', 'tp'), may hold values from -0.0625 to 0.0625
- state_proj: bfloat16 [8192, 2, 4, 256], P('ctx'), may hold values from -1.5 to 1.5
- rates: float32 [8192, 128], P('ctx', 'tp'), may hold values from 0 to 4.5, as said below
- read_weights: float32 [6, 8192, 128], P(None, 'ctx', 'tp'), may hold values from 0.25 to 2
- prior_state: float32 [128, 64, 256], P('tp'), may hold values from -24 to 24
- skip_weight: float32 [128], P('tp'), may hold values from 0.5 to 2
- norm_gain: float32 [8192], P('tp'), may hold values from 0.25 to 1.75
Outputs:
- layer_out: bfloat16 [8192, 8192], P('ctx', 'tp')
Inputs may be any that keep to these rules, and one draw needn't show every extreme that they name: Positive rates.
All inputs are finite; a program needn't handle non-finite values.
Results may differ from a plain program's by a relative error of at most 0.0085.
Values may be sent and summed in bfloat16 or wider, within the bound.
No kernel may reach another device: no remote copies, remote signals or barrier semaphores. Data moves between devices by JAX's collectives and lax.ppermute only.
A program may use at most 128 MiB of HBM per device.

v0:
```python
import jax
import jax.numpy as jnp
from jax import lax
from jax.sharding import PartitionSpec as P

HEAD_DIM = 64
HPG = 32
LEVELS = 6


def level_of(distance, level_count):
    level = jnp.zeros(distance.shape, jnp.int32)
    for bit_pos in range(level_count):
        level = level + (jnp.right_shift(distance, bit_pos) > 0).astype(jnp.int32)
    return level


def on_device(
    hidden_rows,
    w_value,
    w_gate,
    state_proj,
    rates,
    read_weights,
    prior_state,
    skip_weight,
    norm_gain,
):
    tok_rows = rates.shape[0]
    head_count = rates.shape[1]
    level_total = LEVELS - 2
    full_rows = lax.all_gather(hidden_rows, "tp", axis=1, tiled=True)
    value_sum = jnp.dot(
        full_rows,
        lax.all_gather(w_value, "ctx", axis=0, tiled=True),
        preferred_element_type=jnp.float32,
    )
    gate_sum = jnp.dot(
        full_rows,
        lax.all_gather(w_gate, "ctx", axis=0, tiled=True),
        preferred_element_type=jnp.float32,
    )
    values_proj = value_sum.astype(jnp.bfloat16)
    gates_proj = gate_sum.astype(jnp.bfloat16)
    values3 = values_proj.reshape(tok_rows, head_count, HEAD_DIM)
    group_index = lax.axis_index("tp") * head_count // HPG
    write_vec = lax.dynamic_index_in_dim(state_proj[:, 0], group_index, 1, keepdims=False)
    read_vec = lax.dynamic_index_in_dim(state_proj[:, 1], group_index, 1, keepdims=False)
    cum_rate = jnp.cumsum(rates, axis=0)
    scores = lax.dot_general(
        read_vec, write_vec, (((1,), (1,)), ((), ())), preferred_element_type=jnp.float32
    )
    rate_lag = cum_rate.T[:, :, None] - cum_rate.T[:, None, :]
    causal = (jnp.arange(tok_rows)[:, None] >= jnp.arange(tok_rows)[None, :])[None]
    mixing = (
        jnp.where(causal, jnp.exp(-jnp.where(causal, rate_lag, 0.0)), 0.0) * scores[None]
    ).astype(jnp.bfloat16)
    local_out = jnp.einsum("hts,shp->thp", mixing, values3, preferred_element_type=jnp.float32)
    span_total = cum_rate[-1]
    write_weighted = (
        jnp.exp(-(span_total[None] - cum_rate))[:, :, None]
        * write_vec[:, None, :].astype(jnp.float32)
    ).astype(jnp.bfloat16)
    end_state = jnp.einsum(
        "thn,thp->hpn", write_weighted, values3, preferred_element_type=jnp.float32
    )
    my_block = lax.axis_index("ctx")
    totals = lax.all_gather(span_total[None], "ctx", axis=0, tiled=True)
    before = jnp.cumsum(totals, axis=0) - totals
    start_rate = lax.dynamic_index_in_dim(before, my_block, 0, keepdims=False)
    piece_states = lax.all_gather(end_state[None], "ctx", axis=0, tiled=True)
    piece_count = piece_states.shape[0]
    source_input = jnp.arange(piece_count, dtype=jnp.int32)
    earlier = (source_input < my_block)[:, None]
    exponent = jnp.where(earlier, start_rate[None] - before - totals, 0.0)
    weight = jnp.where(earlier, jnp.exp(-exponent), 0.0)
    levels = level_of(jnp.bitwise_xor(source_input, my_block), level_total)
    onehot = (levels[:, None] == jnp.arange(1, level_total + 1, dtype=jnp.int32)[None]).astype(
        jnp.float32
    )
    coefficient = onehot[:, :, None] * weight[:, None, :]
    carried = jnp.einsum(
        "mlh,mhpn->lhpn", coefficient, piece_states, precision=lax.Precision.HIGHEST
    )
    prior_part = jnp.exp(-start_rate)[:, None, None] * prior_state
    states = jnp.concatenate([carried, prior_part[None]], axis=0)
    projected = jnp.einsum(
        "tn,lhpn->tlhp", read_vec.astype(jnp.float32), states, precision=lax.Precision.HIGHEST
    )
    read_scale = read_weights[1:] * jnp.exp(-cum_rate)[None]
    carried_out = jnp.einsum(
        "lth,tlhp->thp", read_scale, projected, precision=lax.Precision.HIGHEST
    )
    mixed_out = (
        read_weights[0][:, :, None] * local_out
        + carried_out
        + skip_weight[None, :, None] * values3.astype(jnp.float32)
    )
    gates3 = gates_proj.reshape(tok_rows, head_count, HEAD_DIM).astype(jnp.float32)
    filtered_result = mixed_out * jax.nn.silu(gates3)
    inverse = lax.rsqrt(jnp.mean(filtered_result * filtered_result, axis=2, keepdims=True) + 1e-05)
    result = filtered_result * inverse * norm_gain.reshape(head_count, HEAD_DIM)[None]
    return result.reshape(tok_rows, head_count * HEAD_DIM).astype(jnp.bfloat16)


def solution(mesh):
    in_specs = (
        P("ctx", "tp"),
        P("ctx", "tp"),
        P("ctx", "tp"),
        P("ctx", None, None, None),
        P("ctx", "tp"),
        P(None, "ctx", "tp"),
        P("tp", None, None),
        P("tp"),
        P("tp"),
    )
    out_specs = P("ctx", "tp")
    return jax.shard_map(
        on_device, mesh=mesh, in_specs=in_specs, out_specs=out_specs, check_vma=False
    )
```

profile of v0, /device:TPU:1, one launch (start us, length us, event | category | flops | bytes accessed | tf_op | source)
XLA Modules:
  0.0 294.6 jit_solution(1288173570568783712)
XLA Ops:
  6.5 0.0 all-gather.7.cloned.1.call-start
  6.5 0.7 all-gather.7.cloned.1.call-update
  7.3 0.0 all-gather.9.cloned.1.call-start
  7.3 0.7 all-gather.9.cloned.1.call-update
  8.0 0.0 all-gather.11.cloned.1.call-start
  8.1 0.7 all-gather.11.cloned.1.call-update
  8.7 0.0 all-gather.13.cloned.1.call-start
  8.8 2.2 reduce-window.6
  11.0 0.2 slice_reduce_fusion
  11.2 0.1 negate_exponential_fusion.1
  11.3 0.2 slice_reduce_fusion.1
  11.5 2.3 fusion.38
  13.7 1.1 constant_dynamic-slice_fusion.1
  14.8 0.1 negate_exponential_fusion
  15.0 0.0 copy-start
  15.0 0.0 copy-start.2
  15.0 0.0 copy-start.1
  15.0 81.1 %all-gather.7.cloned.1.call-done = bf16[512,8192]{1,0:T(8,128)(2,1)} async-done(((bf16[512,512]{1,0:T(8,128)(2,1)}), bf16[512,8192]{1,0:T(8,128)(2,1)}) %all-gather.7.cloned.1.call-update) | async-done | bytes 8388624 | tf_op jit(solution)/shard_map/all_gather | solution.py:32
  96.1 58.5 %all-gather.9.cloned.1.call-done = bf16[8192,512]{1,0:T(8,128)(2,1)} async-done(((bf16[512,512]{1,0:T(8,128)(2,1)}), bf16[8192,512]{1,0:T(8,128)(2,1)}) %all-gather.9.cloned.1.call-update) | async-done | bytes 8388624 | tf_op jit(solution)/shard_map/all_gather | solution.py:35
  154.6 10.3 %convolution_convert_fusion.1 = bf16[512,512]{0,1:T(8,128)(2,1)S(1)} fusion(bf16[512,8192]{1,0:T(8,128)(2,1)} %all-gather.7.cloned.1.call-done, bf16[8192,512]{1,0:T(8,128)(2,1)} %all-gather.9.cloned.1.call-done), kind=kOutput, calls=%fused_computation.22 | convolution fusion | flops 4295229440 | bytes 17301504 | tf_op jit(solution)/shard_map/dot_general | solution.py:33
  164.9 0.0 copy-start.4
  164.9 0.8 copy-done.4
  165.8 1.7 fusion.6
  167.4 0.0 all-gather.13.cloned.1.call-update
  167.4 15.6 %all-gather.1 = f32[16,1,8]{2,1,0:T(1,128)S(1)} all-gather(f32[1,1,8]{2,1,0:T(1,128)S(1)} %bitcast.73), channel_id=1, replica_groups=mesh['ctx'=16,'tp'=16] {'ctx'}, dimensions={0}, use_global_device_ids=true | all-gather | bytes 544 | tf_op jit(solution)/shard_map/all_gather | solution.py:68
  183.1 0.0 copy-done
  183.1 0.1 broadcast_multiply_fusion
  183.2 0.4 broadcast_in_dim.63
  183.6 0.1 exponential_select_fusion
  183.7 0.1 copy.53
  183.8 0.0 copy-done.2
  183.8 0.1 mul.122
  183.9 0.1 iota_compare_fusion
  184.0 0.1 compare_convert_fusion
  184.0 0.0 copy-done.1
  184.0 0.1 add_bitcast_fusion.1
  184.1 0.3 fusion.23
  184.5 26.5 %all-gather.11.cloned.1.call-done = bf16[8192,512]{1,0:T(8,128)(2,1)} async-done(((bf16[512,512]{1,0:T(8,128)(2,1)}), bf16[8192,512]{1,0:T(8,128)(2,1)}) %all-gather.11.cloned.1.call-update) | async-done | bytes 8388624 | tf_op jit(solution)/shard_map/all_gather | solution.py:40
  211.0 11.1 %convolution_convert_fusion = bf16[512,512]{0,1:T(8,128)(2,1)} fusion(bf16[512,8192]{1,0:T(8,128)(2,1)} %all-gather.7.cloned.1.call-done, bf16[8192,512]{1,0:T(8,128)(2,1)} %all-gather.11.cloned.1.call-done), kind=kOutput, calls=%fused_computation.21 | convolution fusion | flops 4295229440 | bytes 17301504 | tf_op jit(solution)/shard_map/dot_general | solution.py:38
  222.1 45.1 %all-gather.13.cloned.1.call-done = f32[128,64,256]{2,1,0:T(8,128)} async-done(((f32[8,64,256]{2,1,0:T(8,128)}), f32[128,64,256]{2,1,0:T(8,128)}) %all-gather.13.cloned.1.call-update) | async-done | bytes 8388624 | tf_op jit(solution)/shard_map/all_gather | solution.py:71
  267.2 12.5 %fusion.9 = f32[4,8,64,256]{3,0,2,1:T(4,128)S(1)} fusion(f32[16,8,64,256]{3,2,1,0:T(8,128)} %bitcast.67, f32[16,8]{0,1:T(8,128)S(1)} %copy.53, f32[16,4]{0,1:T(4,128)S(1)} %compare_convert_fusion), kind=kOutput, calls=%fused_computation.13 | convolution fusion | flops 100663808 | bytes 10486528 | tf_op jit(solution)/shard_map/mlh,mhpn->lhpn/dot_general | solution.py:82
  279.6 0.0 copy-start.3
  279.7 0.0 copy-start.5
  279.7 0.0 copy-start.6
  279.7 0.9 pad_maximum_fusion
  280.5 2.9 multiply_reduce_fusion
  283.5 0.0 copy-done.3
  283.5 0.0 copy-done.5
  283.5 0.0 copy-done.6
  283.5 3.3 %multiply_reduce_fusion.1 = (f32[512,8]{0,1:T(8,128)S(1)}, f32[512,8,64]{0,2,1:T(8,128)S(1)}) fusion(bf16[512,8,64]{0,2,1:T(8,128)(2,1)S(1)} %bitcast.76, bf16[512,8,64]{0,2,1:T(8,128)(2,1)S(1)} %bitcast.75, f32[8]{0:T(128)S(1)} %copy-done.3, f32[512,8,64]{0,2,1:T(8,128)S(1)} %multiply_reduce_fusion, f32[512,512]{1,0:T(8,128)S(1)} %fusion.23, ...), kind=kOutput, calls=%fused_computation.27 | convolution fusion | flops 284422144 | bytes 4505632 | tf_op jit(solution)/shard_map/hts,shp->thp/dot_general | solution.py:58
  286.9 0.2 multiply_convert_fusion.14
  287.0 1.0 copy.56
  (12 shorter events, 0.2 us)
Async XLA Ops:
  6.5 89.6 %all-gather.7.cloned.1.call-start = ((), (), s32[]{:S(2)}) async-start(), calls=%async_computation | async-start | bytes 8912896 | tf_op jit(solution)/shard_map/all_gather | solution.py:32
  7.3 147.4 %all-gather.9.cloned.1.call-start = ((), (), s32[]{:S(2)}) async-start(), calls=%async_computation.1 | async-start | bytes 8912896 | tf_op jit(solution)/shard_map/all_gather | solution.py:35
  8.0 203.0 %all-gather.11.cloned.1.call-start = ((), (), s32[]{:S(2)}) async-start(), calls=%async_computation.2 | async-start | bytes 8912896 | tf_op jit(solution)/shard_map/all_gather | solution.py:40
  8.7 258.4 %all-gather.13.cloned.1.call-start = ((), (), s32[]{:S(2)}) async-start(), calls=%async_computation.3 | async-start | bytes 8912896 | tf_op jit(solution)/shard_map/all_gather | solution.py:71
  15.0 168.2 %copy-start = (f32[8,64,256]{2,1,0:T(8,128)S(1)}, f32[8,64,256]{2,1,0:T(8,128)}, u32[]{:S(2)}) copy-start(f32[8,64,256]{2,1,0:T(8,128)} %param.15) | copy-start | bytes 1572868
  15.0 168.8 %copy-start.2 = (f32[512]{0:T(512)S(1)}, f32[512]{0:T(512)}, u32[]{:S(2)}) copy-start(f32[512]{0:T(512)} %param.17) | copy-start | bytes 6148
  15.0 169.1 %copy-start.1 = (f32[6,512,8]{1,2,0:T(8,128)S(1)}, f32[6,512,8]{1,2,0:T(8,128)}, u32[]{:S(2)}) copy-start(f32[6,512,8]{1,2,0:T(8,128)} %param.14) | copy-start | bytes 294916
  164.9 0.8 copy-start.4
  279.6 3.8 %copy-start.3 = (f32[8]{0:T(128)S(1)}, f32[8]{0:T(128)}, u32[]{:S(2)}) copy-start(f32[8]{0:T(128)} %param.16) | copy-start | bytes 100
  279.7 3.8 %copy-start.5 = (bf16[512,512]{0,1:T(8,128)(2,1)S(1)}, bf16[512,512]{0,1:T(8,128)(2,1)}, u32[]{:S(2)}) copy-start(bf16[512,512]{0,1:T(8,128)(2,1)} %copy-done.4) | copy-start | bytes 1572868
  279.7 3.8 %copy-start.6 = (bf16[512,512]{0,1:T(8,128)(2,1)S(1)}, bf16[512,512]{0,1:T(8,128)(2,1)}, u32[]{:S(2)}) copy-start(bf16[512,512]{0,1:T(8,128)(2,1)} %convolution_convert_fusion) | copy-start | bytes 1572868
Sparse Core Ops, SparseCore 0:
  9.8 86.3 all-gather.6
  97.9 56.6 all-gather.8
  156.5 54.5 all-gather.10
  212.7 54.4 all-gather.12
where the time goes:
time: 295 us
  waiting for transfers between devices  213 us (72%)
  matrix products  42.1 us (14%)
  blocking collectives  15.6 us (5%)
  between operations  13.4 us (5%)
  local copies, waits for them, and re-layouts  6.08 us (2%)
  other arithmetic  3.97 us (1%)
    all_gather x1, waiting for transfers between devices, on_device(): full_rows = lax.all_gather(hidden_rows, 'tp', axis=1, tiled=True)  81.1 us
    all_gather x1, waiting for transfers between devices, on_device(): lax.all_gather(w_value, 'ctx', axis=0, tiled=True)  58.5 us
    all_gather x1, waiting for transfers between devices, on_device(): piece_states = lax.all_gather(end_state[None], 'ctx', axis=0, tiled=True)  45.1 us
    all_gather x1, waiting for transfers between devices, on_device(): lax.all_gather(w_gate, 'ctx', axis=0, tiled=True)  26.5 us
    all_gather x1, blocking collectives, on_device(): totals = lax.all_gather(span_total[None], 'ctx', axis=0, tiled=True)  15.6 us
    dot_general x1, matrix products, on_device(): jnp.einsum('mlh,mhpn->lhpn', coefficient, piece_states, precision=lax.Pre...  12.5 us
    dot_general x1, matrix products, on_device(): jnp.dot(full_rows, lax.all_gather(w_gate, 'ctx', axis=0, tiled=True), pre...  11.1 us
    dot_general x1, matrix products, on_device(): jnp.dot(full_rows, lax.all_gather(w_value, 'ctx', axis=0, tiled=True), pr...  10.3 us
  transfers between devices with their start and end apart: 4, of which 4 were waited for; matrix products, arithmetic and copies ran while one was open for 10% of the time, Pallas kernels for 0%

commit v1 on v0

v1 whole, which is shorter than its diff:
```python
import jax
import jax.numpy as jnp
from jax import lax
from jax.experimental import pallas as pl
from jax.experimental.pallas import tpu as pltpu
from jax.sharding import PartitionSpec as P

HEAD_DIM = 64
STATE = 256
HPG = 32
LEVELS = 6
HIGH = lax.Precision.HIGHEST
CTX = 16
SIDE = 4
ANY = pl.BlockSpec(memory_space=pl.ANY)
VMEM = pl.BlockSpec(memory_space=pltpu.VMEM)


def along_x(a, step):
    pairs = [(i, (i // SIDE) * SIDE + (i + step) % SIDE) for i in range(SIDE * SIDE)]
    return lax.ppermute(a, "tp", pairs)


def along_y(a, step):
    pairs = [(i, (i + SIDE * step) % (SIDE * SIDE)) for i in range(SIDE * SIDE)]
    return lax.ppermute(a, "tp", pairs)


def swap_ctx(a, mask):
    return lax.ppermute(a, "ctx", [(i, i ^ mask) for i in range(CTX)])


def gather_plane(rows, first, second):
    half = rows.shape[0] // 2
    lower, upper = first(rows, 1), first(rows, -1)
    far_top, far_bottom = first(lower[:half], 1), first(upper[half:], -1)
    line = jnp.concatenate([rows, lower, upper, far_top, far_bottom], axis=0)
    line_lower, line_upper = second(line, 1), second(line, -1)
    middle = line.shape[0] // 2
    line_top = second(line_lower[:middle], 1)
    line_bottom = second(line_upper[middle:], -1)
    return line, line_lower, line_upper, line_top, line_bottom


OFFSETS = (0, -1, 1, 2)


def values_kernel(*refs):
    pieces_a, pieces_b = refs[0:5], refs[5:10]
    w_ref, rows_out, values_out = refs[10:13]
    rows, weights, total, row_sem, weight_sem, out_sem = refs[13:]
    blocks, tok, depth = rows.shape
    part = tok // 2
    tp = lax.axis_index("tp")
    y, x = tp // SIDE, tp % SIDE
    for k in range(blocks):
        pltpu.make_async_copy(
            w_ref.at[pl.ds(k * depth, depth)], weights.at[k], weight_sem.at[k]
        ).start()

    def fetch(pieces, base, x_first):
        for i, near in enumerate(OFFSETS):
            for j, far in enumerate(OFFSETS):
                dx, dy = (near, far) if x_first else (far, near)
                k = ((y + dy + SIDE) % SIDE) * SIDE + (x + dx + SIDE) % SIDE
                if j < 3:
                    source = pieces[j].at[pl.ds(i * part, part)]
                else:
                    source = pieces[3 + i // 2].at[pl.ds((i % 2) * part, part)]
                pltpu.make_async_copy(
                    source, rows.at[k, pl.ds(base, part)], row_sem.at[k]
                ).start()

    fetch(pieces_a, 0, True)
    fetch(pieces_b, part, False)
    total[...] = jnp.zeros_like(total)

    @pl.loop(0, blocks)
    def _(k):
        pltpu.make_async_copy(rows.at[k], rows.at[k], row_sem.at[k]).wait()
        pltpu.make_async_copy(weights.at[k], weights.at[k], weight_sem.at[k]).wait()
        pltpu.make_async_copy(rows.at[k], rows_out.at[k], out_sem).start()
        total[...] += jnp.dot(
            rows[k], weights[k], preferred_element_type=jnp.float32
        )

    values_out[...] = total[...].astype(values_out.dtype)
    pltpu.make_async_copy(rows, rows_out, out_sem).wait()


def project_values(pieces_a, pieces_b, w_full, tok, depth):
    blocks = w_full.shape[0] // depth
    cols = w_full.shape[1]
    return pl.pallas_call(
        values_kernel,
        out_shape=(
            jax.ShapeDtypeStruct((blocks, tok, depth), jnp.bfloat16),
            jax.ShapeDtypeStruct((tok, cols), jnp.bfloat16),
        ),
        in_specs=[ANY] * 11,
        out_specs=(ANY, VMEM),
        scratch_shapes=[
            pltpu.VMEM((blocks, tok, depth), jnp.bfloat16),
            pltpu.VMEM((blocks, depth, cols), jnp.bfloat16),
            pltpu.VMEM((tok, cols), jnp.float32),
            pltpu.SemaphoreType.DMA((blocks,)),
            pltpu.SemaphoreType.DMA((blocks,)),
            pltpu.SemaphoreType.DMA,
        ],
        compiler_params=pltpu.CompilerParams(vmem_limit_bytes=32 * 2**20),
        cost_estimate=pl.CostEstimate(
            flops=2 * tok * cols * blocks * depth,
            bytes_accessed=2 * blocks * depth * (2 * tok + cols),
            transcendentals=0,
        ),
    )(*pieces_a, *pieces_b, w_full)


def gates_kernel(rows_ref, w_ref, mixed_ref, gain_ref, out_ref, rows, weights, total, row_sem, weight_sem):
    blocks, tok, depth = rows.shape
    cols = total.shape[1]
    for k in range(blocks):
        pltpu.make_async_copy(
            w_ref.at[pl.ds(k * depth, depth)], weights.at[k], weight_sem.at[k]
        ).start()
        pltpu.make_async_copy(rows_ref.at[k], rows.at[k], row_sem.at[k]).start()
    total[...] = jnp.zeros_like(total)

    @pl.loop(0, blocks)
    def _(k):
        pltpu.make_async_copy(rows.at[k], rows.at[k], row_sem.at[k]).wait()
        pltpu.make_async_copy(weights.at[k], weights.at[k], weight_sem.at[k]).wait()
        total[...] += jnp.dot(
            rows[k], weights[k], preferred_element_type=jnp.float32
        )

    gates = total[...].astype(jnp.bfloat16).astype(jnp.float32)
    gated = mixed_ref[...] * (gates / (1.0 + jnp.exp(-gates)))
    lanes = 128
    owner = lax.broadcasted_iota(jnp.int32, (cols, lanes), 0) // HEAD_DIM
    head = lax.broadcasted_iota(jnp.int32, (cols, lanes), 1)
    pick = jnp.where(owner == head, 1.0, 0.0).astype(jnp.float32)
    square_sum = jnp.dot(gated * gated, pick, precision=HIGH, preferred_element_type=jnp.float32)
    inverse = lax.rsqrt(square_sum * (1.0 / HEAD_DIM) + 1e-05)
    spread = lax.dot_general(
        inverse, pick, (((1,), (1,)), ((), ())), precision=HIGH, preferred_element_type=jnp.float32
    )
    out_ref[...] = (gated * spread * gain_ref[...]).astype(out_ref.dtype)


def finish(rows_all, w_full, mixed, gain):
    blocks, tok, depth = rows_all.shape
    cols = w_full.shape[1]
    return pl.pallas_call(
        gates_kernel,
        out_shape=jax.ShapeDtypeStruct((tok, cols), jnp.bfloat16),
        in_specs=[ANY, ANY, VMEM, VMEM],
        out_specs=VMEM,
        scratch_shapes=[
            pltpu.VMEM((blocks, tok, depth), jnp.bfloat16),
            pltpu.VMEM((blocks, depth, cols), jnp.bfloat16),
            pltpu.VMEM((tok, cols), jnp.float32),
            pltpu.SemaphoreType.DMA((blocks,)),
            pltpu.SemaphoreType.DMA((blocks,)),
        ],
        compiler_params=pltpu.CompilerParams(vmem_limit_bytes=40 * 2**20),
        cost_estimate=pl.CostEstimate(
            flops=2 * tok * cols * blocks * depth,
            bytes_accessed=2 * blocks * depth * (tok + cols),
            transcendentals=tok * cols,
        ),
    )(rows_all, w_full, mixed, gain)


def on_device(
    hidden_rows,
    w_value,
    w_gate,
    state_proj,
    rates,
    read_weights,
    prior_state,
    skip_weight,
    norm_gain,
):
    tok, heads = rates.shape
    depth = hidden_rows.shape[1]
    half = tok // 2
    me = lax.axis_index("ctx")
    core = me % 2
    plane = me // 2

    value_weights = lax.all_gather(w_value, "ctx", axis=0, tiled=True)
    gate_weights = lax.all_gather(w_gate, "ctx", axis=0, tiled=True)
    pieces_a = gather_plane(hidden_rows[:half], along_x, along_y)
    pieces_b = gather_plane(hidden_rows[half:], along_y, along_x)

    order = jnp.arange(tok)
    causal = order[:, None] >= order[None, :]
    cum_rate = jnp.dot(causal.astype(jnp.float32), rates, precision=HIGH)
    others = cum_rate[tok - 1 :]
    for bit in range(4):
        others = jnp.concatenate([others, swap_ctx(others, 1 << bit)], axis=0)
    block = jnp.arange(CTX, dtype=jnp.int32) ^ me
    between = (block[:, None] < block[None, :]) & (block[None, :] < me)
    gap = jnp.sum(jnp.where(between[:, :, None], others[None], 0.0), axis=1)
    start_rate = jnp.sum(jnp.where((block < me)[:, None], others, 0.0), axis=0)

    def total_of(distance):
        return others[distance]

    group = lax.axis_index("tp") * heads // HPG
    write_vec = lax.dynamic_index_in_dim(state_proj[:, 0], group, 1, keepdims=False)
    read_vec = lax.dynamic_index_in_dim(state_proj[:, 1], group, 1, keepdims=False)
    scores = lax.dot_general(
        read_vec, write_vec, (((1,), (1,)), ((), ())), preferred_element_type=jnp.float32
    )

    rows_all, values = project_values(pieces_a, pieces_b, value_weights, tok, depth)
    values3 = values.reshape(tok, heads, HEAD_DIM)

    span_total = cum_rate[tok - 1]
    write_weighted = (
        jnp.exp(-(span_total[None] - cum_rate))[:, :, None]
        * write_vec[:, None, :].astype(jnp.float32)
    ).astype(jnp.bfloat16)
    ends = jnp.einsum(
        "thn,thp->hpn", write_weighted, values3, preferred_element_type=jnp.float32
    )

    mine = ends.astype(jnp.bfloat16)
    sibling = swap_ctx(mine, 1)
    my_total, sibling_total = others[0], others[1]
    first_fade = jnp.where(core == 0, 1.0, 0.0)

    def fade(rate):
        return jnp.exp(-rate)

    own_scale = jnp.where(core == 0, fade(sibling_total), 1.0)
    sibling_scale = jnp.where(core == 0, 1.0, fade(my_total))
    plane_end = own_scale[:, None, None] * ends + sibling_scale[:, None, None] * sibling.astype(jnp.float32)
    share = heads // 2
    plane_share = lax.dynamic_slice_in_dim(plane_end, core * share, share, 0)
    plane_sent = plane_share.astype(jnp.bfloat16)
    near = [swap_ctx(plane_sent, 2 * m).astype(jnp.float32) for m in (1, 2, 3)]
    plane_totals = others.reshape(CTX // 2, 2, heads).sum(axis=1)
    share_totals = lax.dynamic_slice_in_dim(plane_totals, core * share, share, 1)
    planes = jnp.arange(SIDE, dtype=jnp.int32) ^ plane
    near_all = [plane_share, *near]

    def faded_sum(among):
        result = 0.0
        for m in among:
            later = jnp.zeros((share,), jnp.float32)
            for o in among:
                later = later + jnp.where((plane ^ o) > (plane ^ m), share_totals[o], 0.0)
            result = result + fade(later)[:, None, None] * near_all[m]
        return result

    pair_sum = faded_sum((2, 3)).astype(jnp.bfloat16)
    quad_sum = faded_sum((0, 1, 2, 3)).astype(jnp.bfloat16)
    quad_other = lax.ppermute(
        quad_sum, "ctx", [(2 * z + c, 2 * (7 - z) + c) for z in range(4) for c in range(2)]
    )
    shared = jnp.stack([near[0].astype(jnp.bfloat16), pair_sum, quad_other])
    shared_other = swap_ctx(shared, 1)
    lower = jnp.where(core == 0, shared, shared_other)
    upper = jnp.where(core == 0, shared_other, shared)
    states = jnp.concatenate([sibling[None], jnp.concatenate([lower, upper], axis=1)], axis=0)

    level_fade = []
    for level in range(4):
        last = (me >> level << level) - 1
        there = (me >> level) & 1
        since = jnp.sum(
            jnp.where(((block > last) & (block < me))[:, None], others, 0.0), axis=0
        )
        level_fade.append(jnp.where(there == 1, fade(since), 0.0))
    level_fade = jnp.stack(level_fade)

    prior_read = jnp.einsum(
        "tn,hpn->thp", read_vec.astype(jnp.float32), prior_state, precision=HIGH
    )
    cum_fade = jnp.exp(-cum_rate)
    rate_lag = cum_rate.T[:, :, None] - cum_rate.T[:, None, :]
    mixing = (
        jnp.where(causal[None], jnp.exp(-jnp.where(causal[None], rate_lag, 0.0)), 0.0) * scores[None]
    ).astype(jnp.bfloat16)
    local_out = jnp.einsum("hts,shp->thp", mixing, values3, preferred_element_type=jnp.float32)
    prior_scale = read_weights[5] * (cum_fade * fade(start_rate)[None])
    early = (
        read_weights[0][:, :, None] * local_out
        + prior_scale[:, :, None] * prior_read
        + skip_weight[None, :, None] * values3.astype(jnp.float32)
    )
    level_read = jnp.einsum(
        "tn,lhpn->lthp", read_vec, states, preferred_element_type=jnp.float32
    )
    level_scale = read_weights[1:5] * (cum_fade[None] * level_fade[:, None])
    mixed = early + jnp.sum(level_scale[:, :, :, None] * level_read, axis=0)

    return finish(
        rows_all, gate_weights, mixed.reshape(tok, heads * HEAD_DIM), norm_gain[None]
    )


def solution(mesh):
    in_specs = (
        P("ctx", "tp"),
        P("ctx", "tp"),
        P("ctx", "tp"),
        P("ctx", None, None, None),
        P("ctx", "tp"),
        P(None, "ctx", "tp"),
        P("tp", None, None),
        P("tp"),
        P("tp"),
    )
    out_specs = P("ctx", "tp")
    return jax.shard_map(
        on_device, mesh=mesh, in_specs=in_specs, out_specs=out_specs, check_vma=False
    )
```

time: 295 us -> 174 us (0.59)
  waiting for transfers between devices: 213 us -> 34.4 us
  starting transfers between devices: 0.12 us -> 48.7 us
  matrix products: 42.1 us -> 9.96 us
  local copies, waits for them, and re-layouts: 6.08 us -> 30.7 us
  Pallas kernels: 0 us -> 24.3 us
  blocking collectives: 15.6 us -> 0 us
  other arithmetic: 3.97 us -> 11.7 us
    all_gather x4 -> x2, waiting for transfers between devices: 211 us -> 0.02 us  [the longest x1 0.02 us: on_device(): gate_weights = lax.all_gather(w_gate, 'ctx', axis=0, tiled=True)]
    ppermute x0 -> x26, starting transfers between devices: none -> 48.6 us  [the longest x9 20.3 us: swap_ctx(): return lax.ppermute(a, 'ctx', [(i, i ^ mask) for i in range(CTX)])]
    dot_general x4 -> x3, matrix products: 36.8 us -> 2.71 us  [the longest x1 1.09 us: on_device(): cum_rate = jnp.dot(causal.astype(jnp.float32), rates, precision=HIGH)]
    ppermute x0 -> x26, waiting for transfers between devices: none -> 33 us  [the longest x9 17.1 us: swap_ctx(): return lax.ppermute(a, 'ctx', [(i, i ^ mask) for i in range(CTX)])]
    pallas_call x0 -> x2, Pallas kernels: none -> 24.3 us  [the longest x1 12.8 us: finish(): pl.pallas_call(gates_kernel, out_shape=jax.ShapeDtypeStruct((tok, cols),...]
    unnamed x14 -> x44, local copies, waits for them, and re-layouts: 0.86 us -> 17.9 us
    all_gather x1 -> x0, blocking collectives: 15.6 us -> none  [on_device(): totals = lax.all_gather(span_total[None], 'ctx', axis=0, tiled=True)]
    slice x2 -> x11, local copies, waits for them, and re-layouts: 0.34 us -> 4.44 us  [the longest x1 1.8 us: on_device(): pieces_b = gather_plane(hidden_rows[half:], along_y, along_x)]
  transfers between devices with their start and end apart: 4 -> 28, of which waited for: 4 -> 9; matrix products, arithmetic and copies ran while one was open for 10% -> 21% of each run, Pallas kernels for 0% -> 7%
where the time goes in v1:
time: 174 us
  starting transfers between devices  48.7 us (28%)
  waiting for transfers between devices  34.4 us (20%)
  local copies, waits for them, and re-layouts  30.7 us (18%)
  Pallas kernels  24.3 us (14%)
  between operations  13.8 us (8%)
  other arithmetic  11.7 us (7%)
  matrix products  9.96 us (6%)
    ppermute x9, starting transfers between devices, swap_ctx(): return lax.ppermute(a, 'ctx', [(i, i ^ mask) for i in range(CTX)])  20.3 us
    unnamed x44, local copies, waits for them, and re-layouts  17.9 us
    ppermute x9, waiting for transfers between devices, swap_ctx(): return lax.ppermute(a, 'ctx', [(i, i ^ mask) for i in range(CTX)])  17.1 us
    pallas_call x1, Pallas kernels, finish(): pl.pallas_call(gates_kernel, out_shape=jax.ShapeDtypeStruct((tok, cols),...  12.8 us
    ppermute x8, starting transfers between devices, along_x(): return lax.ppermute(a, 'tp', pairs)  11.6 us
    pallas_call x1, Pallas kernels, project_values(): pl.pallas_call(values_kernel, out_shape=(jax.ShapeDtypeStruct((blocks, to...  11.5 us
    ppermute x8, starting transfers between devices, along_y(): return lax.ppermute(a, 'tp', pairs)  11.2 us
    ppermute x8, waiting for transfers between devices, along_y(): return lax.ppermute(a, 'tp', pairs)  6.41 us
  transfers between devices with their start and end apart: 28, of which 9 were waited for; matrix products, arithmetic and copies ran while one was open for 21% of the time, Pallas kernels for 7%

profile of v1, /device:TPU:1, one launch (start us, length us, event | category | flops | bytes accessed | tf_op | source)
XLA Modules:
  0.0 173.5 jit_solution(15005167599623201276)
XLA Ops:
  6.5 0.7 all-gather.3.cloned.1.call-update
  7.3 0.7 all-gather.5.cloned.1.call-update
  8.0 1.8 %fusion.49 = (bf16[256,512]{1,0:T(8,128)(2,1)S(1)}, bf16[1024,512]{1,0:T(8,128)(2,1)}, bf16[1024,512]{1,0:T(8,128)(2,1)S(1)}, bf16[256,512]{1,0:T(8,128)(2,1)S(1)}) fusion(bf16[512,512]{1,0:T(8,128)(2,1)} %param.9), kind=kLoop, calls=%fused_computation.121 | loop fusion | bytes 1572864 | tf_op jit(solution)/shard_map/slice | solution.py:196
  9.8 2.1 %collective-permute-start = (bf16[256,512]{1,0:T(8,128)(2,1)S(1)}, bf16[256,512]{1,0:T(8,128)(2,1)S(1)}, u32[]{:S(2)}, u32[]{:S(2)}) collective-permute-start(bf16[256,512]{1,0:T(8,128)(2,1)S(1)} %get-tuple-element.21), channel_id=1, source_target_pairs={{0,1},{1,2},{2,3},{3,0},{4,5},{5,6},{6,7},{7,4},{8,9},{9,10},{10,1... | collective-permute-start | bytes 786440 | tf_op jit(solution)/shard_map/ppermute | solution.py:21
  11.9 1.3 collective-permute-start.1
  13.1 1.5 collective-permute-start.8
  14.6 1.4 collective-permute-start.9
  16.1 1.1 fusion.16
  17.4 3.6 %collective-permute-start.16 = (f32[1,8]{0,1:T(8,128)S(1)}, f32[1,8]{0,1:T(8,128)S(1)}, u32[]{:S(2)}, u32[]{:S(2)}) collective-permute-start(f32[1,8]{0,1:T(8,128)S(1)} %get-tuple-element.28), channel_id=1, source_target_pairs={{0,16},{16,0},{32,48},{48,32},{64,80},{80,64},{96,112},{112,96},{1... | collective-permute-start | bytes 104 | tf_op jit(solution)/shard_map/ppermute | solution.py:30
  22.2 2.3 %fusion.48 = (bf16[512,1,4,256]{3,2,1,0:T(4,128)(2,1)S(1)}, bf16[512,1,4,256]{3,2,1,0:T(4,128)(2,1)S(1)}) fusion(bf16[512,2,4,256]{3,2,1,0:T(4,128)(2,1)} %param.12), kind=kLoop, calls=%fused_computation.120 | loop fusion | bytes 4194304 | tf_op jit(solution)/shard_map/slice | solution.py:214
  25.6 0.7 slice_bitcast_fusion
  26.2 0.8 fusion.29
  27.1 1.3 fusion.25
  29.4 2.7 %collective-permute-start.3 = (bf16[128,512]{1,0:T(8,128)(2,1)S(1)}, bf16[128,512]{1,0:T(8,128)(2,1)S(1)}, u32[]{:S(2)}, u32[]{:S(2)}) collective-permute-start(bf16[128,512]{1,0:T(8,128)(2,1)S(1)} %slice.98), channel_id=1, source_target_pairs={{0,3},{1,0},{2,1},{3,2},{4,7},{5,4},{6,5},{7,6},{8,11},{9,8},{10,9... | collective-permute-start | bytes 393224 | tf_op jit(solution)/shard_map/ppermute | solution.py:21
  32.3 2.7 %collective-permute-start.11 = (bf16[128,512]{1,0:T(8,128)(2,1)S(1)}, bf16[128,512]{1,0:T(8,128)(2,1)S(1)}, u32[]{:S(2)}, u32[]{:S(2)}) collective-permute-start(bf16[128,512]{1,0:T(8,128)(2,1)S(1)} %slice.102), channel_id=1, source_target_pairs={{0,12},{1,13},{2,14},{3,15},{4,0},{5,1},{6,2},{7,3},{8,4},{9,5},{1... | collective-permute-start | bytes 393224 | tf_op jit(solution)/shard_map/ppermute | solution.py:26
  35.0 0.7 constant_dynamic-update-slice_fusion.3
  35.7 0.7 constant_dynamic-update-slice_fusion.2
  36.5 0.7 constant_dynamic-update-slice_fusion.1
  37.5 0.7 constant_dynamic-update-slice_fusion.refs_0_
  38.2 2.7 %collective-permute-start.5 = (bf16[1024,512]{1,0:T(8,128)(2,1)}, bf16[1024,512]{1,0:T(8,128)(2,1)S(1)}, u32[]{:S(2)}, u32[]{:S(2)}) collective-permute-start(bf16[1024,512]{1,0:T(8,128)(2,1)} %constant_dynamic-update-slice_fusion.refs_0_), channel_id=1, source_target_pairs={{0,12},{1,13},{2,14},{3,15},{4,0},{5,1},{6,2},{7,3},{8,4},{9,5},{1... | collective-permute-start | bytes 3145736 | tf_op jit(solution)/shard_map/ppermute | solution.py:26
  40.9 0.7 constant_dynamic-update-slice_fusion.6
  41.6 0.7 constant_dynamic-update-slice_fusion.5.refs_5_
  42.2 2.7 %collective-permute-start.13 = (bf16[1024,512]{1,0:T(8,128)(2,1)}, bf16[1024,512]{1,0:T(8,128)(2,1)}, u32[]{:S(2)}, u32[]{:S(2)}) collective-permute-start(bf16[1024,512]{1,0:T(8,128)(2,1)} %constant_dynamic-update-slice_fusion.5.refs_5_), channel_id=1, source_target_pairs={{0,3},{1,0},{2,1},{3,2},{4,7},{5,4},{6,5},{7,6},{8,11},{9,8},{10,9... | collective-permute-start | bytes 3145736 | tf_op jit(solution)/shard_map/ppermute | solution.py:21
  44.9 2.9 %collective-permute-start.18 = (f32[4,8]{1,0:T(4,128)S(1)}, f32[4,8]{1,0:T(4,128)S(1)}, u32[]{:S(2)}, u32[]{:S(2)}) collective-permute-start(f32[4,8]{1,0:T(4,128)S(1)} %pad_maximum_fusion.2), channel_id=1, source_target_pairs={{0,64},{16,80},{32,96},{48,112},{64,0},{80,16},{96,32},{112,48},{1... | collective-permute-start | bytes 392 | tf_op jit(solution)/shard_map/ppermute | solution.py:30
  48.4 0.8 collective-permute-done.18
  49.3 5.5 %collective-permute-start.19 = (f32[8,8]{1,0:T(8,128)S(1)}, f32[8,8]{1,0:T(8,128)S(1)}, u32[]{:S(2)}, u32[]{:S(2)}) collective-permute-start(f32[8,8]{1,0:T(8,128)S(1)} %pad_maximum_fusion.1), channel_id=1, source_target_pairs={{0,128},{16,144},{32,160},{48,176},{64,192},{80,208},{96,224},{112... | collective-permute-start | bytes 776 | tf_op jit(solution)/shard_map/ppermute | solution.py:30
  54.9 0.7 dynamic-slice.2
  55.9 1.3 select_reduce_fusion.4
  58.3 4.8 %collective-permute-done.4.refs_1_ = bf16[1024,512]{1,0:T(8,128)(2,1)S(1)} collective-permute-done((bf16[1024,512]{1,0:T(8,128)(2,1)}, bf16[1024,512]{1,0:T(8,128)(2,1)S(1)}, u32[]{:S(2)}, u32[]{:S(2)}) %collective-permute-start.4) | collective-permute-done | bytes 1048608 | tf_op jit(solution)/shard_map/ppermute | solution.py:26
  63.3 2.7 %collective-permute-start.7 = (bf16[512,512]{1,0:T(8,128)(2,1)S(1)}, bf16[512,512]{1,0:T(8,128)(2,1)S(1)}, u32[]{:S(2)}, u32[]{:S(2)}) collective-permute-start(bf16[512,512]{1,0:T(8,128)(2,1)S(1)} %slice.100), channel_id=1, source_target_pairs={{0,12},{1,13},{2,14},{3,15},{4,0},{5,1},{6,2},{7,3},{8,4},{9,5},{1... | collective-permute-start | bytes 1572872 | tf_op jit(solution)/shard_map/ppermute | solution.py:26
  66.5 1.1 slice.103
  67.7 1.1 slice.104
  68.8 2.7 %collective-permute-start.15 = (bf16[512,512]{1,0:T(8,128)(2,1)S(1)}, bf16[512,512]{1,0:T(8,128)(2,1)S(1)}, u32[]{:S(2)}, u32[]{:S(2)}) collective-permute-start(bf16[512,512]{1,0:T(8,128)(2,1)S(1)} %slice.104), channel_id=1, source_target_pairs={{0,3},{1,0},{2,1},{3,2},{4,7},{5,4},{6,5},{7,6},{8,11},{9,8},{10,9... | collective-permute-start | bytes 1572872 | tf_op jit(solution)/shard_map/ppermute | solution.py:21
  72.8 1.3 bitcast_multiply_fusion.1
  74.1 1.6 collective-permute-done.6.refs_3_
  75.7 0.8 copy-done.5
  76.5 3.0 %collective-permute-done.14.refs_8_ = bf16[512,512]{1,0:T(8,128)(2,1)S(1)} collective-permute-done((bf16[512,512]{1,0:T(8,128)(2,1)S(1)}, bf16[512,512]{1,0:T(8,128)(2,1)S(1)}, u32[]{:S(2)}, u32[]{:S(2)}) %collective-permute-start.14) | collective-permute-done | bytes 524320 | tf_op jit(solution)/shard_map/ppermute | solution.py:21
  79.5 0.8 copy-done.7
  80.3 0.8 copy-done.9
  81.1 1.2 copy-done.4
  82.3 1.0 copy-done.6
  83.4 1.0 copy-done.8
  84.4 1.0 copy-done.10
  85.4 11.5 %shard_map.91 = (bf16[16,512,512]{2,1,0:T(8,128)(2,1)S(1)}, bf16[512,512]{1,0:T(8,128)(2,1)S(1)}) custom-call(bf16[1024,512]{1,0:T(8,128)(2,1)} %constant_dynamic-update-slice_fusion.refs_0_, bf16[1024,512]{1,0:T(8,128)(2,1)S(1)} %collective-permute-done.4.refs_1_, bf16[1024,512]{1,0:T(8,128)(2,1)S(1)} %collective-permute-done.5.refs_2_, ...), custom_call_target="tpu_custom_call" | custom-call | flops 4294967296 | bytes 25165824 | tf_op jit(solution)/shard_map/pallas_call | solution.py:94
  97.0 3.2 %copy-done.1 = bf16[16,512,512]{2,1,0:T(8,128)(2,1)} copy-done((bf16[16,512,512]{2,1,0:T(8,128)(2,1)}, bf16[16,512,512]{2,1,0:T(8,128)(2,1)S(1)}, u32[]{:S(2)}) %copy-start.1) | copy-done | bytes 8388632
  100.3 0.8 copy-done.11
  101.0 1.3 copy.20
  102.3 1.9 %fusion.50 = (bf16[8,64,256]{2,1,0:T(8,128)(2,1)S(1)}, f32[8,64,256]{2,1,0:T(8,128)S(1)}) fusion(bf16[512,8,64]{0,2,1:T(8,128)(2,1)S(1)} %bitcast.66, f32[512,256]{1,0:T(8,128)} %fusion.29, f32[512,8]{0,1:T(8,128)} %get-tuple-element.25), kind=kOutput, calls=%fused_computation.122 | convolution fusion | flops 136445952 | bytes 1851392 | tf_op jit(solution)/shard_map/thn,thp->hpn/dot_general | solution.py:227
  104.2 3.8 %collective-permute-start.20 = (bf16[8,64,256]{2,1,0:T(8,128)(2,1)S(1)}, bf16[8,64,256]{2,1,0:T(8,128)(2,1)S(1)}, u32[]{:S(2)}, u32[]{:S(2)}) collective-permute-start(bf16[8,64,256]{2,1,0:T(8,128)(2,1)S(1)} %get-tuple-element.35), channel_id=1, source_target_pairs={{0,16},{16,0},{32,48},{48,32},{64,80},{80,64},{96,112},{112,96},{1... | collective-permute-start | bytes 786440 | tf_op jit(solution)/shard_map/ppermute | solution.py:30
  108.6 0.8 exponential_bitcast_fusion.5
  109.5 0.8 fusion.27
  110.3 2.7 %collective-permute-start.23 = (bf16[4,64,256]{2,1,0:T(8,128)(2,1)S(1)}, bf16[4,64,256]{2,1,0:T(8,128)(2,1)S(1)}, u32[]{:S(2)}, u32[]{:S(2)}) collective-permute-start(bf16[4,64,256]{2,1,0:T(8,128)(2,1)S(1)} %fusion.27), channel_id=1, source_target_pairs={{0,96},{16,112},{32,64},{48,80},{64,32},{80,48},{96,0},{112,16},{1... | collective-permute-start | bytes 393224 | tf_op jit(solution)/shard_map/ppermute | solution.py:30
  113.2 0.7 collective-permute-start.21
  115.2 4.9 %collective-permute-done.23 = bf16[4,64,256]{2,1,0:T(8,128)(2,1)S(1)} collective-permute-done((bf16[4,64,256]{2,1,0:T(8,128)(2,1)S(1)}, bf16[4,64,256]{2,1,0:T(8,128)(2,1)S(1)}, u32[]{:S(2)}, u32[]{:S(2)}) %collective-permute-start.23) | collective-permute-done | bytes 131104 | tf_op jit(solution)/shard_map/ppermute | solution.py:30
  120.0 11.1 %collective-permute-done.22 = bf16[4,64,256]{2,1,0:T(8,128)(2,1)S(1)} collective-permute-done((bf16[4,64,256]{2,1,0:T(8,128)(2,1)S(1)}, bf16[4,64,256]{2,1,0:T(8,128)(2,1)S(1)}, u32[]{:S(2)}, u32[]{:S(2)}) %collective-permute-start.22) | collective-permute-done | bytes 131104 | tf_op jit(solution)/shard_map/ppermute | solution.py:30
  131.1 0.9 fusion.28
  132.0 5.4 %collective-permute-start.24 = (bf16[4,64,256]{2,1,0:T(8,128)(2,1)S(1)}, bf16[4,64,256]{2,1,0:T(8,128)(2,1)S(1)}, u32[]{:S(2)}, u32[]{:S(2)}) collective-permute-start(bf16[4,64,256]{2,1,0:T(8,128)(2,1)S(1)} %get-tuple-element.23), channel_id=1, source_target_pairs={{0,224},{16,240},{32,192},{48,208},{64,160},{80,176},{96,128},{112... | collective-permute-start | bytes 393224 | tf_op jit(solution)/shard_map/ppermute | solution.py:262
  137.6 5.8 %collective-permute-done.24 = bf16[4,64,256]{2,1,0:T(8,128)(2,1)S(1)} collective-permute-done((bf16[4,64,256]{2,1,0:T(8,128)(2,1)S(1)}, bf16[4,64,256]{2,1,0:T(8,128)(2,1)S(1)}, u32[]{:S(2)}, u32[]{:S(2)}) %collective-permute-start.24) | collective-permute-done | bytes 131104 | tf_op jit(solution)/shard_map/ppermute | solution.py:262
  143.5 0.8 collective-permute-start.25
  144.3 4.1 %fusion.10 = f32[512,8,64]{0,2,1:T(8,128)S(1)} fusion(bf16[512,8,64]{0,2,1:T(8,128)(2,1)S(1)} %bitcast.67, f32[512,512]{1,0:T(8,128)} %fusion.25, f32[8,512]{1,0:T(8,128)S(1)} %bitcast.75, pred[512,512]{1,0:T(8,128)(4,1)S(1)} %iota_compare_fusion, f32[512,8]{0,1:T(8,128)} %slice_bitcast_fusion), kind=kOutput, calls=%fused_computation.14 | convolution fusion | flops 281280512 | bytes 2916352 | tf_op jit(solution)/shard_map/hts,shp->thp/dot_general | solution.py:289
  148.5 0.8 fusion
  149.3 0.9 fusion.9
  150.5 3.4 %copy-done.2 = bf16[16,512,512]{2,1,0:T(8,128)(2,1)S(1)} copy-done((bf16[16,512,512]{2,1,0:T(8,128)(2,1)S(1)}, bf16[16,512,512]{2,1,0:T(8,128)(2,1)}, u32[]{:S(2)}) %copy-start.2) | copy-done | bytes 8388632
  153.9 12.8 %shard_map.92 = bf16[512,512]{1,0:T(8,128)(2,1)} custom-call(bf16[16,512,512]{2,1,0:T(8,128)(2,1)S(1)} %copy-done.2, bf16[8192,512]{1,0:T(8,128)(2,1)} %all-gather.5.cloned.1.call-done.w_ref, f32[512,512]{1,0:T(8,128)S(1)} %copy.31.mixed_ref, f32[1,512]{1,0:T(1,128)S(1)} %bitcast.64), custom_call_target="tpu_custom_call" | custom-call | flops 4294967296 | bytes 16777216 | tf_op jit(solution)/shard_map/pallas_call | solution.py:154
  (96 shorter events, 10.9 us)
Async XLA Ops:
  6.5 142.7 %copy-start = (f32[8,64,256]{2,1,0:T(8,128)S(1)}, f32[8,64,256]{2,1,0:T(8,128)}, u32[]{:S(2)}) copy-start(f32[8,64,256]{2,1,0:T(8,128)} %param.15) | copy-start | bytes 1572868
  6.5 19.0 %copy-start.15 = (f32[6,512,8]{1,2,0:T(8,128)S(1)}, f32[6,512,8]{1,2,0:T(8,128)}, u32[]{:S(2)}) copy-start(f32[6,512,8]{1,2,0:T(8,128)} %param.14) | copy-start | bytes 294916
  6.5 74.5 %all-gather.3.cloned.1.call-start = ((), (), s32[]{:S(2)}) async-start(), calls=%async_computation | async-start | bytes 8912896 | tf_op jit(solution)/shard_map/all_gather | solution.py:193
  7.3 143.2 %all-gather.5.cloned.1.call-start = ((), (), s32[]{:S(2)}) async-start(), calls=%async_computation.1 | async-start | bytes 8912896 | tf_op jit(solution)/shard_map/all_gather | solution.py:194
  9.8 19.5 %collective-permute-start = (bf16[256,512]{1,0:T(8,128)(2,1)S(1)}, bf16[256,512]{1,0:T(8,128)(2,1)S(1)}, u32[]{:S(2)}, u32[]{:S(2)}) collective-permute-start(bf16[256,512]{1,0:T(8,128)(2,1)S(1)} %get-tuple-element.21), channel_id=1, source_target_pairs={{0,1},{1,2},{2,3},{3,0},{4,5},{5,6},{6,7},{7,4},{8,9},{9,10},{10,1... | collective-permute-start | bytes 786440 | tf_op jit(solution)/shard_map/ppermute | solution.py:21
  11.9 17.5 %collective-permute-start.1 = (bf16[256,512]{1,0:T(8,128)(2,1)S(1)}, bf16[256,512]{1,0:T(8,128)(2,1)S(1)}, u32[]{:S(2)}, u32[]{:S(2)}) collective-permute-start(bf16[256,512]{1,0:T(8,128)(2,1)S(1)} %get-tuple-element.21), channel_id=1, source_target_pairs={{0,3},{1,0},{2,1},{3,2},{4,7},{5,4},{6,5},{7,6},{8,11},{9,8},{10,9... | collective-permute-start | bytes 786440 | tf_op jit(solution)/shard_map/ppermute | solution.py:21
  13.1 19.0 %collective-permute-start.8 = (bf16[256,512]{1,0:T(8,128)(2,1)S(1)}, bf16[256,512]{1,0:T(8,128)(2,1)S(1)}, u32[]{:S(2)}, u32[]{:S(2)}) collective-permute-start(bf16[256,512]{1,0:T(8,128)(2,1)S(1)} %get-tuple-element.18), channel_id=1, source_target_pairs={{0,4},{1,5},{2,6},{3,7},{4,8},{5,9},{6,10},{7,11},{8,12},{9,13},{1... | collective-permute-start | bytes 786440 | tf_op jit(solution)/shard_map/ppermute | solution.py:26
  14.6 17.6 %collective-permute-start.9 = (bf16[256,512]{1,0:T(8,128)(2,1)S(1)}, bf16[256,512]{1,0:T(8,128)(2,1)S(1)}, u32[]{:S(2)}, u32[]{:S(2)}) collective-permute-start(bf16[256,512]{1,0:T(8,128)(2,1)S(1)} %get-tuple-element.18), channel_id=1, source_target_pairs={{0,12},{1,13},{2,14},{3,15},{4,0},{5,1},{6,2},{7,3},{8,4},{9,5},{1... | collective-permute-start | bytes 786440 | tf_op jit(solution)/shard_map/ppermute | solution.py:26
  17.4 11.5 %copy-start.17 = (f32[8]{0:T(128)}, f32[8]{0:T(128)S(1)}, u32[]{:S(2)}) copy-start(f32[8]{0:T(128)S(1)} %get-tuple-element.27) | copy-start | bytes 100
  17.4 11.6 %collective-permute-start.16 = (f32[1,8]{0,1:T(8,128)S(1)}, f32[1,8]{0,1:T(8,128)S(1)}, u32[]{:S(2)}, u32[]{:S(2)}) collective-permute-start(f32[1,8]{0,1:T(8,128)S(1)} %get-tuple-element.28), channel_id=1, source_target_pairs={{0,16},{16,0},{32,48},{48,32},{64,80},{80,64},{96,112},{112,96},{1... | collective-permute-start | bytes 104 | tf_op jit(solution)/shard_map/ppermute | solution.py:30
  25.5 2.8 %copy-start.13 = (bf16[512,1,1,256]{3,2,1,0:T(2,128)(2,1)}, bf16[512,1,1,256]{3,2,1,0:T(2,128)(2,1)S(1)}, u32[]{:S(2)}) copy-start(bf16[512,1,1,256]{3,2,1,0:T(2,128)(2,1)S(1)} %constant_dynamic-slice_fusion.2) | copy-start | bytes 786436
  29.2 15.7 %collective-permute-start.17 = (f32[2,8]{1,0:T(2,128)S(1)}, f32[2,8]{1,0:T(2,128)S(1)}, u32[]{:S(2)}, u32[]{:S(2)}) collective-permute-start(f32[2,8]{1,0:T(2,128)S(1)} %pad_maximum_fusion.4), channel_id=1, source_target_pairs={{0,32},{16,48},{32,0},{48,16},{64,96},{80,112},{96,64},{112,80},{1... | collective-permute-start | bytes 200 | tf_op jit(solution)/shard_map/ppermute | solution.py:30
  29.3 7.2 %collective-permute-start.2 = (bf16[128,512]{1,0:T(8,128)(2,1)S(1)}, bf16[128,512]{1,0:T(8,128)(2,1)S(1)}, u32[]{:S(2)}, u32[]{:S(2)}) collective-permute-start(bf16[128,512]{1,0:T(8,128)(2,1)S(1)} %slice.97), channel_id=1, source_target_pairs={{0,1},{1,2},{2,3},{3,0},{4,5},{5,6},{6,7},{7,4},{8,9},{9,10},{10,1... | collective-permute-start | bytes 393224 | tf_op jit(solution)/shard_map/ppermute | solution.py:21
  29.4 7.8 %collective-permute-start.3 = (bf16[128,512]{1,0:T(8,128)(2,1)S(1)}, bf16[128,512]{1,0:T(8,128)(2,1)S(1)}, u32[]{:S(2)}, u32[]{:S(2)}) collective-permute-start(bf16[128,512]{1,0:T(8,128)(2,1)S(1)} %slice.98), channel_id=1, source_target_pairs={{0,3},{1,0},{2,1},{3,2},{4,7},{5,4},{6,5},{7,6},{8,11},{9,8},{10,9... | collective-permute-start | bytes 393224 | tf_op jit(solution)/shard_map/ppermute | solution.py:21
  32.2 8.7 %collective-permute-start.10 = (bf16[128,512]{1,0:T(8,128)(2,1)S(1)}, bf16[128,512]{1,0:T(8,128)(2,1)S(1)}, u32[]{:S(2)}, u32[]{:S(2)}) collective-permute-start(bf16[128,512]{1,0:T(8,128)(2,1)S(1)} %slice.101), channel_id=1, source_target_pairs={{0,4},{1,5},{2,6},{3,7},{4,8},{5,9},{6,10},{7,11},{8,12},{9,13},{1... | collective-permute-start | bytes 393224 | tf_op jit(solution)/shard_map/ppermute | solution.py:26
  32.3 9.3 %collective-permute-start.11 = (bf16[128,512]{1,0:T(8,128)(2,1)S(1)}, bf16[128,512]{1,0:T(8,128)(2,1)S(1)}, u32[]{:S(2)}, u32[]{:S(2)}) collective-permute-start(bf16[128,512]{1,0:T(8,128)(2,1)S(1)} %slice.102), channel_id=1, source_target_pairs={{0,12},{1,13},{2,14},{3,15},{4,0},{5,1},{6,2},{7,3},{8,4},{9,5},{1... | collective-permute-start | bytes 393224 | tf_op jit(solution)/shard_map/ppermute | solution.py:26
  36.5 1.1 copy-start.3
  38.2 24.9 %collective-permute-start.4 = (bf16[1024,512]{1,0:T(8,128)(2,1)}, bf16[1024,512]{1,0:T(8,128)(2,1)S(1)}, u32[]{:S(2)}, u32[]{:S(2)}) collective-permute-start(bf16[1024,512]{1,0:T(8,128)(2,1)} %constant_dynamic-update-slice_fusion.refs_0_), channel_id=1, source_target_pairs={{0,4},{1,5},{2,6},{3,7},{4,8},{5,9},{6,10},{7,11},{8,12},{9,13},{1... | collective-permute-start | bytes 3145736 | tf_op jit(solution)/shard_map/ppermute | solution.py:26
  38.2 25.0 %collective-permute-start.5 = (bf16[1024,512]{1,0:T(8,128)(2,1)}, bf16[1024,512]{1,0:T(8,128)(2,1)S(1)}, u32[]{:S(2)}, u32[]{:S(2)}) collective-permute-start(bf16[1024,512]{1,0:T(8,128)(2,1)} %constant_dynamic-update-slice_fusion.refs_0_), channel_id=1, source_target_pairs={{0,12},{1,13},{2,14},{3,15},{4,0},{5,1},{6,2},{7,3},{8,4},{9,5},{1... | collective-permute-start | bytes 3145736 | tf_op jit(solution)/shard_map/ppermute | solution.py:26
  42.2 24.3 %collective-permute-start.12 = (bf16[1024,512]{1,0:T(8,128)(2,1)}, bf16[1024,512]{1,0:T(8,128)(2,1)}, u32[]{:S(2)}, u32[]{:S(2)}) collective-permute-start(bf16[1024,512]{1,0:T(8,128)(2,1)} %constant_dynamic-update-slice_fusion.5.refs_5_), channel_id=1, source_target_pairs={{0,1},{1,2},{2,3},{3,0},{4,5},{5,6},{6,7},{7,4},{8,9},{9,10},{10,1... | collective-permute-start | bytes 3145736 | tf_op jit(solution)/shard_map/ppermute | solution.py:21
  42.2 25.5 %collective-permute-start.13 = (bf16[1024,512]{1,0:T(8,128)(2,1)}, bf16[1024,512]{1,0:T(8,128)(2,1)}, u32[]{:S(2)}, u32[]{:S(2)}) collective-permute-start(bf16[1024,512]{1,0:T(8,128)(2,1)} %constant_dynamic-update-slice_fusion.5.refs_5_), channel_id=1, source_target_pairs={{0,3},{1,0},{2,1},{3,2},{4,7},{5,4},{6,5},{7,6},{8,11},{9,8},{10,9... | collective-permute-start | bytes 3145736 | tf_op jit(solution)/shard_map/ppermute | solution.py:21
  44.9 4.3 %collective-permute-start.18 = (f32[4,8]{1,0:T(4,128)S(1)}, f32[4,8]{1,0:T(4,128)S(1)}, u32[]{:S(2)}, u32[]{:S(2)}) collective-permute-start(f32[4,8]{1,0:T(4,128)S(1)} %pad_maximum_fusion.2), channel_id=1, source_target_pairs={{0,64},{16,80},{32,96},{48,112},{64,0},{80,16},{96,32},{112,48},{1... | collective-permute-start | bytes 392 | tf_op jit(solution)/shard_map/ppermute | solution.py:30
  49.3 6.6 %collective-permute-start.19 = (f32[8,8]{1,0:T(8,128)S(1)}, f32[8,8]{1,0:T(8,128)S(1)}, u32[]{:S(2)}, u32[]{:S(2)}) collective-permute-start(f32[8,8]{1,0:T(8,128)S(1)} %pad_maximum_fusion.1), channel_id=1, source_target_pairs={{0,128},{16,144},{32,160},{48,176},{64,192},{80,208},{96,224},{112... | collective-permute-start | bytes 776 | tf_op jit(solution)/shard_map/ppermute | solution.py:30
  63.1 12.6 %collective-permute-start.6 = (bf16[512,512]{1,0:T(8,128)(2,1)S(1)}, bf16[512,512]{1,0:T(8,128)(2,1)S(1)}, u32[]{:S(2)}, u32[]{:S(2)}) collective-permute-start(bf16[512,512]{1,0:T(8,128)(2,1)S(1)} %slice.99), channel_id=1, source_target_pairs={{0,4},{1,5},{2,6},{3,7},{4,8},{5,9},{6,10},{7,11},{8,12},{9,13},{1... | collective-permute-start | bytes 1572872 | tf_op jit(solution)/shard_map/ppermute | solution.py:26
  63.3 12.4 %collective-permute-start.7 = (bf16[512,512]{1,0:T(8,128)(2,1)S(1)}, bf16[512,512]{1,0:T(8,128)(2,1)S(1)}, u32[]{:S(2)}, u32[]{:S(2)}) collective-permute-start(bf16[512,512]{1,0:T(8,128)(2,1)S(1)} %slice.100), channel_id=1, source_target_pairs={{0,12},{1,13},{2,14},{3,15},{4,0},{5,1},{6,2},{7,3},{8,4},{9,5},{1... | collective-permute-start | bytes 1572872 | tf_op jit(solution)/shard_map/ppermute | solution.py:26
  67.6 11.9 %collective-permute-start.14 = (bf16[512,512]{1,0:T(8,128)(2,1)S(1)}, bf16[512,512]{1,0:T(8,128)(2,1)S(1)}, u32[]{:S(2)}, u32[]{:S(2)}) collective-permute-start(bf16[512,512]{1,0:T(8,128)(2,1)S(1)} %slice.103), channel_id=1, source_target_pairs={{0,1},{1,2},{2,3},{3,0},{4,5},{5,6},{6,7},{7,4},{8,9},{9,10},{10,1... | collective-permute-start | bytes 1572872 | tf_op jit(solution)/shard_map/ppermute | solution.py:21
  68.8 11.5 %collective-permute-start.15 = (bf16[512,512]{1,0:T(8,128)(2,1)S(1)}, bf16[512,512]{1,0:T(8,128)(2,1)S(1)}, u32[]{:S(2)}, u32[]{:S(2)}) collective-permute-start(bf16[512,512]{1,0:T(8,128)(2,1)S(1)} %slice.104), channel_id=1, source_target_pairs={{0,3},{1,0},{2,1},{3,2},{4,7},{5,4},{6,5},{7,6},{8,11},{9,8},{10,9... | collective-permute-start | bytes 1572872 | tf_op jit(solution)/shard_map/ppermute | solution.py:21
  71.6 0.6 copy-start.16
  75.7 0.8 copy-start.5
  79.5 0.8 copy-start.7
  80.3 0.8 copy-start.9
  81.1 1.2 copy-start.4
  82.3 1.0 copy-start.6
  83.4 1.0 copy-start.8
  84.4 1.0 copy-start.10
  97.0 3.3 %copy-start.1 = (bf16[16,512,512]{2,1,0:T(8,128)(2,1)}, bf16[16,512,512]{2,1,0:T(8,128)(2,1)S(1)}, u32[]{:S(2)}) copy-start(bf16[16,512,512]{2,1,0:T(8,128)(2,1)S(1)} %get-tuple-element.7.rows_ref) | copy-start | bytes 25165828
  100.2 0.8 copy-start.11
  104.2 5.3 %collective-permute-start.20 = (bf16[8,64,256]{2,1,0:T(8,128)(2,1)S(1)}, bf16[8,64,256]{2,1,0:T(8,128)(2,1)S(1)}, u32[]{:S(2)}, u32[]{:S(2)}) collective-permute-start(bf16[8,64,256]{2,1,0:T(8,128)(2,1)S(1)} %get-tuple-element.35), channel_id=1, source_target_pairs={{0,16},{16,0},{32,48},{48,32},{64,80},{80,64},{96,112},{112,96},{1... | collective-permute-start | bytes 786440 | tf_op jit(solution)/shard_map/ppermute | solution.py:30
  110.3 9.7 %collective-permute-start.23 = (bf16[4,64,256]{2,1,0:T(8,128)(2,1)S(1)}, bf16[4,64,256]{2,1,0:T(8,128)(2,1)S(1)}, u32[]{:S(2)}, u32[]{:S(2)}) collective-permute-start(bf16[4,64,256]{2,1,0:T(8,128)(2,1)S(1)} %fusion.27), channel_id=1, source_target_pairs={{0,96},{16,112},{32,64},{48,80},{64,32},{80,48},{96,0},{112,16},{1... | collective-permute-start | bytes 393224 | tf_op jit(solution)/shard_map/ppermute | solution.py:30
  113.0 18.1 %collective-permute-start.22 = (bf16[4,64,256]{2,1,0:T(8,128)(2,1)S(1)}, bf16[4,64,256]{2,1,0:T(8,128)(2,1)S(1)}, u32[]{:S(2)}, u32[]{:S(2)}) collective-permute-start(bf16[4,64,256]{2,1,0:T(8,128)(2,1)S(1)} %fusion.27), channel_id=1, source_target_pairs={{0,64},{16,80},{32,96},{48,112},{64,0},{80,16},{96,32},{112,48},{1... | collective-permute-start | bytes 393224 | tf_op jit(solution)/shard_map/ppermute | solution.py:30
  113.2 17.9 %collective-permute-start.21 = (bf16[4,64,256]{2,1,0:T(8,128)(2,1)S(1)}, bf16[4,64,256]{2,1,0:T(8,128)(2,1)S(1)}, u32[]{:S(2)}, u32[]{:S(2)}) collective-permute-start(bf16[4,64,256]{2,1,0:T(8,128)(2,1)S(1)} %fusion.27), channel_id=1, source_target_pairs={{0,32},{16,48},{32,0},{48,16},{64,96},{80,112},{96,64},{112,80},{1... | collective-permute-start | bytes 393224 | tf_op jit(solution)/shard_map/ppermute | solution.py:30
  132.0 11.4 %collective-permute-start.24 = (bf16[4,64,256]{2,1,0:T(8,128)(2,1)S(1)}, bf16[4,64,256]{2,1,0:T(8,128)(2,1)S(1)}, u32[]{:S(2)}, u32[]{:S(2)}) collective-permute-start(bf16[4,64,256]{2,1,0:T(8,128)(2,1)S(1)} %get-tuple-element.23), channel_id=1, source_target_pairs={{0,224},{16,240},{32,192},{48,208},{64,160},{80,176},{96,128},{112... | collective-permute-start | bytes 393224 | tf_op jit(solution)/shard_map/ppermute | solution.py:262
  143.5 4.9 %collective-permute-start.25 = (bf16[3,4,64,256]{3,2,1,0:T(8,128)(2,1)S(1)}, bf16[3,4,64,256]{3,2,1,0:T(8,128)(2,1)S(1)}, u32[]{:S(2)}, u32[]{:S(2)}) collective-permute-start(bf16[3,4,64,256]{3,2,1,0:T(8,128)(2,1)S(1)} %pad_maximum_fusion), channel_id=1, source_target_pairs={{0,16},{16,0},{32,48},{48,32},{64,80},{80,64},{96,112},{112,96},{1... | collective-permute-start | bytes 1179656 | tf_op jit(solution)/shard_map/ppermute | solution.py:30
  144.3 4.2 %copy-start.14 = (bf16[512,1,1,256]{3,2,1,0:T(2,128)(2,1)S(1)}, bf16[512,1,1,256]{3,2,1,0:T(2,128)(2,1)}, u32[]{:S(2)}) copy-start(bf16[512,1,1,256]{3,2,1,0:T(2,128)(2,1)} %copy-done.13) | copy-start | bytes 786436
  144.3 5.0 %copy-start.18 = (f32[8]{0:T(128)S(1)}, f32[8]{0:T(128)}, u32[]{:S(2)}) copy-start(f32[8]{0:T(128)} %param.16) | copy-start | bytes 100
  148.4 2.1 %copy-start.12 = (f32[512]{0:T(512)S(1)}, f32[512]{0:T(512)}, u32[]{:S(2)}) copy-start(f32[512]{0:T(512)} %param.17) | copy-start | bytes 6148
  150.5 3.4 %copy-start.2 = (bf16[16,512,512]{2,1,0:T(8,128)(2,1)S(1)}, bf16[16,512,512]{2,1,0:T(8,128)(2,1)}, u32[]{:S(2)}) copy-start(bf16[16,512,512]{2,1,0:T(8,128)(2,1)} %copy-done.1) | copy-start | bytes 25165828
Sparse Core Ops, SparseCore 0:
  9.2 60.2 all-gather.2
  71.4 61.2 all-gather.4

commit v2 on v1

v2 whole, which is shorter than its diff:
```python
import jax
import jax.numpy as jnp
from jax import lax
from jax.experimental import pallas as pl
from jax.experimental.pallas import tpu as pltpu
from jax.sharding import PartitionSpec as P

HEAD_DIM = 64
STATE = 256
HPG = 32
LEVELS = 6
HIGH = lax.Precision.HIGHEST
CTX = 16
SIDE = 4
HBM = pl.BlockSpec(memory_space=pltpu.HBM)
VMEM = pl.BlockSpec(memory_space=pltpu.VMEM)


def along_x(a, step):
    pairs = [(i, (i // SIDE) * SIDE + (i + step) % SIDE) for i in range(SIDE * SIDE)]
    return lax.ppermute(a, "tp", pairs)


def along_y(a, step):
    pairs = [(i, (i + SIDE * step) % (SIDE * SIDE)) for i in range(SIDE * SIDE)]
    return lax.ppermute(a, "tp", pairs)


def swap_ctx(a, mask):
    return lax.ppermute(a, "ctx", [(i, i ^ mask) for i in range(CTX)])


OFFSETS = (0, -1, 1, 2)


def in_hbm(*arrays):
    return [pltpu.with_memory_space_constraint(a, pltpu.HBM) for a in arrays]


def copies(moves, sem):
    started = []
    for i, (source, target) in enumerate(moves):
        copy = pltpu.make_async_copy(source, target, sem.at[i])
        copy.start()
        started.append(copy)
    for copy in started:
        copy.wait()


def stack_kernel(*refs):
    sources, targets = refs[:10], refs[10:12]
    held, in_sem, out_sem = refs[12:]
    moves = []
    for line in range(2):
        at = 0
        for source in sources[5 * line : 5 * line + 5]:
            rows = source.shape[0]
            moves.append((source, held.at[line, pl.ds(at, rows)]))
            at += rows
    copies(moves, in_sem)
    copies([(held.at[line], targets[line]) for line in range(2)], out_sem)


def stack(line_a, line_b):
    rows = sum(a.shape[0] for a in line_a)
    cols = line_a[0].shape[1]
    shape = jax.ShapeDtypeStruct((rows, cols), jnp.bfloat16)
    return pl.pallas_call(
        stack_kernel,
        out_shape=(shape, shape),
        in_specs=[HBM] * 10,
        out_specs=(HBM, HBM),
        scratch_shapes=[
            pltpu.VMEM((2, rows, cols), jnp.bfloat16),
            pltpu.SemaphoreType.DMA((10,)),
            pltpu.SemaphoreType.DMA((2,)),
        ],
    )(*in_hbm(*line_a, *line_b))


def gather_rows(rows):
    half = rows.shape[0] // 2
    top, bottom = rows[:half], rows[half:]
    near = along_x(top, 1), along_x(top, -1), along_y(bottom, 1), along_y(bottom, -1)
    cut = half // 2
    part = (near[0][:cut], near[1][cut:], near[2][:cut], near[3][cut:])
    far = along_x(part[0], 1), along_x(part[1], -1), along_y(part[2], 1), along_y(part[3], -1)
    line_a, line_b = stack((top, *near[:2], *far[:2]), (bottom, *near[2:], *far[2:]))
    next_ = along_y(line_a, 1), along_y(line_a, -1), along_x(line_b, 1), along_x(line_b, -1)
    part = (next_[0][: 2 * half], next_[1][2 * half :], next_[2][: 2 * half], next_[3][2 * half :])
    last = along_y(part[0], 1), along_y(part[1], -1), along_x(part[2], 1), along_x(part[3], -1)
    return (line_a, *next_[:2], *last[:2]), (line_b, *next_[2:], *last[2:])


def fetch_weights(w_ref, weights, sem, k, slot, depth):
    apart = w_ref.shape[0] // 16
    pltpu.make_async_copy(
        w_ref.at[pl.ds(pl.multiple_of(k * apart, 16), depth)],
        weights.at[pl.ds(slot * depth, depth)],
        sem.at[slot],
    ).start()


def sources_of_slots():
    tp = lax.axis_index("tp")
    y, x = tp // SIDE, tp % SIDE
    return [
        (i, j, ((y + dy + SIDE) % SIDE) * SIDE + (x + dx + SIDE) % SIDE)
        for j, dy in enumerate(OFFSETS)
        for i, dx in enumerate(OFFSETS)
    ]


def multiply(rows, weights, total, row_sem, weight_sem):
    deep = rows.shape[1]
    depth = deep // 16
    group = 4
    for first in range(0, 16, group):
        for s in range(first, first + group):
            columns = pl.ds(s * depth, depth)
            pltpu.make_async_copy(rows.at[:, columns], rows.at[:, columns], row_sem.at[s]).wait()
            pltpu.make_async_copy(weights.at[columns], weights.at[columns], weight_sem.at[s]).wait()
        span = pl.ds(first * depth, group * depth)
        product = jnp.dot(rows[:, span], weights[span], preferred_element_type=jnp.float32)
        if first == 0:
            total[...] = product
        else:
            total[...] += product


def project_cost(tok, cols, deep):
    return pl.CostEstimate(
        flops=2 * tok * cols * deep, bytes_accessed=2 * deep * (tok + cols), transcendentals=0
    )


def fetch_and_multiply(refs, w_ref, rows, weights, total, row_sem, weight_sem):
    pieces_a, pieces_b = refs[0:5], refs[5:10]
    tok, deep = rows.shape
    depth = deep // 16
    part = tok // 2

    def piece(pieces, near, far):
        if far < 3:
            return pieces[far].at[pl.ds(near * part, part)]
        return pieces[3 + near // 2].at[pl.ds((near % 2) * part, part)]

    for slot, (i, j, k) in enumerate(sources_of_slots()):
        columns = pl.ds(slot * depth, depth)
        pltpu.make_async_copy(
            piece(pieces_a, i, j), rows.at[pl.ds(0, part), columns], row_sem.at[slot]
        ).start()
        pltpu.make_async_copy(
            piece(pieces_b, j, i), rows.at[pl.ds(part, part), columns], row_sem.at[slot]
        ).start()
        fetch_weights(w_ref, weights, weight_sem, k, slot, depth)
    multiply(rows, weights, total, row_sem, weight_sem)


def project_scratch(tok, cols, deep):
    return [
        pltpu.VMEM((tok, deep), jnp.bfloat16),
        pltpu.VMEM((deep, cols), jnp.bfloat16),
        pltpu.VMEM((tok, cols), jnp.float32),
        pltpu.SemaphoreType.DMA((16,)),
        pltpu.SemaphoreType.DMA((16,)),
    ]


def values_kernel(*refs):
    values_out, total = refs[11], refs[14]
    fetch_and_multiply(refs[:10], refs[10], *refs[12:])
    values_out[...] = total[...].astype(values_out.dtype)


def project_values(pieces, w_full, tok, depth):
    cols = w_full.shape[1]
    deep = 16 * depth
    return pl.pallas_call(
        values_kernel,
        out_shape=jax.ShapeDtypeStruct((tok, cols), jnp.bfloat16),
        in_specs=[HBM] * 11,
        out_specs=VMEM,
        scratch_shapes=project_scratch(tok, cols, deep),
        compiler_params=pltpu.CompilerParams(vmem_limit_bytes=40 * 2**20),
        cost_estimate=project_cost(tok, cols, deep),
    )(*in_hbm(*pieces, w_full))


def gates_kernel(*refs):
    mixed_ref, gain_ref, out_ref = refs[11:14]
    total = refs[16]
    fetch_and_multiply(refs[:10], refs[10], *refs[14:])
    tok, cols = total.shape
    lanes = 128
    owner = lax.broadcasted_iota(jnp.int32, (cols, lanes), 0) // HEAD_DIM
    head = lax.broadcasted_iota(jnp.int32, (cols, lanes), 1)
    pick = jnp.where(owner == head, 1.0, 0.0).astype(jnp.bfloat16)
    gain = gain_ref[...]

    def select(a, axis):
        high = a.astype(jnp.bfloat16)
        low = (a - high.astype(jnp.float32)).astype(jnp.bfloat16)
        dims = (((1,), (axis,)), ((), ()))
        return lax.dot_general(high, pick, dims, preferred_element_type=jnp.float32) + lax.dot_general(
            low, pick, dims, preferred_element_type=jnp.float32
        )

    chunk = 64
    for first in range(0, tok, chunk):
        span = pl.ds(first, chunk)
        gates = total[span].astype(jnp.bfloat16).astype(jnp.float32)
        gated = mixed_ref[span] * (gates / (1.0 + jnp.exp(-gates)))
        inverse = lax.rsqrt(select(gated * gated, 0) * (1.0 / HEAD_DIM) + 1e-05)
        out_ref[span] = (gated * select(inverse, 1) * gain).astype(out_ref.dtype)


def finish(pieces, w_full, mixed, gain):
    deep, cols = w_full.shape
    tok = mixed.shape[0]
    return pl.pallas_call(
        gates_kernel,
        out_shape=jax.ShapeDtypeStruct((tok, cols), jnp.bfloat16),
        in_specs=[HBM] * 11 + [VMEM, VMEM],
        out_specs=VMEM,
        scratch_shapes=project_scratch(tok, cols, deep),
        compiler_params=pltpu.CompilerParams(vmem_limit_bytes=40 * 2**20),
        cost_estimate=project_cost(tok, cols, deep),
    )(*in_hbm(*pieces, w_full), mixed, gain)


def on_device(
    hidden_rows,
    w_value,
    w_gate,
    state_proj,
    rates,
    read_weights,
    prior_state,
    skip_weight,
    norm_gain,
):
    tok, heads = rates.shape
    me = lax.axis_index("ctx")
    core = me % 2
    plane = me // 2

    depth = hidden_rows.shape[1]

    rest = jnp.sum(rates, axis=0)
    terms = []
    for _ in range(3):
        terms.append(lax.reduce_precision(rest, 8, 7))
        rest = rest - terms[-1]
    tail = jnp.pad(jnp.stack(terms).astype(jnp.bfloat16), ((0, 13), (0, w_value.shape[1] - heads)))
    value_weights = lax.all_gather(
        jnp.concatenate([w_value, tail], axis=0), "ctx", axis=0, tiled=True
    )
    gate_weights = lax.all_gather(w_gate, "ctx", axis=0, tiled=True)
    pieces_a, pieces_b = gather_rows(hidden_rows)
    group = lax.axis_index("tp") * heads // HPG
    rates, prior_state, read_weights, group, line = lax.optimization_barrier(
        (rates, prior_state, read_weights, group, pieces_a[0])
    )
    pieces = (line, *pieces_a[1:], *pieces_b)

    order = jnp.arange(tok)
    causal = order[:, None] >= order[None, :]
    cum_rate = jnp.dot(causal.astype(jnp.float32), rates, precision=HIGH)
    totals = value_weights.reshape(CTX, depth + 16, -1)[:, depth : depth + 3, :heads]
    totals = jnp.sum(totals.astype(jnp.float32), axis=1)
    block = jnp.arange(CTX, dtype=jnp.int32)
    start_rate = jnp.sum(jnp.where((block < me)[:, None], totals, 0.0), axis=0)

    write_vec = lax.dynamic_index_in_dim(state_proj[:, 0], group, 1, keepdims=False)
    read_vec = lax.dynamic_index_in_dim(state_proj[:, 1], group, 1, keepdims=False)
    scores = lax.dot_general(
        read_vec, write_vec, (((1,), (1,)), ((), ())), preferred_element_type=jnp.float32
    )

    values = project_values(pieces, value_weights, tok, depth)
    values3 = values.reshape(tok, heads, HEAD_DIM)

    span_total = cum_rate[tok - 1]
    write_weighted = (
        jnp.exp(-(span_total[None] - cum_rate))[:, :, None]
        * write_vec[:, None, :].astype(jnp.float32)
    ).astype(jnp.bfloat16)
    ends = jnp.einsum(
        "thn,thp->hpn", write_weighted, values3, preferred_element_type=jnp.float32
    )

    mine = ends.astype(jnp.bfloat16)
    sibling = swap_ctx(mine, 1)
    my_total = lax.dynamic_index_in_dim(totals, me, 0, keepdims=False)
    sibling_total = lax.dynamic_index_in_dim(totals, me ^ 1, 0, keepdims=False)

    def fade(rate):
        return jnp.exp(-rate)

    own_scale = jnp.where(core == 0, fade(sibling_total), 1.0)
    sibling_scale = jnp.where(core == 0, 1.0, fade(my_total))
    plane_end = own_scale[:, None, None] * ends + sibling_scale[:, None, None] * sibling.astype(jnp.float32)
    share = heads // 2
    plane_share = lax.dynamic_slice_in_dim(plane_end, core * share, share, 0)
    plane_sent = plane_share.astype(jnp.bfloat16)
    near = [swap_ctx(plane_sent, 2 * m).astype(jnp.float32) for m in (1, 2, 3)]
    plane_totals = totals.reshape(CTX // 2, 2, heads).sum(axis=1)
    share_totals = lax.dynamic_slice_in_dim(plane_totals, core * share, share, 1)
    all_planes = jnp.arange(CTX // 2, dtype=jnp.int32)
    near_all = [plane_share, *near]

    def faded_sum(among):
        result = 0.0
        for m in among:
            here = (plane ^ among[0]) // len(among)
            after = (all_planes // len(among) == here) & (all_planes > (plane ^ m))
            later = jnp.sum(jnp.where(after[:, None], share_totals, 0.0), axis=0)
            result = result + fade(later)[:, None, None] * near_all[m]
        return result

    pair_sum = faded_sum((2, 3)).astype(jnp.bfloat16)
    quad_sum = faded_sum((0, 1, 2, 3)).astype(jnp.bfloat16)
    quad_other = lax.ppermute(
        quad_sum, "ctx", [(2 * z + c, 2 * (7 - z) + c) for z in range(4) for c in range(2)]
    )
    shared = jnp.stack([near[0].astype(jnp.bfloat16), pair_sum, quad_other])
    shared_other = swap_ctx(shared, 1)
    lower = jnp.where(core == 0, shared, shared_other)
    upper = jnp.where(core == 0, shared_other, shared)
    states = jnp.concatenate([sibling[None], jnp.concatenate([lower, upper], axis=1)], axis=0)

    level_fade = []
    for level in range(4):
        last = (me >> level << level) - 1
        there = (me >> level) & 1
        since = jnp.sum(
            jnp.where(((block > last) & (block < me))[:, None], totals, 0.0), axis=0
        )
        level_fade.append(jnp.where(there == 1, fade(since), 0.0))
    level_fade = jnp.stack(level_fade)

    prior_read = jnp.einsum(
        "tn,hpn->thp", read_vec.astype(jnp.float32), prior_state, precision=HIGH
    )
    cum_fade = jnp.exp(-cum_rate)
    rate_lag = cum_rate.T[:, :, None] - cum_rate.T[:, None, :]
    mixing = (
        jnp.where(causal[None], jnp.exp(-jnp.where(causal[None], rate_lag, 0.0)), 0.0) * scores[None]
    ).astype(jnp.bfloat16)
    local_out = jnp.einsum("hts,shp->thp", mixing, values3, preferred_element_type=jnp.float32)
    prior_scale = read_weights[5] * (cum_fade * fade(start_rate)[None])
    early = (
        read_weights[0][:, :, None] * local_out
        + prior_scale[:, :, None] * prior_read
        + skip_weight[None, :, None] * values3.astype(jnp.float32)
    )
    level_read = jnp.einsum(
        "tn,lhpn->lthp", read_vec, states, preferred_element_type=jnp.float32
    )
    level_scale = read_weights[1:5] * (cum_fade[None] * level_fade[:, None])
    mixed = early + jnp.sum(level_scale[:, :, :, None] * level_read, axis=0)

    return finish(
        pieces, gate_weights, mixed.reshape(tok, heads * HEAD_DIM), norm_gain[None]
    )


def solution(mesh):
    in_specs = (
        P("ctx", "tp"),
        P("ctx", "tp"),
        P("ctx", "tp"),
        P("ctx", None, None, None),
        P("ctx", "tp"),
        P(None, "ctx", "tp"),
        P("tp", None, None),
        P("tp"),
        P("tp"),
    )
    out_specs = P("ctx", "tp")
    return jax.shard_map(
        on_device, mesh=mesh, in_specs=in_specs, out_specs=out_specs, check_vma=False
    )
```

time: 174 us -> 156 us (0.90)
  local copies, waits for them, and re-layouts: 30.7 us -> 12.8 us
  waiting for transfers between devices: 34.4 us -> 45.8 us
  starting transfers between devices: 48.7 us -> 44.7 us
  matrix products: 9.96 us -> 7.1 us
  Pallas kernels: 24.3 us -> 21.8 us
  other arithmetic: 11.7 us -> 9.6 us
    unnamed x44, local copies, waits for them, and re-layouts: 17.9 us -> 0.8 us
    ppermute x9 -> x5, starting transfers between devices: 20.3 us -> 14.5 us  [swap_ctx(): return lax.ppermute(a, 'ctx', [(i, i ^ mask) for i in range(CTX)])]
    ppermute x8, waiting for transfers between devices: 3.58 us -> 9.38 us  [along_x(): return lax.ppermute(a, 'tp', pairs)]
    all_gather x1, waiting for transfers between devices: 0.02 us -> 4.78 us  [on_device(): gate_weights = lax.all_gather(w_gate, 'ctx', axis=0, tiled=True)]
    select_n x4, other arithmetic: 2.3 us -> 0.02 us  [on_device(): level_fade.append(jnp.where(there == 1, fade(since), 0.0))]
    pallas_call x1, Pallas kernels: 12.8 us -> 10.7 us  [finish(): pl.pallas_call(gates_kernel, out_shape=jax.ShapeDtypeStruct((tok, cols),...]
    concatenate x3 -> x1, other arithmetic: 0.03 us -> 1.92 us  [on_device(): jnp.concatenate([w_value, tail], axis=0)]
    reduce_sum x2 -> x5, other arithmetic: 1.35 us -> 3.2 us  [the longest x1 0.89 us: on_device(): rest = jnp.sum(rates, axis=0)]
  transfers between devices with their start and end apart: 28 -> 24, of which waited for: 9 -> 12; matrix products, arithmetic and copies ran while one was open for 21% -> 17% of each run, Pallas kernels for 7% -> 7%
where the time goes in v2:
time: 156 us
  waiting for transfers between devices  45.8 us (29%)
  starting transfers between devices  44.7 us (29%)
  Pallas kernels  21.8 us (14%)
  between operations  13.9 us (9%)
  local copies, waits for them, and re-layouts  12.8 us (8%)
  other arithmetic  9.6 us (6%)
  matrix products  7.1 us (5%)
    ppermute x5, waiting for transfers between devices, swap_ctx(): return lax.ppermute(a, 'ctx', [(i, i ^ mask) for i in range(CTX)])  18.4 us
    ppermute x5, starting transfers between devices, swap_ctx(): return lax.ppermute(a, 'ctx', [(i, i ^ mask) for i in range(CTX)])  14.5 us
    ppermute x8, starting transfers between devices, along_y(): return lax.ppermute(a, 'tp', pairs)  12.8 us
    ppermute x8, starting transfers between devices, along_x(): return lax.ppermute(a, 'tp', pairs)  12.3 us
    pallas_call x1, Pallas kernels, finish(): pl.pallas_call(gates_kernel, out_shape=jax.ShapeDtypeStruct((tok, cols),...  10.7 us
    ppermute x8, waiting for transfers between devices, along_x(): return lax.ppermute(a, 'tp', pairs)  9.38 us
    pallas_call x1, Pallas kernels, project_values(): pl.pallas_call(values_kernel, out_shape=jax.ShapeDtypeStruct((tok, cols),...  8.09 us
    ppermute x8, waiting for transfers between devices, along_y(): return lax.ppermute(a, 'tp', pairs)  6.6 us
  transfers between devices with their start and end apart: 24, of which 12 were waited for; matrix products, arithmetic and copies ran while one was open for 17% of the time, Pallas kernels for 7%

profile of v2, /device:TPU:1, one launch (start us, length us, event | category | flops | bytes accessed | tf_op | source)
XLA Modules:
  0.0 155.8 jit_solution(2940054414544214955)
XLA Ops:
  6.5 0.9 reduce_sum.137
  7.5 1.9 %pad_maximum_fusion = bf16[528,512]{1,0:T(8,128)(2,1)} fusion(bf16[16,512]{1,0:T(8,128)(2,1)S(1)} %fusion.38, bf16[512,512]{1,0:T(8,128)(2,1)} %param.10), kind=kLoop, calls=%fused_computation.21 | loop fusion | flops 1081344 | bytes 1081344 | tf_op jit(solution)/shard_map/concatenate | solution.py:257
  9.5 0.7 all-gather.3.cloned.1.call-update
  10.2 1.1 fusion.58
  11.3 2.1 %collective-permute-start = (bf16[256,512]{1,0:T(8,128)(2,1)S(1)}, bf16[256,512]{1,0:T(8,128)(2,1)S(1)}, u32[]{:S(2)}, u32[]{:S(2)}) collective-permute-start(bf16[256,512]{1,0:T(8,128)(2,1)S(1)} %get-tuple-element.35.refs_0_), channel_id=1, source_target_pairs={{0,1},{1,2},{2,3},{3,0},{4,5},{5,6},{6,7},{7,4},{8,9},{9,10},{10,1... | collective-permute-start | bytes 786440 | tf_op jit(solution)/shard_map/ppermute | solution.py:21
  13.4 1.4 collective-permute-start.1
  14.7 1.4 collective-permute-start.4
  16.1 1.4 collective-permute-start.5
  17.6 0.5 compare_and_fusion
  18.1 0.5 compare_and_fusion.2
  18.7 1.6 %collective-permute-start.2 = (bf16[128,512]{1,0:T(8,128)(2,1)S(1)}, bf16[128,512]{1,0:T(8,128)(2,1)S(1)}, u32[]{:S(2)}, u32[]{:S(2)}) collective-permute-start(bf16[128,512]{1,0:T(8,128)(2,1)S(1)} %slice.68), channel_id=1, source_target_pairs={{0,1},{1,2},{2,3},{3,0},{4,5},{5,6},{6,7},{7,4},{8,9},{9,10},{10,1... | collective-permute-start | bytes 393224 | tf_op jit(solution)/shard_map/ppermute | solution.py:21
  20.4 1.7 %collective-permute-start.3 = (bf16[128,512]{1,0:T(8,128)(2,1)S(1)}, bf16[128,512]{1,0:T(8,128)(2,1)S(1)}, u32[]{:S(2)}, u32[]{:S(2)}) collective-permute-start(bf16[128,512]{1,0:T(8,128)(2,1)S(1)} %slice.69), channel_id=1, source_target_pairs={{0,3},{1,0},{2,1},{3,2},{4,7},{5,4},{6,5},{7,6},{8,11},{9,8},{10,9... | collective-permute-start | bytes 393224 | tf_op jit(solution)/shard_map/ppermute | solution.py:21
  22.1 2.7 %collective-permute-start.6 = (bf16[128,512]{1,0:T(8,128)(2,1)S(1)}, bf16[128,512]{1,0:T(8,128)(2,1)S(1)}, u32[]{:S(2)}, u32[]{:S(2)}) collective-permute-start(bf16[128,512]{1,0:T(8,128)(2,1)S(1)} %slice.70), channel_id=1, source_target_pairs={{0,4},{1,5},{2,6},{3,7},{4,8},{5,9},{6,10},{7,11},{8,12},{9,13},{1... | collective-permute-start | bytes 393224 | tf_op jit(solution)/shard_map/ppermute | solution.py:26
  24.8 1.5 collective-permute-start.7
  26.4 0.6 compare_and_fusion.4
  27.1 1.5 collective-permute-done.6.refs_8_
  28.6 0.5 collective-permute-done.7.refs_9_
  29.2 0.6 copy-done.18
  29.9 3.0 %shard_map.91 = (bf16[1024,512]{1,0:T(8,128)(2,1)}, bf16[1024,512]{1,0:T(8,128)(2,1)}) custom-call(bf16[256,512]{1,0:T(8,128)(2,1)} %copy-done.9, bf16[256,512]{1,0:T(8,128)(2,1)} %copy-done.10, bf16[256,512]{1,0:T(8,128)(2,1)} %copy-done.11, bf16[128,512]{1,0:T(8,128)(2,1)} %copy-done.15, bf16[128,512]{1,0:T(8,128)(2,1)} %copy-done.16, ...), custom_call_target="tpu_custom_call" | custom-call | tf_op jit(solution)/shard_map/pallas_call | solution.py:68
  33.0 2.7 %collective-permute-start.13 = (bf16[1024,512]{1,0:T(8,128)(2,1)}, bf16[1024,512]{1,0:T(8,128)(2,1)S(1)}, u32[]{:S(2)}, u32[]{:S(2)}) collective-permute-start(bf16[1024,512]{1,0:T(8,128)(2,1)} %get-tuple-element.14.refs_5_), channel_id=1, source_target_pairs={{0,3},{1,0},{2,1},{3,2},{4,7},{5,4},{6,5},{7,6},{8,11},{9,8},{10,9... | collective-permute-start | bytes 3145736 | tf_op jit(solution)/shard_map/ppermute | solution.py:21
  35.7 1.2 collective-permute-start.8
  36.9 1.4 collective-permute-start.9
  38.3 0.5 iota_compare_fusion.4
  38.9 3.7 %fusion.57 = (bf16[512,1,4,256]{3,2,1,0:T(4,128)(2,1)}, bf16[512,1,4,256]{3,2,1,0:T(4,128)(2,1)}) fusion(bf16[512,2,4,256]{3,2,1,0:T(4,128)(2,1)} %param.12), kind=kLoop, calls=%fused_computation.133 | loop fusion | bytes 4194304 | tf_op jit(solution)/shard_map/slice | solution.py:276
  42.6 1.8 %constant_dynamic-slice_fusion.3 = bf16[512,1,1,256]{3,2,1,0:T(2,128)(2,1)S(1)} fusion(bf16[512,1,4,256]{3,2,1,0:T(4,128)(2,1)} %get-tuple-element.31, s32[]{:T(128)S(6)} %select_n.221), kind=kLoop, calls=%fused_computation.86 | loop fusion | bytes 524292 | tf_op jit(solution)/shard_map/jit(dynamic_index_in_dim)/dynamic_slice | solution.py:275
  44.4 1.8 %constant_dynamic-slice_fusion.4 = bf16[512,1,1,256]{3,2,1,0:T(2,128)(2,1)S(1)} fusion(bf16[512,1,4,256]{3,2,1,0:T(4,128)(2,1)} %get-tuple-element.30, s32[]{:T(128)S(6)} %select_n.221), kind=kLoop, calls=%fused_computation.87 | loop fusion | bytes 524292 | tf_op jit(solution)/shard_map/jit(dynamic_index_in_dim)/dynamic_slice | solution.py:276
  46.2 0.4 fusion.16
  46.6 9.4 %collective-permute-done.12.refs_6_ = bf16[1024,512]{1,0:T(8,128)(2,1)S(1)} collective-permute-done((bf16[1024,512]{1,0:T(8,128)(2,1)}, bf16[1024,512]{1,0:T(8,128)(2,1)S(1)}, u32[]{:S(2)}, u32[]{:S(2)}) %collective-permute-start.12) | collective-permute-done | bytes 1048608 | tf_op jit(solution)/shard_map/ppermute | solution.py:21
  56.2 2.7 %collective-permute-start.15 = (bf16[512,512]{1,0:T(8,128)(2,1)S(1)}, bf16[512,512]{1,0:T(8,128)(2,1)}, u32[]{:S(2)}, u32[]{:S(2)}) collective-permute-start(bf16[512,512]{1,0:T(8,128)(2,1)S(1)} %slice.75), channel_id=1, source_target_pairs={{0,3},{1,0},{2,1},{3,2},{4,7},{5,4},{6,5},{7,6},{8,11},{9,8},{10,9... | collective-permute-start | bytes 1572872 | tf_op jit(solution)/shard_map/ppermute | solution.py:21
  58.9 1.1 slice.72
  60.0 1.5 collective-permute-start.10
  61.5 1.1 slice.73
  62.6 1.5 collective-permute-start.11
  64.1 0.7 slice_reduce_fusion
  64.8 0.8 fusion.29
  65.6 1.3 fusion.25
  66.9 3.6 %collective-permute-done.10.refs_3_ = bf16[512,512]{1,0:T(8,128)(2,1)} collective-permute-done((bf16[512,512]{1,0:T(8,128)(2,1)S(1)}, bf16[512,512]{1,0:T(8,128)(2,1)}, u32[]{:S(2)}, u32[]{:S(2)}) %collective-permute-start.10) | collective-permute-done | bytes 524320 | tf_op jit(solution)/shard_map/ppermute | solution.py:26
  70.5 1.0 collective-permute-done.11.refs_4_
  71.5 8.1 %shard_map.92 = bf16[512,512]{1,0:T(8,128)(2,1)S(1)} custom-call(bf16[1024,512]{1,0:T(8,128)(2,1)} %get-tuple-element.13.refs_0_, bf16[1024,512]{1,0:T(8,128)(2,1)} %collective-permute-done.8.refs_1_, bf16[1024,512]{1,0:T(8,128)(2,1)} %collective-permute-done.9.refs_2_, bf16[512,512]{1,0:T(8,128)(2,1)} %collective-permute-done.10.refs_3_, ...), custom_call_target="tpu_custom_call" | custom-call | flops 4294967296 | bytes 16777216 | tf_op jit(solution)/shard_map/pallas_call | solution.py:179
  79.6 0.2 copy.22
  79.8 0.8 convert_reduce_fusion
  80.6 0.8 select_reduce_fusion.4
  81.4 0.7 bitcast_multiply_fusion.1
  82.1 0.8 fusion.59
  82.9 5.7 %collective-permute-start.16 = (bf16[8,64,256]{2,1,0:T(8,128)(2,1)S(1)}, bf16[8,64,256]{2,1,0:T(8,128)(2,1)S(1)}, u32[]{:S(2)}, u32[]{:S(2)}) collective-permute-start(bf16[8,64,256]{2,1,0:T(8,128)(2,1)S(1)} %get-tuple-element.46), channel_id=1, source_target_pairs={{0,16},{16,0},{32,48},{48,32},{64,80},{80,64},{96,112},{112,96},{1... | collective-permute-start | bytes 786440 | tf_op jit(solution)/shard_map/ppermute | solution.py:30
  88.6 0.7 select_reduce_fusion.10
  89.6 0.1 collective-permute-done.16
  89.8 0.1 fusion.27
  89.9 1.7 %collective-permute-start.17 = (bf16[4,64,256]{2,1,0:T(8,128)(2,1)S(1)}, bf16[4,64,256]{2,1,0:T(8,128)(2,1)S(1)}, u32[]{:S(2)}, u32[]{:S(2)}) collective-permute-start(bf16[4,64,256]{2,1,0:T(8,128)(2,1)S(1)} %fusion.27), channel_id=1, source_target_pairs={{0,32},{16,48},{32,0},{48,16},{64,96},{80,112},{96,64},{112,80},{1... | collective-permute-start | bytes 393224 | tf_op jit(solution)/shard_map/ppermute | solution.py:30
  91.5 3.0 %collective-permute-start.18 = (bf16[4,64,256]{2,1,0:T(8,128)(2,1)S(1)}, bf16[4,64,256]{2,1,0:T(8,128)(2,1)S(1)}, u32[]{:S(2)}, u32[]{:S(2)}) collective-permute-start(bf16[4,64,256]{2,1,0:T(8,128)(2,1)S(1)} %fusion.27), channel_id=1, source_target_pairs={{0,64},{16,80},{32,96},{48,112},{64,0},{80,16},{96,32},{112,48},{1... | collective-permute-start | bytes 393224 | tf_op jit(solution)/shard_map/ppermute | solution.py:30
  94.6 5.7 %collective-permute-done.17 = bf16[4,64,256]{2,1,0:T(8,128)(2,1)S(1)} collective-permute-done((bf16[4,64,256]{2,1,0:T(8,128)(2,1)S(1)}, bf16[4,64,256]{2,1,0:T(8,128)(2,1)S(1)}, u32[]{:S(2)}, u32[]{:S(2)}) %collective-permute-start.17) | collective-permute-done | bytes 131104 | tf_op jit(solution)/shard_map/ppermute | solution.py:30
  100.3 2.7 %collective-permute-done.18 = bf16[4,64,256]{2,1,0:T(8,128)(2,1)S(1)} collective-permute-done((bf16[4,64,256]{2,1,0:T(8,128)(2,1)S(1)}, bf16[4,64,256]{2,1,0:T(8,128)(2,1)S(1)}, u32[]{:S(2)}, u32[]{:S(2)}) %collective-permute-start.18) | collective-permute-done | bytes 131104 | tf_op jit(solution)/shard_map/ppermute | solution.py:30
  103.0 9.3 %collective-permute-done.19 = bf16[4,64,256]{2,1,0:T(8,128)(2,1)S(1)} collective-permute-done((bf16[4,64,256]{2,1,0:T(8,128)(2,1)S(1)}, bf16[4,64,256]{2,1,0:T(8,128)(2,1)S(1)}, u32[]{:S(2)}, u32[]{:S(2)}) %collective-permute-start.19) | collective-permute-done | bytes 131104 | tf_op jit(solution)/shard_map/ppermute | solution.py:30
  112.3 0.2 fusion.28
  112.5 5.0 %collective-permute-start.20 = (bf16[4,64,256]{2,1,0:T(8,128)(2,1)S(1)}, bf16[4,64,256]{2,1,0:T(8,128)(2,1)S(1)}, u32[]{:S(2)}, u32[]{:S(2)}) collective-permute-start(bf16[4,64,256]{2,1,0:T(8,128)(2,1)S(1)} %get-tuple-element.37), channel_id=1, source_target_pairs={{0,224},{16,240},{32,192},{48,208},{64,160},{80,176},{96,128},{112... | collective-permute-start | bytes 393224 | tf_op jit(solution)/shard_map/ppermute | solution.py:324
  117.6 5.9 %collective-permute-done.20 = bf16[4,64,256]{2,1,0:T(8,128)(2,1)S(1)} collective-permute-done((bf16[4,64,256]{2,1,0:T(8,128)(2,1)S(1)}, bf16[4,64,256]{2,1,0:T(8,128)(2,1)S(1)}, u32[]{:S(2)}, u32[]{:S(2)}) %collective-permute-start.20) | collective-permute-done | bytes 131104 | tf_op jit(solution)/shard_map/ppermute | solution.py:324
  123.5 4.1 %collective-permute-start.21 = (bf16[3,4,64,256]{3,2,1,0:T(8,128)(2,1)S(1)}, bf16[3,4,64,256]{3,2,1,0:T(8,128)(2,1)S(1)}, u32[]{:S(2)}, u32[]{:S(2)}) collective-permute-start(bf16[3,4,64,256]{3,2,1,0:T(8,128)(2,1)S(1)} %pad_maximum_fusion.1), channel_id=1, source_target_pairs={{0,16},{16,0},{32,48},{48,32},{64,80},{80,64},{96,112},{112,96},{1... | collective-permute-start | bytes 1179656 | tf_op jit(solution)/shard_map/ppermute | solution.py:30
  127.7 0.6 convolution_multiply_fusion
  128.3 0.6 collective-permute-done.21
  129.0 0.8 fusion
  129.8 3.3 %fusion.10 = f32[512,8,64]{0,2,1:T(8,128)S(1)} fusion(f32[512,8,64]{0,2,1:T(8,128)S(1)} %fusion, f32[512,8,64]{0,2,1:T(8,128)S(1)} %convolution_multiply_fusion, bf16[512,8,64]{0,2,1:T(8,128)(2,1)S(1)} %bitcast.76, f32[512,512]{1,0:T(8,128)S(1)} %copy-done.7, f32[8,512]{1,0:T(8,128)S(1)} %bitcast.81, pred[512,512]{1,0:T(8,128)(4,1)S(1)} %iota_compare_fusion, ...), kind=kOutput, calls=%fused_computation.14 | convolution fusion | flops 282591232 | bytes 5013536 | tf_op jit(solution)/shard_map/hts,shp->thp/dot_general | solution.py:351
  133.1 0.3 copy.31.refs_11_
  133.4 4.8 %all-gather.3.cloned.1.call-done.refs_10_ = bf16[8192,512]{1,0:T(8,128)(2,1)} async-done(((bf16[512,512]{1,0:T(8,128)(2,1)}), bf16[8192,512]{1,0:T(8,128)(2,1)}) %all-gather.3.cloned.1.call-update) | async-done | bytes 8388624 | tf_op jit(solution)/shard_map/all_gather | solution.py:259
  138.2 10.7 %shard_map.93 = bf16[512,512]{1,0:T(8,128)(2,1)} custom-call(bf16[1024,512]{1,0:T(8,128)(2,1)} %get-tuple-element.13.refs_0_, bf16[1024,512]{1,0:T(8,128)(2,1)} %collective-permute-done.8.refs_1_, bf16[1024,512]{1,0:T(8,128)(2,1)} %collective-permute-done.9.refs_2_, bf16[512,512]{1,0:T(8,128)(2,1)} %collective-permute-done.10.refs_3_, ...), custom_call_target="tpu_custom_call" | custom-call | flops 4294967296 | bytes 16777216 | tf_op jit(solution)/shard_map/pallas_call | solution.py:221
  (92 shorter events, 1.1 us)
Async XLA Ops:
  6.5 121.1 %copy-start = (f32[8,64,256]{2,1,0:T(8,128)S(1)}, f32[8,64,256]{2,1,0:T(8,128)}, u32[]{:S(2)}) copy-start(f32[8,64,256]{2,1,0:T(8,128)} %param.15) | copy-start | bytes 1572868
  6.5 65.0 %all-gather.5.cloned.1.call-start = ((), (), s32[]{:S(2)}) async-start(), calls=%async_computation.1 | async-start | bytes 9191424 | tf_op jit(solution)/shard_map/all_gather | solution.py:256
  9.4 128.8 %all-gather.3.cloned.1.call-start = ((), (), s32[]{:S(2)}) async-start(), calls=%async_computation | async-start | bytes 8912896 | tf_op jit(solution)/shard_map/all_gather | solution.py:259
  11.2 17.9 %copy-start.8 = (bf16[256,512]{1,0:T(8,128)(2,1)}, bf16[256,512]{1,0:T(8,128)(2,1)S(1)}, u32[]{:S(2)}) copy-start(bf16[256,512]{1,0:T(8,128)(2,1)S(1)} %get-tuple-element.34.refs_5_) | copy-start | bytes 786436
  11.2 17.9 %copy-start.9 = (bf16[256,512]{1,0:T(8,128)(2,1)}, bf16[256,512]{1,0:T(8,128)(2,1)S(1)}, u32[]{:S(2)}) copy-start(bf16[256,512]{1,0:T(8,128)(2,1)S(1)} %get-tuple-element.35.refs_0_) | copy-start | bytes 786436
  11.3 7.4 %collective-permute-start = (bf16[256,512]{1,0:T(8,128)(2,1)S(1)}, bf16[256,512]{1,0:T(8,128)(2,1)S(1)}, u32[]{:S(2)}, u32[]{:S(2)}) collective-permute-start(bf16[256,512]{1,0:T(8,128)(2,1)S(1)} %get-tuple-element.35.refs_0_), channel_id=1, source_target_pairs={{0,1},{1,2},{2,3},{3,0},{4,5},{5,6},{6,7},{7,4},{8,9},{9,10},{10,1... | collective-permute-start | bytes 786440 | tf_op jit(solution)/shard_map/ppermute | solution.py:21
  13.4 7.0 %collective-permute-start.1 = (bf16[256,512]{1,0:T(8,128)(2,1)S(1)}, bf16[256,512]{1,0:T(8,128)(2,1)S(1)}, u32[]{:S(2)}, u32[]{:S(2)}) collective-permute-start(bf16[256,512]{1,0:T(8,128)(2,1)S(1)} %get-tuple-element.35.refs_0_), channel_id=1, source_target_pairs={{0,3},{1,0},{2,1},{3,2},{4,7},{5,4},{6,5},{7,6},{8,11},{9,8},{10,9... | collective-permute-start | bytes 786440 | tf_op jit(solution)/shard_map/ppermute | solution.py:21
  14.7 7.3 %collective-permute-start.4 = (bf16[256,512]{1,0:T(8,128)(2,1)S(1)}, bf16[256,512]{1,0:T(8,128)(2,1)S(1)}, u32[]{:S(2)}, u32[]{:S(2)}) collective-permute-start(bf16[256,512]{1,0:T(8,128)(2,1)S(1)} %get-tuple-element.34.refs_5_), channel_id=1, source_target_pairs={{0,4},{1,5},{2,6},{3,7},{4,8},{5,9},{6,10},{7,11},{8,12},{9,13},{1... | collective-permute-start | bytes 786440 | tf_op jit(solution)/shard_map/ppermute | solution.py:26
  16.1 8.7 %collective-permute-start.5 = (bf16[256,512]{1,0:T(8,128)(2,1)S(1)}, bf16[256,512]{1,0:T(8,128)(2,1)S(1)}, u32[]{:S(2)}, u32[]{:S(2)}) collective-permute-start(bf16[256,512]{1,0:T(8,128)(2,1)S(1)} %get-tuple-element.34.refs_5_), channel_id=1, source_target_pairs={{0,12},{1,13},{2,14},{3,15},{4,0},{5,1},{6,2},{7,3},{8,4},{9,5},{1... | collective-permute-start | bytes 786440 | tf_op jit(solution)/shard_map/ppermute | solution.py:26
  18.7 10.4 %copy-start.10 = (bf16[256,512]{1,0:T(8,128)(2,1)}, bf16[256,512]{1,0:T(8,128)(2,1)S(1)}, u32[]{:S(2)}) copy-start(bf16[256,512]{1,0:T(8,128)(2,1)S(1)} %collective-permute-done.refs_1_) | copy-start | bytes 786436
  18.7 8.4 %collective-permute-start.2 = (bf16[128,512]{1,0:T(8,128)(2,1)S(1)}, bf16[128,512]{1,0:T(8,128)(2,1)S(1)}, u32[]{:S(2)}, u32[]{:S(2)}) collective-permute-start(bf16[128,512]{1,0:T(8,128)(2,1)S(1)} %slice.68), channel_id=1, source_target_pairs={{0,1},{1,2},{2,3},{3,0},{4,5},{5,6},{6,7},{7,4},{8,9},{9,10},{10,1... | collective-permute-start | bytes 393224 | tf_op jit(solution)/shard_map/ppermute | solution.py:21
  20.4 8.8 %copy-start.11 = (bf16[256,512]{1,0:T(8,128)(2,1)}, bf16[256,512]{1,0:T(8,128)(2,1)S(1)}, u32[]{:S(2)}) copy-start(bf16[256,512]{1,0:T(8,128)(2,1)S(1)} %collective-permute-done.1.refs_2_) | copy-start | bytes 786436
  20.4 6.7 %collective-permute-start.3 = (bf16[128,512]{1,0:T(8,128)(2,1)S(1)}, bf16[128,512]{1,0:T(8,128)(2,1)S(1)}, u32[]{:S(2)}, u32[]{:S(2)}) collective-permute-start(bf16[128,512]{1,0:T(8,128)(2,1)S(1)} %slice.69), channel_id=1, source_target_pairs={{0,3},{1,0},{2,1},{3,2},{4,7},{5,4},{6,5},{7,6},{8,11},{9,8},{10,9... | collective-permute-start | bytes 393224 | tf_op jit(solution)/shard_map/ppermute | solution.py:21
  22.0 7.1 %copy-start.12 = (bf16[256,512]{1,0:T(8,128)(2,1)}, bf16[256,512]{1,0:T(8,128)(2,1)S(1)}, u32[]{:S(2)}) copy-start(bf16[256,512]{1,0:T(8,128)(2,1)S(1)} %collective-permute-done.4.refs_6_) | copy-start | bytes 786436
  22.1 6.5 %collective-permute-start.6 = (bf16[128,512]{1,0:T(8,128)(2,1)S(1)}, bf16[128,512]{1,0:T(8,128)(2,1)S(1)}, u32[]{:S(2)}, u32[]{:S(2)}) collective-permute-start(bf16[128,512]{1,0:T(8,128)(2,1)S(1)} %slice.70), channel_id=1, source_target_pairs={{0,4},{1,5},{2,6},{3,7},{4,8},{5,9},{6,10},{7,11},{8,12},{9,13},{1... | collective-permute-start | bytes 393224 | tf_op jit(solution)/shard_map/ppermute | solution.py:26
  24.8 4.3 %copy-start.13 = (bf16[256,512]{1,0:T(8,128)(2,1)}, bf16[256,512]{1,0:T(8,128)(2,1)S(1)}, u32[]{:S(2)}) copy-start(bf16[256,512]{1,0:T(8,128)(2,1)S(1)} %collective-permute-done.5.refs_7_) | copy-start | bytes 786436
  24.8 4.3 %collective-permute-start.7 = (bf16[128,512]{1,0:T(8,128)(2,1)S(1)}, bf16[128,512]{1,0:T(8,128)(2,1)S(1)}, u32[]{:S(2)}, u32[]{:S(2)}) collective-permute-start(bf16[128,512]{1,0:T(8,128)(2,1)S(1)} %slice.71), channel_id=1, source_target_pairs={{0,12},{1,13},{2,14},{3,15},{4,0},{5,1},{6,2},{7,3},{8,4},{9,5},{1... | collective-permute-start | bytes 393224 | tf_op jit(solution)/shard_map/ppermute | solution.py:26
  27.1 19.1 %copy-start.20 = (f32[512,8]{0,1:T(8,128)S(1)}, f32[512,8]{0,1:T(8,128)}, u32[]{:S(2)}) copy-start(f32[512,8]{0,1:T(8,128)} %param.13) | copy-start | bytes 49156
  27.1 19.5 %copy-start.19 = (f32[6,512,8]{1,2,0:T(8,128)S(1)}, f32[6,512,8]{1,2,0:T(8,128)}, u32[]{:S(2)}) copy-start(f32[6,512,8]{1,2,0:T(8,128)} %param.14) | copy-start | bytes 294916
  27.1 2.1 %copy-start.15 = (bf16[128,512]{1,0:T(8,128)(2,1)}, bf16[128,512]{1,0:T(8,128)(2,1)S(1)}, u32[]{:S(2)}) copy-start(bf16[128,512]{1,0:T(8,128)(2,1)S(1)} %collective-permute-done.2.refs_3_) | copy-start | bytes 393220
  27.1 2.1 %copy-start.16 = (bf16[128,512]{1,0:T(8,128)(2,1)}, bf16[128,512]{1,0:T(8,128)(2,1)S(1)}, u32[]{:S(2)}) copy-start(bf16[128,512]{1,0:T(8,128)(2,1)S(1)} %collective-permute-done.3.refs_4_) | copy-start | bytes 393220
  28.6 0.6 copy-start.17
  29.2 0.6 copy-start.18
  32.9 23.1 %collective-permute-start.12 = (bf16[1024,512]{1,0:T(8,128)(2,1)}, bf16[1024,512]{1,0:T(8,128)(2,1)S(1)}, u32[]{:S(2)}, u32[]{:S(2)}) collective-permute-start(bf16[1024,512]{1,0:T(8,128)(2,1)} %get-tuple-element.14.refs_5_), channel_id=1, source_target_pairs={{0,1},{1,2},{2,3},{3,0},{4,5},{5,6},{6,7},{7,4},{8,9},{9,10},{10,1... | collective-permute-start | bytes 3145736 | tf_op jit(solution)/shard_map/ppermute | solution.py:21
  33.0 23.1 %collective-permute-start.13 = (bf16[1024,512]{1,0:T(8,128)(2,1)}, bf16[1024,512]{1,0:T(8,128)(2,1)S(1)}, u32[]{:S(2)}, u32[]{:S(2)}) collective-permute-start(bf16[1024,512]{1,0:T(8,128)(2,1)} %get-tuple-element.14.refs_5_), channel_id=1, source_target_pairs={{0,3},{1,0},{2,1},{3,2},{4,7},{5,4},{6,5},{7,6},{8,11},{9,8},{10,9... | collective-permute-start | bytes 3145736 | tf_op jit(solution)/shard_map/ppermute | solution.py:21
  35.7 23.2 %collective-permute-start.8 = (bf16[1024,512]{1,0:T(8,128)(2,1)}, bf16[1024,512]{1,0:T(8,128)(2,1)}, u32[]{:S(2)}, u32[]{:S(2)}) collective-permute-start(bf16[1024,512]{1,0:T(8,128)(2,1)} %get-tuple-element.13.refs_0_), channel_id=1, source_target_pairs={{0,4},{1,5},{2,6},{3,7},{4,8},{5,9},{6,10},{7,11},{8,12},{9,13},{1... | collective-permute-start | bytes 3145736 | tf_op jit(solution)/shard_map/ppermute | solution.py:26
  36.9 24.6 %collective-permute-start.9 = (bf16[1024,512]{1,0:T(8,128)(2,1)}, bf16[1024,512]{1,0:T(8,128)(2,1)}, u32[]{:S(2)}, u32[]{:S(2)}) collective-permute-start(bf16[1024,512]{1,0:T(8,128)(2,1)} %get-tuple-element.13.refs_0_), channel_id=1, source_target_pairs={{0,12},{1,13},{2,14},{3,15},{4,0},{5,1},{6,2},{7,3},{8,4},{9,5},{1... | collective-permute-start | bytes 3145736 | tf_op jit(solution)/shard_map/ppermute | solution.py:26
  46.2 20.7 %copy-start.5 = (bf16[512,1,1,256]{3,2,1,0:T(2,128)(2,1)}, bf16[512,1,1,256]{3,2,1,0:T(2,128)(2,1)S(1)}, u32[]{:S(2)}) copy-start(bf16[512,1,1,256]{3,2,1,0:T(2,128)(2,1)S(1)} %constant_dynamic-slice_fusion.4) | copy-start | bytes 786436
  56.0 15.5 %copy-start.2 = (bf16[1024,512]{1,0:T(8,128)(2,1)}, bf16[1024,512]{1,0:T(8,128)(2,1)S(1)}, u32[]{:S(2)}) copy-start(bf16[1024,512]{1,0:T(8,128)(2,1)S(1)} %collective-permute-done.12.refs_6_) | copy-start | bytes 3145732
  56.0 10.9 %collective-permute-start.14 = (bf16[512,512]{1,0:T(8,128)(2,1)S(1)}, bf16[512,512]{1,0:T(8,128)(2,1)S(1)}, u32[]{:S(2)}, u32[]{:S(2)}) collective-permute-start(bf16[512,512]{1,0:T(8,128)(2,1)S(1)} %slice.74), channel_id=1, source_target_pairs={{0,1},{1,2},{2,3},{3,0},{4,5},{5,6},{6,7},{7,4},{8,9},{9,10},{10,1... | collective-permute-start | bytes 1572872 | tf_op jit(solution)/shard_map/ppermute | solution.py:21
  56.1 15.4 %copy-start.3 = (bf16[1024,512]{1,0:T(8,128)(2,1)}, bf16[1024,512]{1,0:T(8,128)(2,1)S(1)}, u32[]{:S(2)}) copy-start(bf16[1024,512]{1,0:T(8,128)(2,1)S(1)} %collective-permute-done.13.refs_7_) | copy-start | bytes 3145732
  56.2 10.7 %collective-permute-start.15 = (bf16[512,512]{1,0:T(8,128)(2,1)S(1)}, bf16[512,512]{1,0:T(8,128)(2,1)}, u32[]{:S(2)}, u32[]{:S(2)}) collective-permute-start(bf16[512,512]{1,0:T(8,128)(2,1)S(1)} %slice.75), channel_id=1, source_target_pairs={{0,3},{1,0},{2,1},{3,2},{4,7},{5,4},{6,5},{7,6},{8,11},{9,8},{10,9... | collective-permute-start | bytes 1572872 | tf_op jit(solution)/shard_map/ppermute | solution.py:21
  60.0 10.5 %collective-permute-start.10 = (bf16[512,512]{1,0:T(8,128)(2,1)S(1)}, bf16[512,512]{1,0:T(8,128)(2,1)}, u32[]{:S(2)}, u32[]{:S(2)}) collective-permute-start(bf16[512,512]{1,0:T(8,128)(2,1)S(1)} %slice.72), channel_id=1, source_target_pairs={{0,4},{1,5},{2,6},{3,7},{4,8},{5,9},{6,10},{7,11},{8,12},{9,13},{1... | collective-permute-start | bytes 1572872 | tf_op jit(solution)/shard_map/ppermute | solution.py:26
  62.6 8.9 %collective-permute-start.11 = (bf16[512,512]{1,0:T(8,128)(2,1)S(1)}, bf16[512,512]{1,0:T(8,128)(2,1)}, u32[]{:S(2)}, u32[]{:S(2)}) collective-permute-start(bf16[512,512]{1,0:T(8,128)(2,1)S(1)} %slice.73), channel_id=1, source_target_pairs={{0,12},{1,13},{2,14},{3,15},{4,0},{5,1},{6,2},{7,3},{8,4},{9,5},{1... | collective-permute-start | bytes 1572872 | tf_op jit(solution)/shard_map/ppermute | solution.py:26
  66.9 4.6 %copy-start.4 = (bf16[512,512]{1,0:T(8,128)(2,1)}, bf16[512,512]{1,0:T(8,128)(2,1)S(1)}, u32[]{:S(2)}) copy-start(bf16[512,512]{1,0:T(8,128)(2,1)S(1)} %collective-permute-done.14.refs_8_) | copy-start | bytes 1572868
  71.5 10.6 %copy-start.14 = (f32[512,256]{1,0:T(8,128)S(1)}, f32[512,256]{1,0:T(8,128)}, u32[]{:S(2)}) copy-start(f32[512,256]{1,0:T(8,128)} %fusion.29) | copy-start | bytes 1572868
  79.6 48.1 %copy-start.6 = (bf16[512,1,1,256]{3,2,1,0:T(2,128)(2,1)S(1)}, bf16[512,1,1,256]{3,2,1,0:T(2,128)(2,1)}, u32[]{:S(2)}) copy-start(bf16[512,1,1,256]{3,2,1,0:T(2,128)(2,1)} %copy-done.5) | copy-start | bytes 786436
  82.9 6.8 %collective-permute-start.16 = (bf16[8,64,256]{2,1,0:T(8,128)(2,1)S(1)}, bf16[8,64,256]{2,1,0:T(8,128)(2,1)S(1)}, u32[]{:S(2)}, u32[]{:S(2)}) collective-permute-start(bf16[8,64,256]{2,1,0:T(8,128)(2,1)S(1)} %get-tuple-element.46), channel_id=1, source_target_pairs={{0,16},{16,0},{32,48},{48,32},{64,80},{80,64},{96,112},{112,96},{1... | collective-permute-start | bytes 786440 | tf_op jit(solution)/shard_map/ppermute | solution.py:30
  89.9 10.4 %collective-permute-start.17 = (bf16[4,64,256]{2,1,0:T(8,128)(2,1)S(1)}, bf16[4,64,256]{2,1,0:T(8,128)(2,1)S(1)}, u32[]{:S(2)}, u32[]{:S(2)}) collective-permute-start(bf16[4,64,256]{2,1,0:T(8,128)(2,1)S(1)} %fusion.27), channel_id=1, source_target_pairs={{0,32},{16,48},{32,0},{48,16},{64,96},{80,112},{96,64},{112,80},{1... | collective-permute-start | bytes 393224 | tf_op jit(solution)/shard_map/ppermute | solution.py:30
  91.5 11.5 %collective-permute-start.18 = (bf16[4,64,256]{2,1,0:T(8,128)(2,1)S(1)}, bf16[4,64,256]{2,1,0:T(8,128)(2,1)S(1)}, u32[]{:S(2)}, u32[]{:S(2)}) collective-permute-start(bf16[4,64,256]{2,1,0:T(8,128)(2,1)S(1)} %fusion.27), channel_id=1, source_target_pairs={{0,64},{16,80},{32,96},{48,112},{64,0},{80,16},{96,32},{112,48},{1... | collective-permute-start | bytes 393224 | tf_op jit(solution)/shard_map/ppermute | solution.py:30
  94.6 17.7 %collective-permute-start.19 = (bf16[4,64,256]{2,1,0:T(8,128)(2,1)S(1)}, bf16[4,64,256]{2,1,0:T(8,128)(2,1)S(1)}, u32[]{:S(2)}, u32[]{:S(2)}) collective-permute-start(bf16[4,64,256]{2,1,0:T(8,128)(2,1)S(1)} %fusion.27), channel_id=1, source_target_pairs={{0,96},{16,112},{32,64},{48,80},{64,32},{80,48},{96,0},{112,16},{1... | collective-permute-start | bytes 393224 | tf_op jit(solution)/shard_map/ppermute | solution.py:30
  112.5 10.9 %collective-permute-start.20 = (bf16[4,64,256]{2,1,0:T(8,128)(2,1)S(1)}, bf16[4,64,256]{2,1,0:T(8,128)(2,1)S(1)}, u32[]{:S(2)}, u32[]{:S(2)}) collective-permute-start(bf16[4,64,256]{2,1,0:T(8,128)(2,1)S(1)} %get-tuple-element.37), channel_id=1, source_target_pairs={{0,224},{16,240},{32,192},{48,208},{64,160},{80,176},{96,128},{112... | collective-permute-start | bytes 393224 | tf_op jit(solution)/shard_map/ppermute | solution.py:324
  123.5 5.5 %collective-permute-start.21 = (bf16[3,4,64,256]{3,2,1,0:T(8,128)(2,1)S(1)}, bf16[3,4,64,256]{3,2,1,0:T(8,128)(2,1)S(1)}, u32[]{:S(2)}, u32[]{:S(2)}) collective-permute-start(bf16[3,4,64,256]{3,2,1,0:T(8,128)(2,1)S(1)} %pad_maximum_fusion.1), channel_id=1, source_target_pairs={{0,16},{16,0},{32,48},{48,32},{64,80},{80,64},{96,112},{112,96},{1... | collective-permute-start | bytes 1179656 | tf_op jit(solution)/shard_map/ppermute | solution.py:30
  128.3 1.5 copy-start.7
  128.3 1.5 copy-start.21
  129.8 8.4 %copy-start.1 = (f32[512]{0:T(512)S(1)}, f32[512]{0:T(512)}, u32[]{:S(2)}) copy-start(f32[512]{0:T(512)} %param.17) | copy-start | bytes 6148
Sparse Core Ops, SparseCore 0:
  9.5 61.3 all-gather.4
  72.8 65.3 all-gather.2

commit v3 on v2

--- a/solution.py
+++ b/solution.py
@@ -304,27 +304,26 @@
     share = heads // 2
     plane_share = lax.dynamic_slice_in_dim(plane_end, core * share, share, 0)
     plane_sent = plane_share.astype(jnp.bfloat16)
-    near = [swap_ctx(plane_sent, 2 * m).astype(jnp.float32) for m in (1, 2, 3)]
+    near_sent = swap_ctx(plane_sent, 2)
     plane_totals = totals.reshape(CTX // 2, 2, heads).sum(axis=1)
     share_totals = lax.dynamic_slice_in_dim(plane_totals, core * share, share, 1)
-    all_planes = jnp.arange(CTX // 2, dtype=jnp.int32)
-    near_all = [plane_share, *near]
-
-    def faded_sum(among):
-        result = 0.0
-        for m in among:
-            here = (plane ^ among[0]) // len(among)
-            after = (all_planes // len(among) == here) & (all_planes > (plane ^ m))
-            later = jnp.sum(jnp.where(after[:, None], share_totals, 0.0), axis=0)
-            result = result + fade(later)[:, None, None] * near_all[m]
-        return result
-
-    pair_sum = faded_sum((2, 3)).astype(jnp.bfloat16)
-    quad_sum = faded_sum((0, 1, 2, 3)).astype(jnp.bfloat16)
+
+    def joined(own, other, bit, at):
+        group_totals = share_totals.reshape(-1, bit, share).sum(axis=1)
+        later = lax.dynamic_index_in_dim(group_totals, at | 1, 0, keepdims=False)
+        faded = fade(later)[:, None, None]
+        own_is_later = (at & 1) == 1
+        return jnp.where(own_is_later, own, other) + faded * jnp.where(own_is_later, other, own)
+
+    pair = joined(plane_share, near_sent.astype(jnp.float32), 1, plane)
+    pair_other = swap_ctx(pair.astype(jnp.bfloat16), 4)
+    quad = joined(pair, pair_other.astype(jnp.float32), 2, plane // 2)
     quad_other = lax.ppermute(
-        quad_sum, "ctx", [(2 * z + c, 2 * (7 - z) + c) for z in range(4) for c in range(2)]
-    )
-    shared = jnp.stack([near[0].astype(jnp.bfloat16), pair_sum, quad_other])
+        quad.astype(jnp.bfloat16),
+        "ctx",
+        [(2 * z + c, 2 * (7 - z) + c) for z in range(4) for c in range(2)],
+    )
+    shared = jnp.stack([near_sent, pair_other, quad_other])
     shared_other = swap_ctx(shared, 1)
     lower = jnp.where(core == 0, shared, shared_other)
     upper = jnp.where(core == 0, shared_other, shared)

time: 156 us -> 152 us (0.974)
  waiting for transfers between devices: 45.8 us -> 41.4 us
  other arithmetic: 9.6 us -> 6.28 us
  starting transfers between devices: 44.7 us -> 47.9 us
    ppermute x1, starting transfers between devices: 5 us -> 9.84 us  [on_device(): lax.ppermute(quad.astype(jnp.bfloat16), 'ctx', [(2 * z + c, 2 * (7 - z) +...]
    ppermute x5 -> x4, waiting for transfers between devices: 18.4 us -> 14.5 us  [swap_ctx(): return lax.ppermute(a, 'ctx', [(i, i ^ mask) for i in range(CTX)])]
    all_gather x1, waiting for transfers between devices: 4.78 us -> 1.31 us  [on_device(): gate_weights = lax.all_gather(w_gate, 'ctx', axis=0, tiled=True)]
    ppermute x5 -> x4, starting transfers between devices: 14.5 us -> 12.6 us  [swap_ctx(): return lax.ppermute(a, 'ctx', [(i, i ^ mask) for i in range(CTX)])]
  transfers between devices with their start and end apart: 24 -> 23, of which waited for: 12 -> 13; matrix products, arithmetic and copies ran while one was open for 17% -> 15% of each run, Pallas kernels for 7% -> 7%
where the time goes in v3:
time: 152 us
  starting transfers between devices  47.9 us (32%)
  waiting for transfers between devices  41.4 us (27%)
  Pallas kernels  21.8 us (14%)
  between operations  13.9 us (9%)
  local copies, waits for them, and re-layouts  13 us (9%)
  matrix products  7.15 us (5%)
  other arithmetic  6.28 us (4%)
    ppermute x4, waiting for transfers between devices, swap_ctx(): return lax.ppermute(a, 'ctx', [(i, i ^ mask) for i in range(CTX)])  14.5 us
    ppermute x8, starting transfers between devices, along_y(): return lax.ppermute(a, 'tp', pairs)  12.8 us
    ppermute x8, starting transfers between devices, along_x(): return lax.ppermute(a, 'tp', pairs)  12.6 us
    ppermute x4, starting transfers between devices, swap_ctx(): return lax.ppermute(a, 'ctx', [(i, i ^ mask) for i in range(CTX)])  12.6 us
    pallas_call x1, Pallas kernels, finish(): pl.pallas_call(gates_kernel, out_shape=jax.ShapeDtypeStruct((tok, cols),...  10.7 us
    ppermute x8, waiting for transfers between devices, along_x(): return lax.ppermute(a, 'tp', pairs)  10.5 us
    ppermute x1, starting transfers between devices, on_device(): lax.ppermute(quad.astype(jnp.bfloat16), 'ctx', [(2 * z + c, 2 * (7 - z) +...  9.84 us
    pallas_call x1, Pallas kernels, project_values(): pl.pallas_call(values_kernel, out_shape=jax.ShapeDtypeStruct((tok, cols),...  8.09 us
  transfers between devices with their start and end apart: 23, of which 13 were waited for; matrix products, arithmetic and copies ran while one was open for 15% of the time, Pallas kernels for 7%

profile of v3, /device:TPU:1, one launch (start us, length us, event | category | flops | bytes accessed | tf_op | source)
XLA Modules:
  0.0 151.5 jit_solution(3966571800906773357)
XLA Ops:
  6.5 0.9 reduce_sum.96
  7.5 1.9 %pad_maximum_fusion = bf16[528,512]{1,0:T(8,128)(2,1)} fusion(bf16[16,512]{1,0:T(8,128)(2,1)S(1)} %fusion.37, bf16[512,512]{1,0:T(8,128)(2,1)} %param.10), kind=kLoop, calls=%fused_computation.21 | loop fusion | flops 1081344 | bytes 1081344 | tf_op jit(solution)/shard_map/concatenate | solution.py:257
  9.5 0.7 all-gather.3.cloned.1.call-update
  10.2 1.1 fusion.60
  11.2 2.1 %collective-permute-start = (bf16[256,512]{1,0:T(8,128)(2,1)S(1)}, bf16[256,512]{1,0:T(8,128)(2,1)S(1)}, u32[]{:S(2)}, u32[]{:S(2)}) collective-permute-start(bf16[256,512]{1,0:T(8,128)(2,1)S(1)} %get-tuple-element.29.refs_0_), channel_id=1, source_target_pairs={{0,1},{1,2},{2,3},{3,0},{4,5},{5,6},{6,7},{7,4},{8,9},{9,10},{10,1... | collective-permute-start | bytes 786440 | tf_op jit(solution)/shard_map/ppermute | solution.py:21
  13.4 1.4 collective-permute-start.1
  14.7 1.4 collective-permute-start.4
  16.1 1.4 collective-permute-start.5
  17.6 0.8 collective-permute-done.refs_1_
  18.4 1.9 %collective-permute-start.2 = (bf16[128,512]{1,0:T(8,128)(2,1)S(1)}, bf16[128,512]{1,0:T(8,128)(2,1)S(1)}, u32[]{:S(2)}, u32[]{:S(2)}) collective-permute-start(bf16[128,512]{1,0:T(8,128)(2,1)S(1)} %slice.68), channel_id=1, source_target_pairs={{0,1},{1,2},{2,3},{3,0},{4,5},{5,6},{6,7},{7,4},{8,9},{9,10},{10,1... | collective-permute-start | bytes 393224 | tf_op jit(solution)/shard_map/ppermute | solution.py:21
  20.4 1.7 %collective-permute-start.3 = (bf16[128,512]{1,0:T(8,128)(2,1)S(1)}, bf16[128,512]{1,0:T(8,128)(2,1)S(1)}, u32[]{:S(2)}, u32[]{:S(2)}) collective-permute-start(bf16[128,512]{1,0:T(8,128)(2,1)S(1)} %slice.69), channel_id=1, source_target_pairs={{0,3},{1,0},{2,1},{3,2},{4,7},{5,4},{6,5},{7,6},{8,11},{9,8},{10,9... | collective-permute-start | bytes 393224 | tf_op jit(solution)/shard_map/ppermute | solution.py:21
  22.0 2.7 %collective-permute-start.6 = (bf16[128,512]{1,0:T(8,128)(2,1)S(1)}, bf16[128,512]{1,0:T(8,128)(2,1)S(1)}, u32[]{:S(2)}, u32[]{:S(2)}) collective-permute-start(bf16[128,512]{1,0:T(8,128)(2,1)S(1)} %slice.70), channel_id=1, source_target_pairs={{0,4},{1,5},{2,6},{3,7},{4,8},{5,9},{6,10},{7,11},{8,12},{9,13},{1... | collective-permute-start | bytes 393224 | tf_op jit(solution)/shard_map/ppermute | solution.py:26
  24.8 1.5 %collective-permute-start.7 = (bf16[128,512]{1,0:T(8,128)(2,1)S(1)}, bf16[128,512]{1,0:T(8,128)(2,1)S(1)}, u32[]{:S(2)}, u32[]{:S(2)}) collective-permute-start(bf16[128,512]{1,0:T(8,128)(2,1)S(1)} %slice.71), channel_id=1, source_target_pairs={{0,12},{1,13},{2,14},{3,15},{4,0},{5,1},{6,2},{7,3},{8,4},{9,5},{1... | collective-permute-start | bytes 393224 | tf_op jit(solution)/shard_map/ppermute | solution.py:26
  26.5 2.1 %collective-permute-done.6.refs_8_ = bf16[128,512]{1,0:T(8,128)(2,1)S(1)} collective-permute-done((bf16[128,512]{1,0:T(8,128)(2,1)S(1)}, bf16[128,512]{1,0:T(8,128)(2,1)S(1)}, u32[]{:S(2)}, u32[]{:S(2)}) %collective-permute-start.6) | collective-permute-done | bytes 131104 | tf_op jit(solution)/shard_map/ppermute | solution.py:26
  28.6 0.5 collective-permute-done.7.refs_9_
  29.2 0.7 copy-done.18
  29.9 3.0 %shard_map.91 = (bf16[1024,512]{1,0:T(8,128)(2,1)}, bf16[1024,512]{1,0:T(8,128)(2,1)}) custom-call(bf16[256,512]{1,0:T(8,128)(2,1)} %copy-done.9, bf16[256,512]{1,0:T(8,128)(2,1)} %copy-done.10, bf16[256,512]{1,0:T(8,128)(2,1)} %copy-done.11, bf16[128,512]{1,0:T(8,128)(2,1)} %copy-done.15, bf16[128,512]{1,0:T(8,128)(2,1)} %copy-done.16, ...), custom_call_target="tpu_custom_call" | custom-call | tf_op jit(solution)/shard_map/pallas_call | solution.py:68
  32.9 0.1 collective-permute-start.12
  33.0 2.7 %collective-permute-start.13 = (bf16[1024,512]{1,0:T(8,128)(2,1)}, bf16[1024,512]{1,0:T(8,128)(2,1)S(1)}, u32[]{:S(2)}, u32[]{:S(2)}) collective-permute-start(bf16[1024,512]{1,0:T(8,128)(2,1)} %get-tuple-element.14.refs_5_), channel_id=1, source_target_pairs={{0,3},{1,0},{2,1},{3,2},{4,7},{5,4},{6,5},{7,6},{8,11},{9,8},{10,9... | collective-permute-start | bytes 3145736 | tf_op jit(solution)/shard_map/ppermute | solution.py:21
  35.7 1.2 collective-permute-start.8
  36.9 1.4 collective-permute-start.9
  38.4 3.7 %fusion.59 = (bf16[512,1,4,256]{3,2,1,0:T(4,128)(2,1)}, bf16[512,1,4,256]{3,2,1,0:T(4,128)(2,1)}) fusion(bf16[512,2,4,256]{3,2,1,0:T(4,128)(2,1)} %param.12), kind=kLoop, calls=%fused_computation.112 | loop fusion | bytes 4194304 | tf_op jit(solution)/shard_map/slice | solution.py:276
  42.1 1.8 %constant_dynamic-slice_fusion.4 = bf16[512,1,1,256]{3,2,1,0:T(2,128)(2,1)S(1)} fusion(bf16[512,1,4,256]{3,2,1,0:T(4,128)(2,1)} %get-tuple-element.25, s32[]{:T(128)S(6)} %select_n.197), kind=kLoop, calls=%fused_computation.72 | loop fusion | bytes 524292 | tf_op jit(solution)/shard_map/jit(dynamic_index_in_dim)/dynamic_slice | solution.py:275
  43.8 1.8 %constant_dynamic-slice_fusion.5 = bf16[512,1,1,256]{3,2,1,0:T(2,128)(2,1)S(1)} fusion(bf16[512,1,4,256]{3,2,1,0:T(4,128)(2,1)} %get-tuple-element.24, s32[]{:T(128)S(6)} %select_n.197), kind=kLoop, calls=%fused_computation.73 | loop fusion | bytes 524292 | tf_op jit(solution)/shard_map/jit(dynamic_index_in_dim)/dynamic_slice | solution.py:276
  45.6 0.4 fusion.16
  46.1 0.7 slice_bitcast_fusion
  46.7 9.3 %collective-permute-done.12.refs_6_ = bf16[1024,512]{1,0:T(8,128)(2,1)S(1)} collective-permute-done((bf16[1024,512]{1,0:T(8,128)(2,1)}, bf16[1024,512]{1,0:T(8,128)(2,1)S(1)}, u32[]{:S(2)}, u32[]{:S(2)}) %collective-permute-start.12) | collective-permute-done | bytes 1048608 | tf_op jit(solution)/shard_map/ppermute | solution.py:21
  56.0 0.1 collective-permute-start.14
  56.2 2.7 %collective-permute-start.15 = (bf16[512,512]{1,0:T(8,128)(2,1)S(1)}, bf16[512,512]{1,0:T(8,128)(2,1)}, u32[]{:S(2)}, u32[]{:S(2)}) collective-permute-start(bf16[512,512]{1,0:T(8,128)(2,1)S(1)} %slice.75), channel_id=1, source_target_pairs={{0,3},{1,0},{2,1},{3,2},{4,7},{5,4},{6,5},{7,6},{8,11},{9,8},{10,9... | collective-permute-start | bytes 1572872 | tf_op jit(solution)/shard_map/ppermute | solution.py:21
  58.9 1.1 slice.72
  60.0 1.5 collective-permute-start.10
  61.5 1.1 slice.73
  62.6 1.5 %collective-permute-start.11 = (bf16[512,512]{1,0:T(8,128)(2,1)S(1)}, bf16[512,512]{1,0:T(8,128)(2,1)}, u32[]{:S(2)}, u32[]{:S(2)}) collective-permute-start(bf16[512,512]{1,0:T(8,128)(2,1)S(1)} %slice.73), channel_id=1, source_target_pairs={{0,12},{1,13},{2,14},{3,15},{4,0},{5,1},{6,2},{7,3},{8,4},{9,5},{1... | collective-permute-start | bytes 1572872 | tf_op jit(solution)/shard_map/ppermute | solution.py:26
  64.1 0.2 slice_reduce_fusion
  64.3 0.8 fusion.28
  65.1 1.3 fusion.25
  66.4 0.4 collective-permute-done.14.refs_8_
  66.9 3.6 %collective-permute-done.10.refs_3_ = bf16[512,512]{1,0:T(8,128)(2,1)} collective-permute-done((bf16[512,512]{1,0:T(8,128)(2,1)S(1)}, bf16[512,512]{1,0:T(8,128)(2,1)}, u32[]{:S(2)}, u32[]{:S(2)}) %collective-permute-start.10) | collective-permute-done | bytes 524320 | tf_op jit(solution)/shard_map/ppermute | solution.py:26
  70.5 1.0 collective-permute-done.11.refs_4_
  71.5 8.1 %shard_map.92 = bf16[512,512]{1,0:T(8,128)(2,1)S(1)} custom-call(bf16[1024,512]{1,0:T(8,128)(2,1)} %get-tuple-element.13.refs_0_, bf16[1024,512]{1,0:T(8,128)(2,1)} %collective-permute-done.8.refs_1_, bf16[1024,512]{1,0:T(8,128)(2,1)} %collective-permute-done.9.refs_2_, bf16[512,512]{1,0:T(8,128)(2,1)} %collective-permute-done.10.refs_3_, ...), custom_call_target="tpu_custom_call" | custom-call | flops 4294967296 | bytes 16777216 | tf_op jit(solution)/shard_map/pallas_call | solution.py:179
  79.6 0.2 copy.14
  79.8 0.8 convert_reduce_fusion
  80.6 0.1 select_reduce_fusion.4
  80.7 0.8 bitcast_multiply_fusion.1
  81.6 0.8 fusion.61
  82.4 5.7 %collective-permute-start.16 = (bf16[8,64,256]{2,1,0:T(8,128)(2,1)S(1)}, bf16[8,64,256]{2,1,0:T(8,128)(2,1)S(1)}, u32[]{:S(2)}, u32[]{:S(2)}) collective-permute-start(bf16[8,64,256]{2,1,0:T(8,128)(2,1)S(1)} %get-tuple-element.38), channel_id=1, source_target_pairs={{0,16},{16,0},{32,48},{48,32},{64,80},{80,64},{96,112},{112,96},{1... | collective-permute-start | bytes 786440 | tf_op jit(solution)/shard_map/ppermute | solution.py:30
  88.2 1.0 collective-permute-done.16
  89.2 0.1 fusion.58
  89.3 1.5 collective-permute-start.17
  90.9 6.6 %collective-permute-done.17 = bf16[4,64,256]{2,1,0:T(8,128)(2,1)S(1)} collective-permute-done((bf16[4,64,256]{2,1,0:T(8,128)(2,1)S(1)}, bf16[4,64,256]{2,1,0:T(8,128)(2,1)S(1)}, u32[]{:S(2)}, u32[]{:S(2)}) %collective-permute-start.17) | collective-permute-done | bytes 131104 | tf_op jit(solution)/shard_map/ppermute | solution.py:30
  97.5 0.2 fusion.27
  97.7 3.0 %collective-permute-start.18 = (bf16[4,64,256]{2,1,0:T(8,128)(2,1)S(1)}, bf16[4,64,256]{2,1,0:T(8,128)(2,1)S(1)}, u32[]{:S(2)}, u32[]{:S(2)}) collective-permute-start(bf16[4,64,256]{2,1,0:T(8,128)(2,1)S(1)} %fusion.27), channel_id=1, source_target_pairs={{0,64},{16,80},{32,96},{48,112},{64,0},{80,16},{96,32},{112,48},{1... | collective-permute-start | bytes 393224 | tf_op jit(solution)/shard_map/ppermute | solution.py:30
  100.8 6.3 %collective-permute-done.18 = bf16[4,64,256]{2,1,0:T(8,128)(2,1)S(1)} collective-permute-done((bf16[4,64,256]{2,1,0:T(8,128)(2,1)S(1)}, bf16[4,64,256]{2,1,0:T(8,128)(2,1)S(1)}, u32[]{:S(2)}, u32[]{:S(2)}) %collective-permute-start.18) | collective-permute-done | bytes 131104 | tf_op jit(solution)/shard_map/ppermute | solution.py:30
  107.1 0.2 fusion.20
  107.3 9.8 %collective-permute-start.19 = (bf16[4,64,256]{2,1,0:T(8,128)(2,1)S(1)}, bf16[4,64,256]{2,1,0:T(8,128)(2,1)S(1)}, u32[]{:S(2)}, u32[]{:S(2)}) collective-permute-start(bf16[4,64,256]{2,1,0:T(8,128)(2,1)S(1)} %fusion.20), channel_id=1, source_target_pairs={{0,224},{16,240},{32,192},{48,208},{64,160},{80,176},{96,128},{112... | collective-permute-start | bytes 393224 | tf_op jit(solution)/shard_map/ppermute | solution.py:321
  117.2 7.1 %collective-permute-done.19 = bf16[4,64,256]{2,1,0:T(8,128)(2,1)S(1)} collective-permute-done((bf16[4,64,256]{2,1,0:T(8,128)(2,1)S(1)}, bf16[4,64,256]{2,1,0:T(8,128)(2,1)S(1)}, u32[]{:S(2)}, u32[]{:S(2)}) %collective-permute-start.19) | collective-permute-done | bytes 131104 | tf_op jit(solution)/shard_map/ppermute | solution.py:321
  124.3 2.5 %collective-permute-start.20 = (bf16[3,4,64,256]{3,2,1,0:T(8,128)(2,1)S(1)}, bf16[3,4,64,256]{3,2,1,0:T(8,128)(2,1)S(1)}, u32[]{:S(2)}, u32[]{:S(2)}) collective-permute-start(bf16[3,4,64,256]{3,2,1,0:T(8,128)(2,1)S(1)} %pad_maximum_fusion.1), channel_id=1, source_target_pairs={{0,16},{16,0},{32,48},{48,32},{64,80},{80,64},{96,112},{112,96},{1... | collective-permute-start | bytes 1179656 | tf_op jit(solution)/shard_map/ppermute | solution.py:30
  126.9 0.6 convolution_multiply_fusion
  127.5 0.6 collective-permute-done.20
  128.2 0.8 fusion
  129.0 3.3 %fusion.10 = f32[512,8,64]{0,2,1:T(8,128)S(1)} fusion(f32[512,8,64]{0,2,1:T(8,128)S(1)} %fusion, f32[512,8,64]{0,2,1:T(8,128)S(1)} %convolution_multiply_fusion, bf16[512,8,64]{0,2,1:T(8,128)(2,1)S(1)} %bitcast.83, f32[512,512]{1,0:T(8,128)S(1)} %copy-done.7, f32[8,512]{1,0:T(8,128)S(1)} %bitcast.87, pred[512,512]{1,0:T(8,128)(4,1)S(1)} %iota_compare_fusion, ...), kind=kOutput, calls=%fused_computation.14 | convolution fusion | flops 282591232 | bytes 5013536 | tf_op jit(solution)/shard_map/hts,shp->thp/dot_general | solution.py:350
  132.3 0.3 copy.17.refs_11_
  132.6 1.3 all-gather.3.cloned.1.call-done.refs_10_
  134.0 10.7 %shard_map.93 = bf16[512,512]{1,0:T(8,128)(2,1)} custom-call(bf16[1024,512]{1,0:T(8,128)(2,1)} %get-tuple-element.13.refs_0_, bf16[1024,512]{1,0:T(8,128)(2,1)} %collective-permute-done.8.refs_1_, bf16[1024,512]{1,0:T(8,128)(2,1)} %collective-permute-done.9.refs_2_, bf16[512,512]{1,0:T(8,128)(2,1)} %collective-permute-done.10.refs_3_, ...), custom_call_target="tpu_custom_call" | custom-call | flops 4294967296 | bytes 16777216 | tf_op jit(solution)/shard_map/pallas_call | solution.py:221
  (91 shorter events, 1.1 us)
Async XLA Ops:
  6.5 120.3 %copy-start = (f32[8,64,256]{2,1,0:T(8,128)S(1)}, f32[8,64,256]{2,1,0:T(8,128)}, u32[]{:S(2)}) copy-start(f32[8,64,256]{2,1,0:T(8,128)} %param.15) | copy-start | bytes 1572868
  6.5 65.0 %all-gather.5.cloned.1.call-start = ((), (), s32[]{:S(2)}) async-start(), calls=%async_computation.1 | async-start | bytes 9191424 | tf_op jit(solution)/shard_map/all_gather | solution.py:256
  9.4 124.6 %all-gather.3.cloned.1.call-start = ((), (), s32[]{:S(2)}) async-start(), calls=%async_computation | async-start | bytes 8912896 | tf_op jit(solution)/shard_map/all_gather | solution.py:259
  11.2 17.9 %copy-start.8 = (bf16[256,512]{1,0:T(8,128)(2,1)}, bf16[256,512]{1,0:T(8,128)(2,1)S(1)}, u32[]{:S(2)}) copy-start(bf16[256,512]{1,0:T(8,128)(2,1)S(1)} %get-tuple-element.28.refs_5_) | copy-start | bytes 786436
  11.2 17.9 %copy-start.9 = (bf16[256,512]{1,0:T(8,128)(2,1)}, bf16[256,512]{1,0:T(8,128)(2,1)S(1)}, u32[]{:S(2)}) copy-start(bf16[256,512]{1,0:T(8,128)(2,1)S(1)} %get-tuple-element.29.refs_0_) | copy-start | bytes 786436
  11.2 7.1 %collective-permute-start = (bf16[256,512]{1,0:T(8,128)(2,1)S(1)}, bf16[256,512]{1,0:T(8,128)(2,1)S(1)}, u32[]{:S(2)}, u32[]{:S(2)}) collective-permute-start(bf16[256,512]{1,0:T(8,128)(2,1)S(1)} %get-tuple-element.29.refs_0_), channel_id=1, source_target_pairs={{0,1},{1,2},{2,3},{3,0},{4,5},{5,6},{6,7},{7,4},{8,9},{9,10},{10,1... | collective-permute-start | bytes 786440 | tf_op jit(solution)/shard_map/ppermute | solution.py:21
  13.4 7.0 %collective-permute-start.1 = (bf16[256,512]{1,0:T(8,128)(2,1)S(1)}, bf16[256,512]{1,0:T(8,128)(2,1)S(1)}, u32[]{:S(2)}, u32[]{:S(2)}) collective-permute-start(bf16[256,512]{1,0:T(8,128)(2,1)S(1)} %get-tuple-element.29.refs_0_), channel_id=1, source_target_pairs={{0,3},{1,0},{2,1},{3,2},{4,7},{5,4},{6,5},{7,6},{8,11},{9,8},{10,9... | collective-permute-start | bytes 786440 | tf_op jit(solution)/shard_map/ppermute | solution.py:21
  14.7 7.3 %collective-permute-start.4 = (bf16[256,512]{1,0:T(8,128)(2,1)S(1)}, bf16[256,512]{1,0:T(8,128)(2,1)S(1)}, u32[]{:S(2)}, u32[]{:S(2)}) collective-permute-start(bf16[256,512]{1,0:T(8,128)(2,1)S(1)} %get-tuple-element.28.refs_5_), channel_id=1, source_target_pairs={{0,4},{1,5},{2,6},{3,7},{4,8},{5,9},{6,10},{7,11},{8,12},{9,13},{1... | collective-permute-start | bytes 786440 | tf_op jit(solution)/shard_map/ppermute | solution.py:26
  16.1 8.7 %collective-permute-start.5 = (bf16[256,512]{1,0:T(8,128)(2,1)S(1)}, bf16[256,512]{1,0:T(8,128)(2,1)S(1)}, u32[]{:S(2)}, u32[]{:S(2)}) collective-permute-start(bf16[256,512]{1,0:T(8,128)(2,1)S(1)} %get-tuple-element.28.refs_5_), channel_id=1, source_target_pairs={{0,12},{1,13},{2,14},{3,15},{4,0},{5,1},{6,2},{7,3},{8,4},{9,5},{1... | collective-permute-start | bytes 786440 | tf_op jit(solution)/shard_map/ppermute | solution.py:26
  18.4 10.7 %copy-start.10 = (bf16[256,512]{1,0:T(8,128)(2,1)}, bf16[256,512]{1,0:T(8,128)(2,1)S(1)}, u32[]{:S(2)}) copy-start(bf16[256,512]{1,0:T(8,128)(2,1)S(1)} %collective-permute-done.refs_1_) | copy-start | bytes 786436
  18.4 8.1 %collective-permute-start.2 = (bf16[128,512]{1,0:T(8,128)(2,1)S(1)}, bf16[128,512]{1,0:T(8,128)(2,1)S(1)}, u32[]{:S(2)}, u32[]{:S(2)}) collective-permute-start(bf16[128,512]{1,0:T(8,128)(2,1)S(1)} %slice.68), channel_id=1, source_target_pairs={{0,1},{1,2},{2,3},{3,0},{4,5},{5,6},{6,7},{7,4},{8,9},{9,10},{10,1... | collective-permute-start | bytes 393224 | tf_op jit(solution)/shard_map/ppermute | solution.py:21
  20.4 8.8 %copy-start.11 = (bf16[256,512]{1,0:T(8,128)(2,1)}, bf16[256,512]{1,0:T(8,128)(2,1)S(1)}, u32[]{:S(2)}) copy-start(bf16[256,512]{1,0:T(8,128)(2,1)S(1)} %collective-permute-done.1.refs_2_) | copy-start | bytes 786436
  20.4 6.1 %collective-permute-start.3 = (bf16[128,512]{1,0:T(8,128)(2,1)S(1)}, bf16[128,512]{1,0:T(8,128)(2,1)S(1)}, u32[]{:S(2)}, u32[]{:S(2)}) collective-permute-start(bf16[128,512]{1,0:T(8,128)(2,1)S(1)} %slice.69), channel_id=1, source_target_pairs={{0,3},{1,0},{2,1},{3,2},{4,7},{5,4},{6,5},{7,6},{8,11},{9,8},{10,9... | collective-permute-start | bytes 393224 | tf_op jit(solution)/shard_map/ppermute | solution.py:21
  22.0 7.1 %copy-start.12 = (bf16[256,512]{1,0:T(8,128)(2,1)}, bf16[256,512]{1,0:T(8,128)(2,1)S(1)}, u32[]{:S(2)}) copy-start(bf16[256,512]{1,0:T(8,128)(2,1)S(1)} %collective-permute-done.4.refs_6_) | copy-start | bytes 786436
  22.0 6.5 %collective-permute-start.6 = (bf16[128,512]{1,0:T(8,128)(2,1)S(1)}, bf16[128,512]{1,0:T(8,128)(2,1)S(1)}, u32[]{:S(2)}, u32[]{:S(2)}) collective-permute-start(bf16[128,512]{1,0:T(8,128)(2,1)S(1)} %slice.70), channel_id=1, source_target_pairs={{0,4},{1,5},{2,6},{3,7},{4,8},{5,9},{6,10},{7,11},{8,12},{9,13},{1... | collective-permute-start | bytes 393224 | tf_op jit(solution)/shard_map/ppermute | solution.py:26
  24.8 4.3 %copy-start.13 = (bf16[256,512]{1,0:T(8,128)(2,1)}, bf16[256,512]{1,0:T(8,128)(2,1)S(1)}, u32[]{:S(2)}) copy-start(bf16[256,512]{1,0:T(8,128)(2,1)S(1)} %collective-permute-done.5.refs_7_) | copy-start | bytes 786436
  24.8 4.3 %collective-permute-start.7 = (bf16[128,512]{1,0:T(8,128)(2,1)S(1)}, bf16[128,512]{1,0:T(8,128)(2,1)S(1)}, u32[]{:S(2)}, u32[]{:S(2)}) collective-permute-start(bf16[128,512]{1,0:T(8,128)(2,1)S(1)} %slice.71), channel_id=1, source_target_pairs={{0,12},{1,13},{2,14},{3,15},{4,0},{5,1},{6,2},{7,3},{8,4},{9,5},{1... | collective-permute-start | bytes 393224 | tf_op jit(solution)/shard_map/ppermute | solution.py:26
  26.5 19.2 %copy-start.22 = (f32[512,8]{0,1:T(8,128)S(1)}, f32[512,8]{0,1:T(8,128)}, u32[]{:S(2)}) copy-start(f32[512,8]{0,1:T(8,128)} %param.13) | copy-start | bytes 49156
  26.5 19.6 %copy-start.19 = (f32[6,512,8]{1,2,0:T(8,128)S(1)}, f32[6,512,8]{1,2,0:T(8,128)}, u32[]{:S(2)}) copy-start(f32[6,512,8]{1,2,0:T(8,128)} %param.14) | copy-start | bytes 294916
  26.5 2.7 %copy-start.15 = (bf16[128,512]{1,0:T(8,128)(2,1)}, bf16[128,512]{1,0:T(8,128)(2,1)S(1)}, u32[]{:S(2)}) copy-start(bf16[128,512]{1,0:T(8,128)(2,1)S(1)} %collective-permute-done.2.refs_3_) | copy-start | bytes 393220
  26.5 2.7 %copy-start.16 = (bf16[128,512]{1,0:T(8,128)(2,1)}, bf16[128,512]{1,0:T(8,128)(2,1)S(1)}, u32[]{:S(2)}) copy-start(bf16[128,512]{1,0:T(8,128)(2,1)S(1)} %collective-permute-done.3.refs_4_) | copy-start | bytes 393220
  28.6 0.7 copy-start.17
  29.2 0.7 copy-start.18
  32.9 23.1 %collective-permute-start.12 = (bf16[1024,512]{1,0:T(8,128)(2,1)}, bf16[1024,512]{1,0:T(8,128)(2,1)S(1)}, u32[]{:S(2)}, u32[]{:S(2)}) collective-permute-start(bf16[1024,512]{1,0:T(8,128)(2,1)} %get-tuple-element.14.refs_5_), channel_id=1, source_target_pairs={{0,1},{1,2},{2,3},{3,0},{4,5},{5,6},{6,7},{7,4},{8,9},{9,10},{10,1... | collective-permute-start | bytes 3145736 | tf_op jit(solution)/shard_map/ppermute | solution.py:21
  33.0 23.1 %collective-permute-start.13 = (bf16[1024,512]{1,0:T(8,128)(2,1)}, bf16[1024,512]{1,0:T(8,128)(2,1)S(1)}, u32[]{:S(2)}, u32[]{:S(2)}) collective-permute-start(bf16[1024,512]{1,0:T(8,128)(2,1)} %get-tuple-element.14.refs_5_), channel_id=1, source_target_pairs={{0,3},{1,0},{2,1},{3,2},{4,7},{5,4},{6,5},{7,6},{8,11},{9,8},{10,9... | collective-permute-start | bytes 3145736 | tf_op jit(solution)/shard_map/ppermute | solution.py:21
  35.7 23.2 %collective-permute-start.8 = (bf16[1024,512]{1,0:T(8,128)(2,1)}, bf16[1024,512]{1,0:T(8,128)(2,1)}, u32[]{:S(2)}, u32[]{:S(2)}) collective-permute-start(bf16[1024,512]{1,0:T(8,128)(2,1)} %get-tuple-element.13.refs_0_), channel_id=1, source_target_pairs={{0,4},{1,5},{2,6},{3,7},{4,8},{5,9},{6,10},{7,11},{8,12},{9,13},{1... | collective-permute-start | bytes 3145736 | tf_op jit(solution)/shard_map/ppermute | solution.py:26
  36.9 24.6 %collective-permute-start.9 = (bf16[1024,512]{1,0:T(8,128)(2,1)}, bf16[1024,512]{1,0:T(8,128)(2,1)}, u32[]{:S(2)}, u32[]{:S(2)}) collective-permute-start(bf16[1024,512]{1,0:T(8,128)(2,1)} %get-tuple-element.13.refs_0_), channel_id=1, source_target_pairs={{0,12},{1,13},{2,14},{3,15},{4,0},{5,1},{6,2},{7,3},{8,4},{9,5},{1... | collective-permute-start | bytes 3145736 | tf_op jit(solution)/shard_map/ppermute | solution.py:26
  45.6 21.2 %copy-start.5 = (bf16[512,1,1,256]{3,2,1,0:T(2,128)(2,1)}, bf16[512,1,1,256]{3,2,1,0:T(2,128)(2,1)S(1)}, u32[]{:S(2)}) copy-start(bf16[512,1,1,256]{3,2,1,0:T(2,128)(2,1)S(1)} %constant_dynamic-slice_fusion.5) | copy-start | bytes 786436
  46.0 24.5 %copy-start.20 = (f32[512,8]{0,1:T(8,128)}, f32[512,8]{0,1:T(8,128)S(1)}, u32[]{:S(2)}) copy-start(f32[512,8]{0,1:T(8,128)S(1)} %fusion.16) | copy-start | bytes 49156
  56.0 15.5 %copy-start.2 = (bf16[1024,512]{1,0:T(8,128)(2,1)}, bf16[1024,512]{1,0:T(8,128)(2,1)S(1)}, u32[]{:S(2)}) copy-start(bf16[1024,512]{1,0:T(8,128)(2,1)S(1)} %collective-permute-done.12.refs_6_) | copy-start | bytes 3145732
  56.0 10.8 %collective-permute-start.14 = (bf16[512,512]{1,0:T(8,128)(2,1)S(1)}, bf16[512,512]{1,0:T(8,128)(2,1)S(1)}, u32[]{:S(2)}, u32[]{:S(2)}) collective-permute-start(bf16[512,512]{1,0:T(8,128)(2,1)S(1)} %slice.74), channel_id=1, source_target_pairs={{0,1},{1,2},{2,3},{3,0},{4,5},{5,6},{6,7},{7,4},{8,9},{9,10},{10,1... | collective-permute-start | bytes 1572872 | tf_op jit(solution)/shard_map/ppermute | solution.py:21
  56.1 15.4 %copy-start.3 = (bf16[1024,512]{1,0:T(8,128)(2,1)}, bf16[1024,512]{1,0:T(8,128)(2,1)S(1)}, u32[]{:S(2)}) copy-start(bf16[1024,512]{1,0:T(8,128)(2,1)S(1)} %collective-permute-done.13.refs_7_) | copy-start | bytes 3145732
  56.2 10.7 %collective-permute-start.15 = (bf16[512,512]{1,0:T(8,128)(2,1)S(1)}, bf16[512,512]{1,0:T(8,128)(2,1)}, u32[]{:S(2)}, u32[]{:S(2)}) collective-permute-start(bf16[512,512]{1,0:T(8,128)(2,1)S(1)} %slice.75), channel_id=1, source_target_pairs={{0,3},{1,0},{2,1},{3,2},{4,7},{5,4},{6,5},{7,6},{8,11},{9,8},{10,9... | collective-permute-start | bytes 1572872 | tf_op jit(solution)/shard_map/ppermute | solution.py:21
  60.0 10.5 %collective-permute-start.10 = (bf16[512,512]{1,0:T(8,128)(2,1)S(1)}, bf16[512,512]{1,0:T(8,128)(2,1)}, u32[]{:S(2)}, u32[]{:S(2)}) collective-permute-start(bf16[512,512]{1,0:T(8,128)(2,1)S(1)} %slice.72), channel_id=1, source_target_pairs={{0,4},{1,5},{2,6},{3,7},{4,8},{5,9},{6,10},{7,11},{8,12},{9,13},{1... | collective-permute-start | bytes 1572872 | tf_op jit(solution)/shard_map/ppermute | solution.py:26
  62.6 8.9 %collective-permute-start.11 = (bf16[512,512]{1,0:T(8,128)(2,1)S(1)}, bf16[512,512]{1,0:T(8,128)(2,1)}, u32[]{:S(2)}, u32[]{:S(2)}) collective-permute-start(bf16[512,512]{1,0:T(8,128)(2,1)S(1)} %slice.73), channel_id=1, source_target_pairs={{0,12},{1,13},{2,14},{3,15},{4,0},{5,1},{6,2},{7,3},{8,4},{9,5},{1... | collective-permute-start | bytes 1572872 | tf_op jit(solution)/shard_map/ppermute | solution.py:26
  66.9 4.7 %copy-start.4 = (bf16[512,512]{1,0:T(8,128)(2,1)}, bf16[512,512]{1,0:T(8,128)(2,1)S(1)}, u32[]{:S(2)}) copy-start(bf16[512,512]{1,0:T(8,128)(2,1)S(1)} %collective-permute-done.14.refs_8_) | copy-start | bytes 1572868
  71.5 10.0 %copy-start.14 = (f32[512,256]{1,0:T(8,128)S(1)}, f32[512,256]{1,0:T(8,128)}, u32[]{:S(2)}) copy-start(f32[512,256]{1,0:T(8,128)} %fusion.28) | copy-start | bytes 1572868
  79.6 47.2 %copy-start.6 = (bf16[512,1,1,256]{3,2,1,0:T(2,128)(2,1)S(1)}, bf16[512,1,1,256]{3,2,1,0:T(2,128)(2,1)}, u32[]{:S(2)}) copy-start(bf16[512,1,1,256]{3,2,1,0:T(2,128)(2,1)} %copy-done.5) | copy-start | bytes 786436
  82.4 6.8 %collective-permute-start.16 = (bf16[8,64,256]{2,1,0:T(8,128)(2,1)S(1)}, bf16[8,64,256]{2,1,0:T(8,128)(2,1)S(1)}, u32[]{:S(2)}, u32[]{:S(2)}) collective-permute-start(bf16[8,64,256]{2,1,0:T(8,128)(2,1)S(1)} %get-tuple-element.38), channel_id=1, source_target_pairs={{0,16},{16,0},{32,48},{48,32},{64,80},{80,64},{96,112},{112,96},{1... | collective-permute-start | bytes 786440 | tf_op jit(solution)/shard_map/ppermute | solution.py:30
  89.3 8.2 %collective-permute-start.17 = (bf16[4,64,256]{2,1,0:T(8,128)(2,1)S(1)}, bf16[4,64,256]{2,1,0:T(8,128)(2,1)S(1)}, u32[]{:S(2)}, u32[]{:S(2)}) collective-permute-start(bf16[4,64,256]{2,1,0:T(8,128)(2,1)S(1)} %fusion.58), channel_id=1, source_target_pairs={{0,32},{16,48},{32,0},{48,16},{64,96},{80,112},{96,64},{112,80},{1... | collective-permute-start | bytes 393224 | tf_op jit(solution)/shard_map/ppermute | solution.py:30
  97.7 9.4 %collective-permute-start.18 = (bf16[4,64,256]{2,1,0:T(8,128)(2,1)S(1)}, bf16[4,64,256]{2,1,0:T(8,128)(2,1)S(1)}, u32[]{:S(2)}, u32[]{:S(2)}) collective-permute-start(bf16[4,64,256]{2,1,0:T(8,128)(2,1)S(1)} %fusion.27), channel_id=1, source_target_pairs={{0,64},{16,80},{32,96},{48,112},{64,0},{80,16},{96,32},{112,48},{1... | collective-permute-start | bytes 393224 | tf_op jit(solution)/shard_map/ppermute | solution.py:30
  107.3 17.0 %collective-permute-start.19 = (bf16[4,64,256]{2,1,0:T(8,128)(2,1)S(1)}, bf16[4,64,256]{2,1,0:T(8,128)(2,1)S(1)}, u32[]{:S(2)}, u32[]{:S(2)}) collective-permute-start(bf16[4,64,256]{2,1,0:T(8,128)(2,1)S(1)} %fusion.20), channel_id=1, source_target_pairs={{0,224},{16,240},{32,192},{48,208},{64,160},{80,176},{96,128},{112... | collective-permute-start | bytes 393224 | tf_op jit(solution)/shard_map/ppermute | solution.py:321
  124.3 3.8 %collective-permute-start.20 = (bf16[3,4,64,256]{3,2,1,0:T(8,128)(2,1)S(1)}, bf16[3,4,64,256]{3,2,1,0:T(8,128)(2,1)S(1)}, u32[]{:S(2)}, u32[]{:S(2)}) collective-permute-start(bf16[3,4,64,256]{3,2,1,0:T(8,128)(2,1)S(1)} %pad_maximum_fusion.1), channel_id=1, source_target_pairs={{0,16},{16,0},{32,48},{48,32},{64,80},{80,64},{96,112},{112,96},{1... | collective-permute-start | bytes 1179656 | tf_op jit(solution)/shard_map/ppermute | solution.py:30
  127.5 1.5 copy-start.7
  127.5 1.5 copy-start.21
  127.5 1.5 copy-start.23
  127.5 1.5 copy-start.24
  129.0 5.0 %copy-start.1 = (f32[512]{0:T(512)S(1)}, f32[512]{0:T(512)}, u32[]{:S(2)}) copy-start(f32[512]{0:T(512)} %param.17) | copy-start | bytes 6148
Sparse Core Ops, SparseCore 0:
  9.5 61.3 all-gather.4
  72.7 61.1 all-gather.2

commit v4 on v3

--- a/solution.py
+++ b/solution.py
@@ -31,6 +31,7 @@
 
 
 OFFSETS = (0, -1, 1, 2)
+GROUPS = (1, 2, 4, 4, 3, 1, 1)
 
 
 def in_hbm(*arrays):
@@ -114,8 +115,8 @@
 def multiply(rows, weights, total, row_sem, weight_sem):
     deep = rows.shape[1]
     depth = deep // 16
-    group = 4
-    for first in range(0, 16, group):
+    first = 0
+    for group in GROUPS:
         for s in range(first, first + group):
             columns = pl.ds(s * depth, depth)
             pltpu.make_async_copy(rows.at[:, columns], rows.at[:, columns], row_sem.at[s]).wait()
@@ -126,6 +127,7 @@
             total[...] = product
         else:
             total[...] += product
+        first += group
 
 
 def project_cost(tok, cols, deep):
@@ -305,6 +307,22 @@
     plane_share = lax.dynamic_slice_in_dim(plane_end, core * share, share, 0)
     plane_sent = plane_share.astype(jnp.bfloat16)
     near_sent = swap_ctx(plane_sent, 2)
+    values_late, _ = lax.optimization_barrier((values3, plane_sent))
+    prior_read = jnp.einsum(
+        "tn,hpn->thp", read_vec.astype(jnp.float32), prior_state, precision=HIGH
+    )
+    cum_fade = jnp.exp(-cum_rate)
+    rate_lag = cum_rate.T[:, :, None] - cum_rate.T[:, None, :]
+    mixing = (
+        jnp.where(causal[None], jnp.exp(-jnp.where(causal[None], rate_lag, 0.0)), 0.0) * scores[None]
+    ).astype(jnp.bfloat16)
+    local_out = jnp.einsum("hts,shp->thp", mixing, values_late, preferred_element_type=jnp.float32)
+    prior_scale = read_weights[5] * (cum_fade * fade(start_rate)[None])
+    early = (
+        read_weights[0][:, :, None] * local_out
+        + prior_scale[:, :, None] * prior_read
+        + skip_weight[None, :, None] * values3.astype(jnp.float32)
+    )
     plane_totals = totals.reshape(CTX // 2, 2, heads).sum(axis=1)
     share_totals = lax.dynamic_slice_in_dim(plane_totals, core * share, share, 1)
 
@@ -316,7 +334,8 @@
         return jnp.where(own_is_later, own, other) + faded * jnp.where(own_is_later, other, own)
 
     pair = joined(plane_share, near_sent.astype(jnp.float32), 1, plane)
-    pair_other = swap_ctx(pair.astype(jnp.bfloat16), 4)
+    pair_sent, early = lax.optimization_barrier((pair.astype(jnp.bfloat16), early))
+    pair_other = swap_ctx(pair_sent, 4)
     quad = joined(pair, pair_other.astype(jnp.float32), 2, plane // 2)
     quad_other = lax.ppermute(
         quad.astype(jnp.bfloat16),
@@ -339,21 +358,6 @@
         level_fade.append(jnp.where(there == 1, fade(since), 0.0))
     level_fade = jnp.stack(level_fade)
 
-    prior_read = jnp.einsum(
-        "tn,hpn->thp", read_vec.astype(jnp.float32), prior_state, precision=HIGH
-    )
-    cum_fade = jnp.exp(-cum_rate)
-    rate_lag = cum_rate.T[:, :, None] - cum_rate.T[:, None, :]
-    mixing = (
-        jnp.where(causal[None], jnp.exp(-jnp.where(causal[None], rate_lag, 0.0)), 0.0) * scores[None]
-    ).astype(jnp.bfloat16)
-    local_out = jnp.einsum("hts,shp->thp", mixing, values3, preferred_element_type=jnp.float32)
-    prior_scale = read_weights[5] * (cum_fade * fade(start_rate)[None])
-    early = (
-        read_weights[0][:, :, None] * local_out
-        + prior_scale[:, :, None] * prior_read
-        + skip_weight[None, :, None] * values3.astype(jnp.float32)
-    )
     level_read = jnp.einsum(
         "tn,lhpn->lthp", read_vec, states, preferred_element_type=jnp.float32
     )

time: 152 us -> 152 us (level)
  other arithmetic: 6.28 us -> 12.2 us
  waiting for transfers between devices: 41.4 us -> 36.4 us
  starting transfers between devices: 47.9 us -> 44.4 us
  matrix products: 7.15 us -> 9.36 us
    ppermute x4, waiting for transfers between devices: 14.5 us -> 11.1 us  [swap_ctx(): return lax.ppermute(a, 'ctx', [(i, i ^ mask) for i in range(CTX)])]
    ppermute x1, starting transfers between devices: 9.84 us -> 6.84 us  [on_device(): lax.ppermute(quad.astype(jnp.bfloat16), 'ctx', [(2 * z + c, 2 * (7 - z) +...]
    select_n x4, other arithmetic: 0.02 us -> 2.39 us  [on_device(): level_fade.append(jnp.where(there == 1, fade(since), 0.0))]
  transfers between devices with their start and end apart: 23 -> 23, of which waited for: 13 -> 11; matrix products, arithmetic and copies ran while one was open for 15% -> 21% of each run, Pallas kernels for 7% -> 7%
where the time goes in v4:
time: 152 us
  starting transfers between devices  44.4 us (29%)
  waiting for transfers between devices  36.4 us (24%)
  Pallas kernels  21.5 us (14%)
  local copies, waits for them, and re-layouts  13.9 us (9%)
  between operations  13.8 us (9%)
  other arithmetic  12.2 us (8%)
  matrix products  9.36 us (6%)
    ppermute x8, starting transfers between devices, along_y(): return lax.ppermute(a, 'tp', pairs)  12.9 us
    ppermute x8, starting transfers between devices, along_x(): return lax.ppermute(a, 'tp', pairs)  12.6 us
    ppermute x4, starting transfers between devices, swap_ctx(): return lax.ppermute(a, 'ctx', [(i, i ^ mask) for i in range(CTX)])  12 us
    ppermute x4, waiting for transfers between devices, swap_ctx(): return lax.ppermute(a, 'ctx', [(i, i ^ mask) for i in range(CTX)])  11.1 us
    pallas_call x1, Pallas kernels, finish(): pl.pallas_call(gates_kernel, out_shape=jax.ShapeDtypeStruct((tok, cols),...  10.6 us
    ppermute x8, waiting for transfers between devices, along_x(): return lax.ppermute(a, 'tp', pairs)  9.59 us
    pallas_call x1, Pallas kernels, project_values(): pl.pallas_call(values_kernel, out_shape=jax.ShapeDtypeStruct((tok, cols),...  7.88 us
    ppermute x1, waiting for transfers between devices, on_device(): lax.ppermute(quad.astype(jnp.bfloat16), 'ctx', [(2 * z + c, 2 * (7 - z) +...  7.13 us
  transfers between devices with their start and end apart: 23, of which 11 were waited for; matrix products, arithmetic and copies ran while one was open for 21% of the time, Pallas kernels for 7%

profile of v4, /device:TPU:1, one launch (start us, length us, event | category | flops | bytes accessed | tf_op | source)
XLA Modules:
  0.0 151.6 jit_solution(12621532714193576990)
XLA Ops:
  6.5 0.9 reduce_sum.96
  7.5 1.9 %pad_maximum_fusion = bf16[528,512]{1,0:T(8,128)(2,1)} fusion(bf16[16,512]{1,0:T(8,128)(2,1)S(1)} %fusion.35, bf16[512,512]{1,0:T(8,128)(2,1)} %param.10), kind=kLoop, calls=%fused_computation.20 | loop fusion | flops 1081344 | bytes 1081344 | tf_op jit(solution)/shard_map/concatenate | solution.py:259
  9.5 0.7 all-gather.3.cloned.1.call-update
  10.2 1.1 fusion.58
  11.3 2.1 %collective-permute-start = (bf16[256,512]{1,0:T(8,128)(2,1)S(1)}, bf16[256,512]{1,0:T(8,128)(2,1)S(1)}, u32[]{:S(2)}, u32[]{:S(2)}) collective-permute-start(bf16[256,512]{1,0:T(8,128)(2,1)S(1)} %get-tuple-element.35.refs_0_), channel_id=1, source_target_pairs={{0,1},{1,2},{2,3},{3,0},{4,5},{5,6},{6,7},{7,4},{8,9},{9,10},{10,1... | collective-permute-start | bytes 786440 | tf_op jit(solution)/shard_map/ppermute | solution.py:21
  13.4 1.4 collective-permute-start.1
  14.7 1.4 collective-permute-start.4
  16.1 1.4 collective-permute-start.5
  17.6 0.8 collective-permute-done.refs_1_
  18.4 1.9 %collective-permute-start.2 = (bf16[128,512]{1,0:T(8,128)(2,1)S(1)}, bf16[128,512]{1,0:T(8,128)(2,1)S(1)}, u32[]{:S(2)}, u32[]{:S(2)}) collective-permute-start(bf16[128,512]{1,0:T(8,128)(2,1)S(1)} %slice.68), channel_id=1, source_target_pairs={{0,1},{1,2},{2,3},{3,0},{4,5},{5,6},{6,7},{7,4},{8,9},{9,10},{10,1... | collective-permute-start | bytes 393224 | tf_op jit(solution)/shard_map/ppermute | solution.py:21
  20.4 1.7 %collective-permute-start.3 = (bf16[128,512]{1,0:T(8,128)(2,1)S(1)}, bf16[128,512]{1,0:T(8,128)(2,1)S(1)}, u32[]{:S(2)}, u32[]{:S(2)}) collective-permute-start(bf16[128,512]{1,0:T(8,128)(2,1)S(1)} %slice.69), channel_id=1, source_target_pairs={{0,3},{1,0},{2,1},{3,2},{4,7},{5,4},{6,5},{7,6},{8,11},{9,8},{10,9... | collective-permute-start | bytes 393224 | tf_op jit(solution)/shard_map/ppermute | solution.py:21
  22.1 2.7 %collective-permute-start.6 = (bf16[128,512]{1,0:T(8,128)(2,1)S(1)}, bf16[128,512]{1,0:T(8,128)(2,1)S(1)}, u32[]{:S(2)}, u32[]{:S(2)}) collective-permute-start(bf16[128,512]{1,0:T(8,128)(2,1)S(1)} %slice.70), channel_id=1, source_target_pairs={{0,4},{1,5},{2,6},{3,7},{4,8},{5,9},{6,10},{7,11},{8,12},{9,13},{1... | collective-permute-start | bytes 393224 | tf_op jit(solution)/shard_map/ppermute | solution.py:26
  24.8 1.5 %collective-permute-start.7 = (bf16[128,512]{1,0:T(8,128)(2,1)S(1)}, bf16[128,512]{1,0:T(8,128)(2,1)S(1)}, u32[]{:S(2)}, u32[]{:S(2)}) collective-permute-start(bf16[128,512]{1,0:T(8,128)(2,1)S(1)} %slice.71), channel_id=1, source_target_pairs={{0,12},{1,13},{2,14},{3,15},{4,0},{5,1},{6,2},{7,3},{8,4},{9,5},{1... | collective-permute-start | bytes 393224 | tf_op jit(solution)/shard_map/ppermute | solution.py:26
  26.4 0.8 iota_compare_fusion
  27.2 1.4 collective-permute-done.6.refs_8_
  28.6 0.5 collective-permute-done.7.refs_9_
  29.3 0.7 copy-done.16
  29.9 3.0 %shard_map.91 = (bf16[1024,512]{1,0:T(8,128)(2,1)}, bf16[1024,512]{1,0:T(8,128)(2,1)}) custom-call(bf16[256,512]{1,0:T(8,128)(2,1)} %copy-done.8, bf16[256,512]{1,0:T(8,128)(2,1)} %copy-done.9, bf16[256,512]{1,0:T(8,128)(2,1)} %copy-done.10, bf16[128,512]{1,0:T(8,128)(2,1)} %copy-done.13, bf16[128,512]{1,0:T(8,128)(2,1)} %copy-done.14, ...), custom_call_target="tpu_custom_call" | custom-call | tf_op jit(solution)/shard_map/pallas_call | solution.py:69
  33.0 2.7 %collective-permute-start.13 = (bf16[1024,512]{1,0:T(8,128)(2,1)}, bf16[1024,512]{1,0:T(8,128)(2,1)S(1)}, u32[]{:S(2)}, u32[]{:S(2)}) collective-permute-start(bf16[1024,512]{1,0:T(8,128)(2,1)} %get-tuple-element.17.refs_5_), channel_id=1, source_target_pairs={{0,3},{1,0},{2,1},{3,2},{4,7},{5,4},{6,5},{7,6},{8,11},{9,8},{10,9... | collective-permute-start | bytes 3145736 | tf_op jit(solution)/shard_map/ppermute | solution.py:21
  35.7 1.2 collective-permute-start.8
  37.0 1.4 collective-permute-start.9
  38.4 3.7 %fusion.57 = (bf16[512,1,4,256]{3,2,1,0:T(4,128)(2,1)}, bf16[512,1,4,256]{3,2,1,0:T(4,128)(2,1)}) fusion(bf16[512,2,4,256]{3,2,1,0:T(4,128)(2,1)} %param.12), kind=kLoop, calls=%fused_computation.111 | loop fusion | bytes 4194304 | tf_op jit(solution)/shard_map/slice | solution.py:278
  42.1 1.8 %constant_dynamic-slice_fusion.2 = bf16[512,1,1,256]{3,2,1,0:T(2,128)(2,1)S(1)} fusion(bf16[512,1,4,256]{3,2,1,0:T(4,128)(2,1)} %get-tuple-element.30, s32[]{:T(128)S(6)} %select_n.202), kind=kLoop, calls=%fused_computation.69 | loop fusion | bytes 524292 | tf_op jit(solution)/shard_map/jit(dynamic_index_in_dim)/dynamic_slice | solution.py:278
  43.9 2.0 %constant_dynamic-slice_fusion.4 = bf16[512,1,1,256]{3,2,1,0:T(2,128)(2,1)S(1)} fusion(bf16[512,1,4,256]{3,2,1,0:T(4,128)(2,1)} %get-tuple-element.31, s32[]{:T(128)S(6)} %select_n.202), kind=kLoop, calls=%fused_computation.71 | loop fusion | bytes 524292 | tf_op jit(solution)/shard_map/jit(dynamic_index_in_dim)/dynamic_slice | solution.py:277
  45.9 0.4 fusion.14
  46.3 1.4 slice_bitcast_fusion
  47.7 8.4 %collective-permute-done.12.refs_6_ = bf16[1024,512]{1,0:T(8,128)(2,1)S(1)} collective-permute-done((bf16[1024,512]{1,0:T(8,128)(2,1)}, bf16[1024,512]{1,0:T(8,128)(2,1)S(1)}, u32[]{:S(2)}, u32[]{:S(2)}) %collective-permute-start.12) | collective-permute-done | bytes 1048608 | tf_op jit(solution)/shard_map/ppermute | solution.py:21
  56.2 2.7 %collective-permute-start.15 = (bf16[512,512]{1,0:T(8,128)(2,1)S(1)}, bf16[512,512]{1,0:T(8,128)(2,1)}, u32[]{:S(2)}, u32[]{:S(2)}) collective-permute-start(bf16[512,512]{1,0:T(8,128)(2,1)S(1)} %slice.75), channel_id=1, source_target_pairs={{0,3},{1,0},{2,1},{3,2},{4,7},{5,4},{6,5},{7,6},{8,11},{9,8},{10,9... | collective-permute-start | bytes 1572872 | tf_op jit(solution)/shard_map/ppermute | solution.py:21
  59.0 1.1 slice.72
  60.0 1.5 collective-permute-start.10
  61.5 1.1 slice.73
  62.6 1.5 %collective-permute-start.11 = (bf16[512,512]{1,0:T(8,128)(2,1)S(1)}, bf16[512,512]{1,0:T(8,128)(2,1)}, u32[]{:S(2)}, u32[]{:S(2)}) collective-permute-start(bf16[512,512]{1,0:T(8,128)(2,1)S(1)} %slice.73), channel_id=1, source_target_pairs={{0,12},{1,13},{2,14},{3,15},{4,0},{5,1},{6,2},{7,3},{8,4},{9,5},{1... | collective-permute-start | bytes 1572872 | tf_op jit(solution)/shard_map/ppermute | solution.py:26
  64.3 0.8 fusion.26
  65.2 1.3 fusion.23
  66.5 0.4 collective-permute-done.14.refs_8_
  66.9 3.6 %collective-permute-done.10.refs_3_ = bf16[512,512]{1,0:T(8,128)(2,1)} collective-permute-done((bf16[512,512]{1,0:T(8,128)(2,1)S(1)}, bf16[512,512]{1,0:T(8,128)(2,1)}, u32[]{:S(2)}, u32[]{:S(2)}) %collective-permute-start.10) | collective-permute-done | bytes 524320 | tf_op jit(solution)/shard_map/ppermute | solution.py:26
  70.5 1.0 collective-permute-done.11.refs_4_
  71.5 7.9 %shard_map.92 = bf16[512,512]{1,0:T(8,128)(2,1)S(1)} custom-call(bf16[1024,512]{1,0:T(8,128)(2,1)} %get-tuple-element.16.refs_0_, bf16[1024,512]{1,0:T(8,128)(2,1)} %collective-permute-done.8.refs_1_, bf16[1024,512]{1,0:T(8,128)(2,1)} %collective-permute-done.9.refs_2_, bf16[512,512]{1,0:T(8,128)(2,1)} %collective-permute-done.10.refs_3_, ...), custom_call_target="tpu_custom_call" | custom-call | flops 4294967296 | bytes 16777216 | tf_op jit(solution)/shard_map/pallas_call | solution.py:181
  79.4 0.2 copy.14
  79.7 0.8 convert_reduce_fusion
  80.4 0.7 select_reduce_fusion.3
  81.1 1.4 negate_exponential_fusion
  82.5 1.8 %fusion.59 = (bf16[8,64,256]{2,1,0:T(8,128)(2,1)S(1)}, f32[8,64,256]{2,1,0:T(8,128)S(1)}) fusion(bf16[512,8,64]{0,2,1:T(8,128)(2,1)S(1)} %bitcast.71, f32[512,256]{1,0:T(8,128)} %fusion.26, f32[512,8]{0,1:T(8,128)S(1)} %get-tuple-element.38), kind=kOutput, calls=%fused_computation.113 | convolution fusion | flops 136445952 | bytes 1851392 | tf_op jit(solution)/shard_map/thn,thp->hpn/dot_general | solution.py:291
  84.4 5.7 %collective-permute-start.16 = (bf16[8,64,256]{2,1,0:T(8,128)(2,1)S(1)}, bf16[8,64,256]{2,1,0:T(8,128)(2,1)S(1)}, u32[]{:S(2)}, u32[]{:S(2)}) collective-permute-start(bf16[8,64,256]{2,1,0:T(8,128)(2,1)S(1)} %get-tuple-element.44), channel_id=1, source_target_pairs={{0,16},{16,0},{32,48},{48,32},{64,80},{80,64},{96,112},{112,96},{1... | collective-permute-start | bytes 786440 | tf_op jit(solution)/shard_map/ppermute | solution.py:30
  90.1 0.5 fusion.40
  90.8 0.5 fusion.41
  91.5 1.7 %collective-permute-start.17 = (bf16[4,64,256]{2,1,0:T(8,128)(2,1)S(1)}, bf16[4,64,256]{2,1,0:T(8,128)(2,1)S(1)}, u32[]{:S(2)}, u32[]{:S(2)}) collective-permute-start(bf16[4,64,256]{2,1,0:T(8,128)(2,1)S(1)} %fusion.56), channel_id=1, source_target_pairs={{0,32},{16,48},{32,0},{48,16},{64,96},{80,112},{96,64},{112,80},{1... | collective-permute-start | bytes 393224 | tf_op jit(solution)/shard_map/ppermute | solution.py:30
  93.2 4.3 %fusion.8 = f32[512,8,64]{0,2,1:T(8,128)S(1)} fusion(bf16[512,8,64]{0,2,1:T(8,128)(2,1)S(1)} %bitcast.72, f32[512,512]{1,0:T(8,128)} %fusion.23, f32[8,512]{1,0:T(8,128)} %bitcast.82, pred[512,512]{1,0:T(8,128)(4,1)} %iota_compare_fusion, f32[512,8]{0,1:T(8,128)} %slice_bitcast_fusion), kind=kOutput, calls=%fused_computation.12 | convolution fusion | flops 281280512 | bytes 2916352 | tf_op jit(solution)/shard_map/hts,shp->thp/dot_general | solution.py:319
  97.5 0.8 multiply_add_fusion
  98.3 1.7 %collective-permute-done.17 = bf16[4,64,256]{2,1,0:T(8,128)(2,1)S(1)} collective-permute-done((bf16[4,64,256]{2,1,0:T(8,128)(2,1)S(1)}, bf16[4,64,256]{2,1,0:T(8,128)(2,1)S(1)}, u32[]{:S(2)}, u32[]{:S(2)}) %collective-permute-start.17) | collective-permute-done | bytes 131104 | tf_op jit(solution)/shard_map/ppermute | solution.py:30
  100.1 3.2 %collective-permute-start.18 = (bf16[4,64,256]{2,1,0:T(8,128)(2,1)S(1)}, bf16[4,64,256]{2,1,0:T(8,128)(2,1)S(1)}, u32[]{:S(2)}, u32[]{:S(2)}) collective-permute-start(bf16[4,64,256]{2,1,0:T(8,128)(2,1)S(1)} %fusion.25), channel_id=1, source_target_pairs={{0,64},{16,80},{32,96},{48,112},{64,0},{80,16},{96,32},{112,48},{1... | collective-permute-start | bytes 393224 | tf_op jit(solution)/shard_map/ppermute | solution.py:30
  103.5 9.4 %collective-permute-done.18 = bf16[4,64,256]{2,1,0:T(8,128)(2,1)S(1)} collective-permute-done((bf16[4,64,256]{2,1,0:T(8,128)(2,1)S(1)}, bf16[4,64,256]{2,1,0:T(8,128)(2,1)S(1)}, u32[]{:S(2)}, u32[]{:S(2)}) %collective-permute-start.18) | collective-permute-done | bytes 131104 | tf_op jit(solution)/shard_map/ppermute | solution.py:30
  112.9 0.2 fusion.18
  113.1 6.8 %collective-permute-start.19 = (bf16[4,64,256]{2,1,0:T(8,128)(2,1)S(1)}, bf16[4,64,256]{2,1,0:T(8,128)(2,1)S(1)}, u32[]{:S(2)}, u32[]{:S(2)}) collective-permute-start(bf16[4,64,256]{2,1,0:T(8,128)(2,1)S(1)} %fusion.18), channel_id=1, source_target_pairs={{0,224},{16,240},{32,192},{48,208},{64,160},{80,176},{96,128},{112... | collective-permute-start | bytes 393224 | tf_op jit(solution)/shard_map/ppermute | solution.py:340
  119.9 0.7 fusion.42
  120.6 7.1 %collective-permute-done.19 = bf16[4,64,256]{2,1,0:T(8,128)(2,1)S(1)} collective-permute-done((bf16[4,64,256]{2,1,0:T(8,128)(2,1)S(1)}, bf16[4,64,256]{2,1,0:T(8,128)(2,1)S(1)}, u32[]{:S(2)}, u32[]{:S(2)}) %collective-permute-start.19) | collective-permute-done | bytes 131104 | tf_op jit(solution)/shard_map/ppermute | solution.py:340
  127.8 1.4 collective-permute-start.20
  129.2 0.7 fusion.43
  129.8 0.6 pad_maximum_fusion.2
  130.5 0.9 multiply_multiply_fusion
  131.5 0.8 fusion
  132.5 0.3 copy.17.refs_11_
  132.8 1.3 all-gather.3.cloned.1.call-done.refs_10_
  134.1 10.6 %shard_map.93 = bf16[512,512]{1,0:T(8,128)(2,1)} custom-call(bf16[1024,512]{1,0:T(8,128)(2,1)} %get-tuple-element.16.refs_0_, bf16[1024,512]{1,0:T(8,128)(2,1)} %collective-permute-done.8.refs_1_, bf16[1024,512]{1,0:T(8,128)(2,1)} %collective-permute-done.9.refs_2_, bf16[512,512]{1,0:T(8,128)(2,1)} %collective-permute-done.10.refs_3_, ...), custom_call_target="tpu_custom_call" | custom-call | flops 4294967296 | bytes 16777216 | tf_op jit(solution)/shard_map/pallas_call | solution.py:223
  (84 shorter events, 1.7 us)
Async XLA Ops:
  6.5 90.9 %copy-start = (f32[8,64,256]{2,1,0:T(8,128)S(1)}, f32[8,64,256]{2,1,0:T(8,128)}, u32[]{:S(2)}) copy-start(f32[8,64,256]{2,1,0:T(8,128)} %param.15) | copy-start | bytes 1572868
  6.5 65.0 %all-gather.5.cloned.1.call-start = ((), (), s32[]{:S(2)}) async-start(), calls=%async_computation.1 | async-start | bytes 9191424 | tf_op jit(solution)/shard_map/all_gather | solution.py:258
  9.4 124.7 %all-gather.3.cloned.1.call-start = ((), (), s32[]{:S(2)}) async-start(), calls=%async_computation | async-start | bytes 8912896 | tf_op jit(solution)/shard_map/all_gather | solution.py:261
  11.2 17.9 %copy-start.7 = (bf16[256,512]{1,0:T(8,128)(2,1)}, bf16[256,512]{1,0:T(8,128)(2,1)S(1)}, u32[]{:S(2)}) copy-start(bf16[256,512]{1,0:T(8,128)(2,1)S(1)} %get-tuple-element.34.refs_5_) | copy-start | bytes 786436
  11.3 17.9 %copy-start.8 = (bf16[256,512]{1,0:T(8,128)(2,1)}, bf16[256,512]{1,0:T(8,128)(2,1)S(1)}, u32[]{:S(2)}) copy-start(bf16[256,512]{1,0:T(8,128)(2,1)S(1)} %get-tuple-element.35.refs_0_) | copy-start | bytes 786436
  11.3 7.1 %collective-permute-start = (bf16[256,512]{1,0:T(8,128)(2,1)S(1)}, bf16[256,512]{1,0:T(8,128)(2,1)S(1)}, u32[]{:S(2)}, u32[]{:S(2)}) collective-permute-start(bf16[256,512]{1,0:T(8,128)(2,1)S(1)} %get-tuple-element.35.refs_0_), channel_id=1, source_target_pairs={{0,1},{1,2},{2,3},{3,0},{4,5},{5,6},{6,7},{7,4},{8,9},{9,10},{10,1... | collective-permute-start | bytes 786440 | tf_op jit(solution)/shard_map/ppermute | solution.py:21
  13.4 7.0 %collective-permute-start.1 = (bf16[256,512]{1,0:T(8,128)(2,1)S(1)}, bf16[256,512]{1,0:T(8,128)(2,1)S(1)}, u32[]{:S(2)}, u32[]{:S(2)}) collective-permute-start(bf16[256,512]{1,0:T(8,128)(2,1)S(1)} %get-tuple-element.35.refs_0_), channel_id=1, source_target_pairs={{0,3},{1,0},{2,1},{3,2},{4,7},{5,4},{6,5},{7,6},{8,11},{9,8},{10,9... | collective-permute-start | bytes 786440 | tf_op jit(solution)/shard_map/ppermute | solution.py:21
  14.7 7.3 %collective-permute-start.4 = (bf16[256,512]{1,0:T(8,128)(2,1)S(1)}, bf16[256,512]{1,0:T(8,128)(2,1)S(1)}, u32[]{:S(2)}, u32[]{:S(2)}) collective-permute-start(bf16[256,512]{1,0:T(8,128)(2,1)S(1)} %get-tuple-element.34.refs_5_), channel_id=1, source_target_pairs={{0,4},{1,5},{2,6},{3,7},{4,8},{5,9},{6,10},{7,11},{8,12},{9,13},{1... | collective-permute-start | bytes 786440 | tf_op jit(solution)/shard_map/ppermute | solution.py:26
  16.1 8.7 %collective-permute-start.5 = (bf16[256,512]{1,0:T(8,128)(2,1)S(1)}, bf16[256,512]{1,0:T(8,128)(2,1)S(1)}, u32[]{:S(2)}, u32[]{:S(2)}) collective-permute-start(bf16[256,512]{1,0:T(8,128)(2,1)S(1)} %get-tuple-element.34.refs_5_), channel_id=1, source_target_pairs={{0,12},{1,13},{2,14},{3,15},{4,0},{5,1},{6,2},{7,3},{8,4},{9,5},{1... | collective-permute-start | bytes 786440 | tf_op jit(solution)/shard_map/ppermute | solution.py:26
  18.4 10.7 %copy-start.9 = (bf16[256,512]{1,0:T(8,128)(2,1)}, bf16[256,512]{1,0:T(8,128)(2,1)S(1)}, u32[]{:S(2)}) copy-start(bf16[256,512]{1,0:T(8,128)(2,1)S(1)} %collective-permute-done.refs_1_) | copy-start | bytes 786436
  18.4 8.8 %collective-permute-start.2 = (bf16[128,512]{1,0:T(8,128)(2,1)S(1)}, bf16[128,512]{1,0:T(8,128)(2,1)S(1)}, u32[]{:S(2)}, u32[]{:S(2)}) collective-permute-start(bf16[128,512]{1,0:T(8,128)(2,1)S(1)} %slice.68), channel_id=1, source_target_pairs={{0,1},{1,2},{2,3},{3,0},{4,5},{5,6},{6,7},{7,4},{8,9},{9,10},{10,1... | collective-permute-start | bytes 393224 | tf_op jit(solution)/shard_map/ppermute | solution.py:21
  20.4 8.8 %copy-start.10 = (bf16[256,512]{1,0:T(8,128)(2,1)}, bf16[256,512]{1,0:T(8,128)(2,1)S(1)}, u32[]{:S(2)}) copy-start(bf16[256,512]{1,0:T(8,128)(2,1)S(1)} %collective-permute-done.1.refs_2_) | copy-start | bytes 786436
  20.4 6.8 %collective-permute-start.3 = (bf16[128,512]{1,0:T(8,128)(2,1)S(1)}, bf16[128,512]{1,0:T(8,128)(2,1)S(1)}, u32[]{:S(2)}, u32[]{:S(2)}) collective-permute-start(bf16[128,512]{1,0:T(8,128)(2,1)S(1)} %slice.69), channel_id=1, source_target_pairs={{0,3},{1,0},{2,1},{3,2},{4,7},{5,4},{6,5},{7,6},{8,11},{9,8},{10,9... | collective-permute-start | bytes 393224 | tf_op jit(solution)/shard_map/ppermute | solution.py:21
  22.1 7.1 %copy-start.11 = (bf16[256,512]{1,0:T(8,128)(2,1)}, bf16[256,512]{1,0:T(8,128)(2,1)S(1)}, u32[]{:S(2)}) copy-start(bf16[256,512]{1,0:T(8,128)(2,1)S(1)} %collective-permute-done.4.refs_6_) | copy-start | bytes 786436
  22.1 6.5 %collective-permute-start.6 = (bf16[128,512]{1,0:T(8,128)(2,1)S(1)}, bf16[128,512]{1,0:T(8,128)(2,1)S(1)}, u32[]{:S(2)}, u32[]{:S(2)}) collective-permute-start(bf16[128,512]{1,0:T(8,128)(2,1)S(1)} %slice.70), channel_id=1, source_target_pairs={{0,4},{1,5},{2,6},{3,7},{4,8},{5,9},{6,10},{7,11},{8,12},{9,13},{1... | collective-permute-start | bytes 393224 | tf_op jit(solution)/shard_map/ppermute | solution.py:26
  24.8 4.3 %copy-start.12 = (bf16[256,512]{1,0:T(8,128)(2,1)}, bf16[256,512]{1,0:T(8,128)(2,1)S(1)}, u32[]{:S(2)}) copy-start(bf16[256,512]{1,0:T(8,128)(2,1)S(1)} %collective-permute-done.5.refs_7_) | copy-start | bytes 786436
  24.8 4.3 %collective-permute-start.7 = (bf16[128,512]{1,0:T(8,128)(2,1)S(1)}, bf16[128,512]{1,0:T(8,128)(2,1)S(1)}, u32[]{:S(2)}, u32[]{:S(2)}) collective-permute-start(bf16[128,512]{1,0:T(8,128)(2,1)S(1)} %slice.71), channel_id=1, source_target_pairs={{0,12},{1,13},{2,14},{3,15},{4,0},{5,1},{6,2},{7,3},{8,4},{9,5},{1... | collective-permute-start | bytes 393224 | tf_op jit(solution)/shard_map/ppermute | solution.py:26
  27.2 18.7 %copy-start.19 = (f32[512,8]{0,1:T(8,128)S(1)}, f32[512,8]{0,1:T(8,128)}, u32[]{:S(2)}) copy-start(f32[512,8]{0,1:T(8,128)} %param.13) | copy-start | bytes 49156
  27.2 2.0 %copy-start.13 = (bf16[128,512]{1,0:T(8,128)(2,1)}, bf16[128,512]{1,0:T(8,128)(2,1)S(1)}, u32[]{:S(2)}) copy-start(bf16[128,512]{1,0:T(8,128)(2,1)S(1)} %collective-permute-done.2.refs_3_) | copy-start | bytes 393220
  27.2 2.0 %copy-start.14 = (bf16[128,512]{1,0:T(8,128)(2,1)}, bf16[128,512]{1,0:T(8,128)(2,1)S(1)}, u32[]{:S(2)}) copy-start(bf16[128,512]{1,0:T(8,128)(2,1)S(1)} %collective-permute-done.3.refs_4_) | copy-start | bytes 393220
  28.6 0.6 copy-start.15
  29.3 0.7 copy-start.16
  33.0 23.1 %collective-permute-start.12 = (bf16[1024,512]{1,0:T(8,128)(2,1)}, bf16[1024,512]{1,0:T(8,128)(2,1)S(1)}, u32[]{:S(2)}, u32[]{:S(2)}) collective-permute-start(bf16[1024,512]{1,0:T(8,128)(2,1)} %get-tuple-element.17.refs_5_), channel_id=1, source_target_pairs={{0,1},{1,2},{2,3},{3,0},{4,5},{5,6},{6,7},{7,4},{8,9},{9,10},{10,1... | collective-permute-start | bytes 3145736 | tf_op jit(solution)/shard_map/ppermute | solution.py:21
  33.0 23.1 %collective-permute-start.13 = (bf16[1024,512]{1,0:T(8,128)(2,1)}, bf16[1024,512]{1,0:T(8,128)(2,1)S(1)}, u32[]{:S(2)}, u32[]{:S(2)}) collective-permute-start(bf16[1024,512]{1,0:T(8,128)(2,1)} %get-tuple-element.17.refs_5_), channel_id=1, source_target_pairs={{0,3},{1,0},{2,1},{3,2},{4,7},{5,4},{6,5},{7,6},{8,11},{9,8},{10,9... | collective-permute-start | bytes 3145736 | tf_op jit(solution)/shard_map/ppermute | solution.py:21
  35.7 23.2 %collective-permute-start.8 = (bf16[1024,512]{1,0:T(8,128)(2,1)}, bf16[1024,512]{1,0:T(8,128)(2,1)}, u32[]{:S(2)}, u32[]{:S(2)}) collective-permute-start(bf16[1024,512]{1,0:T(8,128)(2,1)} %get-tuple-element.16.refs_0_), channel_id=1, source_target_pairs={{0,4},{1,5},{2,6},{3,7},{4,8},{5,9},{6,10},{7,11},{8,12},{9,13},{1... | collective-permute-start | bytes 3145736 | tf_op jit(solution)/shard_map/ppermute | solution.py:26
  37.0 24.6 %collective-permute-start.9 = (bf16[1024,512]{1,0:T(8,128)(2,1)}, bf16[1024,512]{1,0:T(8,128)(2,1)}, u32[]{:S(2)}, u32[]{:S(2)}) collective-permute-start(bf16[1024,512]{1,0:T(8,128)(2,1)} %get-tuple-element.16.refs_0_), channel_id=1, source_target_pairs={{0,12},{1,13},{2,14},{3,15},{4,0},{5,1},{6,2},{7,3},{8,4},{9,5},{1... | collective-permute-start | bytes 3145736 | tf_op jit(solution)/shard_map/ppermute | solution.py:26
  43.9 23.0 %copy-start.5 = (bf16[512,1,1,256]{3,2,1,0:T(2,128)(2,1)}, bf16[512,1,1,256]{3,2,1,0:T(2,128)(2,1)S(1)}, u32[]{:S(2)}) copy-start(bf16[512,1,1,256]{3,2,1,0:T(2,128)(2,1)S(1)} %constant_dynamic-slice_fusion.2) | copy-start | bytes 786436
  46.3 34.9 %copy-start.18 = (f32[512,8]{0,1:T(8,128)}, f32[512,8]{0,1:T(8,128)S(1)}, u32[]{:S(2)}) copy-start(f32[512,8]{0,1:T(8,128)S(1)} %fusion.14) | copy-start | bytes 49156
  56.0 15.5 %copy-start.2 = (bf16[1024,512]{1,0:T(8,128)(2,1)}, bf16[1024,512]{1,0:T(8,128)(2,1)S(1)}, u32[]{:S(2)}) copy-start(bf16[1024,512]{1,0:T(8,128)(2,1)S(1)} %collective-permute-done.12.refs_6_) | copy-start | bytes 3145732
  56.1 10.8 %collective-permute-start.14 = (bf16[512,512]{1,0:T(8,128)(2,1)S(1)}, bf16[512,512]{1,0:T(8,128)(2,1)S(1)}, u32[]{:S(2)}, u32[]{:S(2)}) collective-permute-start(bf16[512,512]{1,0:T(8,128)(2,1)S(1)} %slice.74), channel_id=1, source_target_pairs={{0,1},{1,2},{2,3},{3,0},{4,5},{5,6},{6,7},{7,4},{8,9},{9,10},{10,1... | collective-permute-start | bytes 1572872 | tf_op jit(solution)/shard_map/ppermute | solution.py:21
  56.2 15.4 %copy-start.3 = (bf16[1024,512]{1,0:T(8,128)(2,1)}, bf16[1024,512]{1,0:T(8,128)(2,1)S(1)}, u32[]{:S(2)}) copy-start(bf16[1024,512]{1,0:T(8,128)(2,1)S(1)} %collective-permute-done.13.refs_7_) | copy-start | bytes 3145732
  56.2 10.7 %collective-permute-start.15 = (bf16[512,512]{1,0:T(8,128)(2,1)S(1)}, bf16[512,512]{1,0:T(8,128)(2,1)}, u32[]{:S(2)}, u32[]{:S(2)}) collective-permute-start(bf16[512,512]{1,0:T(8,128)(2,1)S(1)} %slice.75), channel_id=1, source_target_pairs={{0,3},{1,0},{2,1},{3,2},{4,7},{5,4},{6,5},{7,6},{8,11},{9,8},{10,9... | collective-permute-start | bytes 1572872 | tf_op jit(solution)/shard_map/ppermute | solution.py:21
  60.0 10.5 %collective-permute-start.10 = (bf16[512,512]{1,0:T(8,128)(2,1)S(1)}, bf16[512,512]{1,0:T(8,128)(2,1)}, u32[]{:S(2)}, u32[]{:S(2)}) collective-permute-start(bf16[512,512]{1,0:T(8,128)(2,1)S(1)} %slice.72), channel_id=1, source_target_pairs={{0,4},{1,5},{2,6},{3,7},{4,8},{5,9},{6,10},{7,11},{8,12},{9,13},{1... | collective-permute-start | bytes 1572872 | tf_op jit(solution)/shard_map/ppermute | solution.py:26
  62.6 8.9 %collective-permute-start.11 = (bf16[512,512]{1,0:T(8,128)(2,1)S(1)}, bf16[512,512]{1,0:T(8,128)(2,1)}, u32[]{:S(2)}, u32[]{:S(2)}) collective-permute-start(bf16[512,512]{1,0:T(8,128)(2,1)S(1)} %slice.73), channel_id=1, source_target_pairs={{0,12},{1,13},{2,14},{3,15},{4,0},{5,1},{6,2},{7,3},{8,4},{9,5},{1... | collective-permute-start | bytes 1572872 | tf_op jit(solution)/shard_map/ppermute | solution.py:26
  66.9 4.7 %copy-start.4 = (bf16[512,512]{1,0:T(8,128)(2,1)}, bf16[512,512]{1,0:T(8,128)(2,1)S(1)}, u32[]{:S(2)}) copy-start(bf16[512,512]{1,0:T(8,128)(2,1)S(1)} %collective-permute-done.14.refs_8_) | copy-start | bytes 1572868
  84.4 7.0 %collective-permute-start.16 = (bf16[8,64,256]{2,1,0:T(8,128)(2,1)S(1)}, bf16[8,64,256]{2,1,0:T(8,128)(2,1)S(1)}, u32[]{:S(2)}, u32[]{:S(2)}) collective-permute-start(bf16[8,64,256]{2,1,0:T(8,128)(2,1)S(1)} %get-tuple-element.44), channel_id=1, source_target_pairs={{0,16},{16,0},{32,48},{48,32},{64,80},{80,64},{96,112},{112,96},{1... | collective-permute-start | bytes 786440 | tf_op jit(solution)/shard_map/ppermute | solution.py:30
  91.5 8.5 %collective-permute-start.17 = (bf16[4,64,256]{2,1,0:T(8,128)(2,1)S(1)}, bf16[4,64,256]{2,1,0:T(8,128)(2,1)S(1)}, u32[]{:S(2)}, u32[]{:S(2)}) collective-permute-start(bf16[4,64,256]{2,1,0:T(8,128)(2,1)S(1)} %fusion.56), channel_id=1, source_target_pairs={{0,32},{16,48},{32,0},{48,16},{64,96},{80,112},{96,64},{112,80},{1... | collective-permute-start | bytes 393224 | tf_op jit(solution)/shard_map/ppermute | solution.py:30
  93.2 4.3 %copy-start.6 = (bf16[512,1,1,256]{3,2,1,0:T(2,128)(2,1)S(1)}, bf16[512,1,1,256]{3,2,1,0:T(2,128)(2,1)}, u32[]{:S(2)}) copy-start(bf16[512,1,1,256]{3,2,1,0:T(2,128)(2,1)} %copy-done.5) | copy-start | bytes 786436
  93.2 4.3 %copy-start.17 = (f32[512,8]{0,1:T(8,128)S(1)}, f32[512,8]{0,1:T(8,128)}, u32[]{:S(2)}) copy-start(f32[512,8]{0,1:T(8,128)} %get-tuple-element.37) | copy-start | bytes 49156
  93.2 4.3 %copy-start.20 = (f32[8]{0:T(128)S(1)}, f32[8]{0:T(128)}, u32[]{:S(2)}) copy-start(f32[8]{0:T(128)} %param.16) | copy-start | bytes 100
  100.1 12.7 %collective-permute-start.18 = (bf16[4,64,256]{2,1,0:T(8,128)(2,1)S(1)}, bf16[4,64,256]{2,1,0:T(8,128)(2,1)S(1)}, u32[]{:S(2)}, u32[]{:S(2)}) collective-permute-start(bf16[4,64,256]{2,1,0:T(8,128)(2,1)S(1)} %fusion.25), channel_id=1, source_target_pairs={{0,64},{16,80},{32,96},{48,112},{64,0},{80,16},{96,32},{112,48},{1... | collective-permute-start | bytes 393224 | tf_op jit(solution)/shard_map/ppermute | solution.py:30
  113.1 14.7 %collective-permute-start.19 = (bf16[4,64,256]{2,1,0:T(8,128)(2,1)S(1)}, bf16[4,64,256]{2,1,0:T(8,128)(2,1)S(1)}, u32[]{:S(2)}, u32[]{:S(2)}) collective-permute-start(bf16[4,64,256]{2,1,0:T(8,128)(2,1)S(1)} %fusion.18), channel_id=1, source_target_pairs={{0,224},{16,240},{32,192},{48,208},{64,160},{80,176},{96,128},{112... | collective-permute-start | bytes 393224 | tf_op jit(solution)/shard_map/ppermute | solution.py:340
  127.8 3.6 %collective-permute-start.20 = (bf16[3,4,64,256]{3,2,1,0:T(8,128)(2,1)S(1)}, bf16[3,4,64,256]{3,2,1,0:T(8,128)(2,1)S(1)}, u32[]{:S(2)}, u32[]{:S(2)}) collective-permute-start(bf16[3,4,64,256]{3,2,1,0:T(8,128)(2,1)S(1)} %pad_maximum_fusion.1), channel_id=1, source_target_pairs={{0,16},{16,0},{32,48},{48,32},{64,80},{80,64},{96,112},{112,96},{1... | collective-permute-start | bytes 1179656 | tf_op jit(solution)/shard_map/ppermute | solution.py:30
  131.5 2.6 %copy-start.1 = (f32[512]{0:T(512)S(1)}, f32[512]{0:T(512)}, u32[]{:S(2)}) copy-start(f32[512]{0:T(512)} %param.17) | copy-start | bytes 6148
Sparse Core Ops, SparseCore 0:
  9.5 61.3 all-gather.4
  72.8 61.2 all-gather.2
